TPU v7x, 32 devices: a whole 2x2x4 slice. The times are simulated.
32 devices in a mesh: member: 2 (over y), lon: 8 (over z, x), lat: 2 (over core).
Axes of the slice: x: 2, y: 2, z: 4, core: 2. Of those that a mesh axis runs over, the one named last changes fastest.
Arguments:
- right_side: float32 [32, 128, 256], P('member', 'lon', 'lat'), parts along dimension 0, may hold values from -5 to 5
- scale: float32 [32, 128, 256], P('member', 'lon', 'lat'), parts along dimension 0, may hold values from 0.5 to 6
- land_mask: int32 [256, 256], P(('member', 'lon'), 'lat'), parts along dimension 0, may hold values 0 or 1
- bottom: int32 [256, 256], P(('member', 'lon'), 'lat'), parts along dimension 0, may hold values from 1 to 16
Outputs:
- solution: float32 [32, 128, 256], P('member', 'lon', 'lat'), parts along dimension 0
- residual: float32 [32, 128, 256], P('member', 'lon', 'lat'), parts along dimension 0
There are 2 independent parts, one for each index of `member`. A program takes and returns all parts, laid end to end along the dimension named above; each array names one. Nothing has to cross between parts.
All inputs are finite; a program needn't handle non-finite values. No bound on the sum of `land_mask` on one device may be relied on, other than what follows from the above.
Results may differ from a plain program's by a relative error of at most 0.0003.
Values sent between devices are 32-bit elements; how exact they have to be, the bound alone decides.
No kernel may reach another device: no remote copies, remote signals or barrier semaphores. Data moves between devices by JAX's collectives and lax.ppermute only.
A program may use at most 64 MiB of HBM per device.

v0:
```python
import jax
import jax.numpy as jnp
from jax import lax
from jax.sharding import PartitionSpec as P

ITERS = 3
CHEB = 3


helm_shift = 0.05
vert_ratio = 4.0
cheb_low = 4.0
cheb_high = 150.0


def with_halo(block, sides, width, periodic):
    for axis, dim in sides:
        count = lax.axis_size(axis)
        forward = [(i, i + 1) for i in range(count - 1)]
        if periodic:
            forward.append((count - 1, 0))
        backward = [(target, source) for source, target in forward]
        low = lax.ppermute(
            lax.slice_in_dim(block, block.shape[dim] - width, None, axis=dim), axis, forward
        )
        high = lax.ppermute(lax.slice_in_dim(block, 0, width, axis=dim), axis, backward)
        block = jnp.concatenate([low, block, high], axis=dim)
    return block


def cheb_factors():
    centre = 0.5 * (cheb_high + cheb_low)
    half_width = 0.5 * (cheb_high - cheb_low)
    ratio = centre / half_width
    previous = 1.0 / ratio
    factors = []
    for sweep_index in range(CHEB):
        current = 1.0 / (2.0 * ratio - previous)
        factors.append((current * previous, 2.0 * current / half_width))
        previous = current
    return (centre, factors)


def operator(padded_field, padded_weight):
    center = padded_field[:, 1:-1, 1:-1]
    own_weight = padded_weight[:, 1:-1, 1:-1]
    wet_cells = jnp.where(own_weight > 0.0, 1.0, 0.0).astype(own_weight.dtype)
    total = helm_shift * own_weight * center
    level_field = jnp.pad(center, ((1, 1), (0, 0), (0, 0)))
    level_weight = jnp.pad(own_weight, ((1, 1), (0, 0), (0, 0)))
    neighbours = [
        (padded_field[:, 2:, 1:-1], padded_weight[:, 2:, 1:-1], 0.5),
        (padded_field[:, :-2, 1:-1], padded_weight[:, :-2, 1:-1], 0.5),
        (padded_field[:, 1:-1, 2:], padded_weight[:, 1:-1, 2:], 0.5),
        (padded_field[:, 1:-1, :-2], padded_weight[:, 1:-1, :-2], 0.5),
        (level_field[2:], level_weight[2:], 0.5 * vert_ratio),
        (level_field[:-2], level_weight[:-2], 0.5 * vert_ratio),
    ]
    for other_field, other_weight, factor in neighbours:
        conduct = jnp.where(other_weight > 0.0, factor * (own_weight + other_weight), 0.0)
        total = total + conduct * (center - other_field)
    return wet_cells * total + (1.0 - wet_cells) * center


def widen_near(values):
    wider = with_halo(values, (("lon", 1),), 1, True)
    return with_halo(wider, (("lat", 2),), 1, False)


def local(right_side, scale, land_mask, bottom):
    levels = lax.broadcasted_iota(jnp.int32, right_side.shape, 0)
    wet = jnp.where((land_mask[None] == 1) & (levels < bottom[None]), 1.0, 0.0).astype(jnp.float32)
    cell_weight = wet * scale
    source = wet * right_side
    centre, factors = cheb_factors()
    weight_pad = widen_near(cell_weight)

    def smooth_apply(values):
        update = values / centre
        iterate = update
        for first, second in factors:
            defect = values - operator(widen_near(iterate), weight_pad)
            update = first * update + second * defect
            iterate = iterate + update
        return (iterate, operator(widen_near(iterate), weight_pad))

    residual = source
    smoothed, applied = smooth_apply(residual)
    solution = jnp.zeros_like(source)
    dir_applied = jnp.zeros_like(source)
    dir_smoothed = jnp.zeros_like(source)
    dir_image = jnp.zeros_like(source)
    direction = jnp.zeros_like(source)
    gamma_prev = None
    alpha_prev = None
    for turn_index in range(ITERS):
        gamma_now, delta_now = lax.psum(
            (jnp.sum(residual * smoothed), jnp.sum(applied * smoothed)), ("lon", "lat")
        )
        smoothed_new, applied_new = smooth_apply(applied)
        if turn_index == 0:
            beta_now = jnp.float32(0.0)
            alpha_now = gamma_now / delta_now
        else:
            beta_now = gamma_now / gamma_prev
            alpha_now = gamma_now / (delta_now - beta_now * gamma_now / alpha_prev)
        dir_applied = applied_new + beta_now * dir_applied
        dir_smoothed = smoothed_new + beta_now * dir_smoothed
        dir_image = applied + beta_now * dir_image
        direction = smoothed + beta_now * direction
        solution = solution + alpha_now * direction
        residual = residual - alpha_now * dir_image
        smoothed = smoothed - alpha_now * dir_smoothed
        applied = applied - alpha_now * dir_applied
        gamma_prev = gamma_now
        alpha_prev = alpha_now
    return (solution, residual)


def solution(mesh):
    in_specs = (
        P("member", "lon", "lat"),
        P("member", "lon", "lat"),
        P(("member", "lon"), "lat"),
        P(("member", "lon"), "lat"),
    )
    out_specs = (P("member", "lon", "lat"), P("member", "lon", "lat"))
    return jax.shard_map(local, mesh=mesh, in_specs=in_specs, out_specs=out_specs, check_vma=False)
```

profile of v0, /device:TPU:0, one launch (start us, length us, event | category | flops | bytes accessed | tf_op | source)
XLA Modules:
  0.0 269.2 jit_solution(15747859759548546548)
XLA Ops:
  2.4 6.0 %collective-permute-start = (f32[16,1,128]{2,1,0:T(1,128)S(1)}, f32[16,1,128]{2,1,0:T(1,128)S(1)}, u32[]{:S(2)}, u32[]{:S(2)}) collective-permute-start(f32[16,1,128]{2,1,0:T(1,128)S(1)} %get-tuple-element.81), channel_id=1, source_target_pairs={{2,0},{4,2},{6,4},{8,6},{10,8},{12,10},{14,12},{0,14},{3,1},{5,3},... | collective-permute-start | bytes 24584 | tf_op jit(solution)/shard_map/ppermute | solution.py:26
  8.5 4.8 %collective-permute-start.1 = (f32[16,1,128]{2,1,0:T(1,128)S(1)}, f32[16,1,128]{2,1,0:T(1,128)S(1)}, u32[]{:S(2)}, u32[]{:S(2)}) collective-permute-start(f32[16,1,128]{2,1,0:T(1,128)S(1)} %get-tuple-element.84), channel_id=1, source_target_pairs={{2,0},{4,2},{6,4},{8,6},{10,8},{12,10},{14,12},{0,14},{3,1},{5,3},... | collective-permute-start | bytes 24584 | tf_op jit(solution)/shard_map/ppermute | solution.py:26
  16.4 3.0 %collective-permute-start.7 = (f32[16,18,1]{2,1,0:T(8,128)S(1)}, f32[16,18,1]{2,1,0:T(8,128)S(1)}, u32[]{:S(2)}, u32[]{:S(2)}) collective-permute-start(f32[16,18,1]{2,1,0:T(8,128)S(1)} %get-tuple-element.58), channel_id=1, source_target_pairs={{0,1},{2,3},{4,5},{6,7},{8,9},{10,11},{12,13},{14,15},{16,17},{18,... | collective-permute-start | bytes 3464 | tf_op jit(solution)/shard_map/ppermute | solution.py:23
  22.1 2.0 collective-permute-done.4
  24.7 4.7 %collective-permute-start.8 = (f32[16,1,128]{2,1,0:T(1,128)S(1)}, f32[16,1,128]{2,1,0:T(1,128)S(1)}, u32[]{:S(2)}, u32[]{:S(2)}) collective-permute-start(f32[16,1,128]{2,1,0:T(1,128)S(1)} %get-tuple-element.80), channel_id=1, source_target_pairs={{2,0},{4,2},{6,4},{8,6},{10,8},{12,10},{14,12},{0,14},{3,1},{5,3},... | collective-permute-start | bytes 24584 | tf_op jit(solution)/shard_map/ppermute | solution.py:26
  29.4 1.6 collective-permute-done.9
  32.5 3.0 %collective-permute-start.11 = (f32[16,18,1]{2,1,0:T(8,128)S(1)}, f32[16,18,1]{2,1,0:T(8,128)S(1)}, u32[]{:S(2)}, u32[]{:S(2)}) collective-permute-start(f32[16,18,1]{2,1,0:T(8,128)S(1)} %get-tuple-element.54), channel_id=1, source_target_pairs={{0,1},{2,3},{4,5},{6,7},{8,9},{10,11},{12,13},{14,15},{16,17},{18,... | collective-permute-start | bytes 3464 | tf_op jit(solution)/shard_map/ppermute | solution.py:23
  37.0 4.8 %collective-permute-start.12 = (f32[16,1,128]{2,1,0:T(1,128)S(1)}, f32[16,1,128]{2,1,0:T(1,128)S(1)}, u32[]{:S(2)}, u32[]{:S(2)}) collective-permute-start(f32[16,1,128]{2,1,0:T(1,128)S(1)} %get-tuple-element.78), channel_id=1, source_target_pairs={{2,0},{4,2},{6,4},{8,6},{10,8},{12,10},{14,12},{0,14},{3,1},{5,3},... | collective-permute-start | bytes 24584 | tf_op jit(solution)/shard_map/ppermute | solution.py:26
  44.8 3.0 %collective-permute-start.15 = (f32[16,18,1]{2,1,0:T(8,128)S(1)}, f32[16,18,1]{2,1,0:T(8,128)S(1)}, u32[]{:S(2)}, u32[]{:S(2)}) collective-permute-start(f32[16,18,1]{2,1,0:T(8,128)S(1)} %get-tuple-element.52), channel_id=1, source_target_pairs={{0,1},{2,3},{4,5},{6,7},{8,9},{10,11},{12,13},{14,15},{16,17},{18,... | collective-permute-start | bytes 3464 | tf_op jit(solution)/shard_map/ppermute | solution.py:23
  49.4 4.9 %collective-permute-start.16 = (f32[16,1,128]{2,1,0:T(1,128)S(1)}, f32[16,1,128]{2,1,0:T(1,128)S(1)}, u32[]{:S(2)}, u32[]{:S(2)}) collective-permute-start(f32[16,1,128]{2,1,0:T(1,128)S(1)} %get-tuple-element.76), channel_id=1, source_target_pairs={{2,0},{4,2},{6,4},{8,6},{10,8},{12,10},{14,12},{0,14},{3,1},{5,3},... | collective-permute-start | bytes 24584 | tf_op jit(solution)/shard_map/ppermute | solution.py:26
  57.3 3.0 %collective-permute-start.19 = (f32[16,18,1]{2,1,0:T(8,128)S(1)}, f32[16,18,1]{2,1,0:T(8,128)S(1)}, u32[]{:S(2)}, u32[]{:S(2)}) collective-permute-start(f32[16,18,1]{2,1,0:T(8,128)S(1)} %get-tuple-element.50), channel_id=1, source_target_pairs={{0,1},{2,3},{4,5},{6,7},{8,9},{10,11},{12,13},{14,15},{16,17},{18,... | collective-permute-start | bytes 3464 | tf_op jit(solution)/shard_map/ppermute | solution.py:23
  62.4 4.9 %collective-permute-start.20 = (f32[16,1,128]{2,1,0:T(1,128)S(1)}, f32[16,1,128]{2,1,0:T(1,128)S(1)}, u32[]{:S(2)}, u32[]{:S(2)}) collective-permute-start(f32[16,1,128]{2,1,0:T(1,128)S(1)} %get-tuple-element.74), channel_id=1, source_target_pairs={{2,0},{4,2},{6,4},{8,6},{10,8},{12,10},{14,12},{0,14},{3,1},{5,3},... | collective-permute-start | bytes 24584 | tf_op jit(solution)/shard_map/ppermute | solution.py:26
  70.3 3.0 %collective-permute-start.23 = (f32[16,18,1]{2,1,0:T(8,128)S(1)}, f32[16,18,1]{2,1,0:T(8,128)S(1)}, u32[]{:S(2)}, u32[]{:S(2)}) collective-permute-start(f32[16,18,1]{2,1,0:T(8,128)S(1)} %get-tuple-element.48), channel_id=1, source_target_pairs={{0,1},{2,3},{4,5},{6,7},{8,9},{10,11},{12,13},{14,15},{16,17},{18,... | collective-permute-start | bytes 3464 | tf_op jit(solution)/shard_map/ppermute | solution.py:23
  74.8 4.9 %collective-permute-start.24 = (f32[16,1,128]{2,1,0:T(1,128)S(1)}, f32[16,1,128]{2,1,0:T(1,128)S(1)}, u32[]{:S(2)}, u32[]{:S(2)}) collective-permute-start(f32[16,1,128]{2,1,0:T(1,128)S(1)} %get-tuple-element.72), channel_id=1, source_target_pairs={{2,0},{4,2},{6,4},{8,6},{10,8},{12,10},{14,12},{0,14},{3,1},{5,3},... | collective-permute-start | bytes 24584 | tf_op jit(solution)/shard_map/ppermute | solution.py:26
  82.7 3.0 %collective-permute-start.27 = (f32[16,18,1]{2,1,0:T(8,128)S(1)}, f32[16,18,1]{2,1,0:T(8,128)S(1)}, u32[]{:S(2)}, u32[]{:S(2)}) collective-permute-start(f32[16,18,1]{2,1,0:T(8,128)S(1)} %get-tuple-element.46), channel_id=1, source_target_pairs={{0,1},{2,3},{4,5},{6,7},{8,9},{10,11},{12,13},{14,15},{16,17},{18,... | collective-permute-start | bytes 3464 | tf_op jit(solution)/shard_map/ppermute | solution.py:23
  87.2 4.9 %collective-permute-start.28 = (f32[16,1,128]{2,1,0:T(1,128)S(1)}, f32[16,1,128]{2,1,0:T(1,128)S(1)}, u32[]{:S(2)}, u32[]{:S(2)}) collective-permute-start(f32[16,1,128]{2,1,0:T(1,128)S(1)} %get-tuple-element.70), channel_id=1, source_target_pairs={{2,0},{4,2},{6,4},{8,6},{10,8},{12,10},{14,12},{0,14},{3,1},{5,3},... | collective-permute-start | bytes 24584 | tf_op jit(solution)/shard_map/ppermute | solution.py:26
  95.1 3.0 %collective-permute-start.31 = (f32[16,18,1]{2,1,0:T(8,128)S(1)}, f32[16,18,1]{2,1,0:T(8,128)S(1)}, u32[]{:S(2)}, u32[]{:S(2)}) collective-permute-start(f32[16,18,1]{2,1,0:T(8,128)S(1)} %get-tuple-element.44), channel_id=1, source_target_pairs={{0,1},{2,3},{4,5},{6,7},{8,9},{10,11},{12,13},{14,15},{16,17},{18,... | collective-permute-start | bytes 3464 | tf_op jit(solution)/shard_map/ppermute | solution.py:23
  99.6 4.9 %collective-permute-start.32 = (f32[16,1,128]{2,1,0:T(1,128)S(1)}, f32[16,1,128]{2,1,0:T(1,128)S(1)}, u32[]{:S(2)}, u32[]{:S(2)}) collective-permute-start(f32[16,1,128]{2,1,0:T(1,128)S(1)} %get-tuple-element.68), channel_id=1, source_target_pairs={{2,0},{4,2},{6,4},{8,6},{10,8},{12,10},{14,12},{0,14},{3,1},{5,3},... | collective-permute-start | bytes 24584 | tf_op jit(solution)/shard_map/ppermute | solution.py:26
  107.5 3.0 %collective-permute-start.35 = (f32[16,18,1]{2,1,0:T(8,128)S(1)}, f32[16,18,1]{2,1,0:T(8,128)S(1)}, u32[]{:S(2)}, u32[]{:S(2)}) collective-permute-start(f32[16,18,1]{2,1,0:T(8,128)S(1)} %get-tuple-element.42), channel_id=1, source_target_pairs={{0,1},{2,3},{4,5},{6,7},{8,9},{10,11},{12,13},{14,15},{16,17},{18,... | collective-permute-start | bytes 3464 | tf_op jit(solution)/shard_map/ppermute | solution.py:23
  110.5 33.9 %all-reduce.15 = (f32[]{:T(128)}, f32[]{:T(128)}) all-reduce(f32[]{:T(128)} %get-tuple-element.7, f32[]{:T(128)} %get-tuple-element.6), channel_id=1, replica_groups=mesh['member'=2,'lon'=8,'lat'=2] {'lon','lat'}, use_global_device_ids=true, to_apply=%region_1.2 | all-reduce | flops 2 | bytes 16 | tf_op jit(solution)/shard_map/psum | solution.py:97
  146.9 4.7 %collective-permute-start.36 = (f32[16,1,128]{2,1,0:T(1,128)S(1)}, f32[16,1,128]{2,1,0:T(1,128)S(1)}, u32[]{:S(2)}, u32[]{:S(2)}) collective-permute-start(f32[16,1,128]{2,1,0:T(1,128)S(1)} %get-tuple-element.66), channel_id=1, source_target_pairs={{2,0},{4,2},{6,4},{8,6},{10,8},{12,10},{14,12},{0,14},{3,1},{5,3},... | collective-permute-start | bytes 24584 | tf_op jit(solution)/shard_map/ppermute | solution.py:26
  151.6 1.6 collective-permute-done.37
  154.7 3.0 %collective-permute-start.39 = (f32[16,18,1]{2,1,0:T(8,128)S(1)}, f32[16,18,1]{2,1,0:T(8,128)S(1)}, u32[]{:S(2)}, u32[]{:S(2)}) collective-permute-start(f32[16,18,1]{2,1,0:T(8,128)S(1)} %get-tuple-element.40), channel_id=1, source_target_pairs={{0,1},{2,3},{4,5},{6,7},{8,9},{10,11},{12,13},{14,15},{16,17},{18,... | collective-permute-start | bytes 3464 | tf_op jit(solution)/shard_map/ppermute | solution.py:23
  159.3 4.8 %collective-permute-start.40 = (f32[16,1,128]{2,1,0:T(1,128)S(1)}, f32[16,1,128]{2,1,0:T(1,128)S(1)}, u32[]{:S(2)}, u32[]{:S(2)}) collective-permute-start(f32[16,1,128]{2,1,0:T(1,128)S(1)} %get-tuple-element.64), channel_id=1, source_target_pairs={{2,0},{4,2},{6,4},{8,6},{10,8},{12,10},{14,12},{0,14},{3,1},{5,3},... | collective-permute-start | bytes 24584 | tf_op jit(solution)/shard_map/ppermute | solution.py:26
  164.0 1.6 collective-permute-done.41
  167.1 3.0 %collective-permute-start.43 = (f32[16,18,1]{2,1,0:T(8,128)S(1)}, f32[16,18,1]{2,1,0:T(8,128)S(1)}, u32[]{:S(2)}, u32[]{:S(2)}) collective-permute-start(f32[16,18,1]{2,1,0:T(8,128)S(1)} %get-tuple-element.38), channel_id=1, source_target_pairs={{0,1},{2,3},{4,5},{6,7},{8,9},{10,11},{12,13},{14,15},{16,17},{18,... | collective-permute-start | bytes 3464 | tf_op jit(solution)/shard_map/ppermute | solution.py:23
  171.6 4.8 %collective-permute-start.44 = (f32[16,1,128]{2,1,0:T(1,128)S(1)}, f32[16,1,128]{2,1,0:T(1,128)S(1)}, u32[]{:S(2)}, u32[]{:S(2)}) collective-permute-start(f32[16,1,128]{2,1,0:T(1,128)S(1)} %get-tuple-element.62), channel_id=1, source_target_pairs={{2,0},{4,2},{6,4},{8,6},{10,8},{12,10},{14,12},{0,14},{3,1},{5,3},... | collective-permute-start | bytes 24584 | tf_op jit(solution)/shard_map/ppermute | solution.py:26
  179.4 3.0 %collective-permute-start.47 = (f32[16,18,1]{2,1,0:T(8,128)S(1)}, f32[16,18,1]{2,1,0:T(8,128)S(1)}, u32[]{:S(2)}, u32[]{:S(2)}) collective-permute-start(f32[16,18,1]{2,1,0:T(8,128)S(1)} %get-tuple-element.36), channel_id=1, source_target_pairs={{0,1},{2,3},{4,5},{6,7},{8,9},{10,11},{12,13},{14,15},{16,17},{18,... | collective-permute-start | bytes 3464 | tf_op jit(solution)/shard_map/ppermute | solution.py:23
  184.0 4.9 %collective-permute-start.48 = (f32[16,1,128]{2,1,0:T(1,128)S(1)}, f32[16,1,128]{2,1,0:T(1,128)S(1)}, u32[]{:S(2)}, u32[]{:S(2)}) collective-permute-start(f32[16,1,128]{2,1,0:T(1,128)S(1)} %get-tuple-element.60), channel_id=1, source_target_pairs={{2,0},{4,2},{6,4},{8,6},{10,8},{12,10},{14,12},{0,14},{3,1},{5,3},... | collective-permute-start | bytes 24584 | tf_op jit(solution)/shard_map/ppermute | solution.py:26
  191.8 3.0 %collective-permute-start.51 = (f32[16,18,1]{2,1,0:T(8,128)S(1)}, f32[16,18,1]{2,1,0:T(8,128)S(1)}, u32[]{:S(2)}, u32[]{:S(2)}) collective-permute-start(f32[16,18,1]{2,1,0:T(8,128)S(1)} %get-tuple-element.34), channel_id=1, source_target_pairs={{0,1},{2,3},{4,5},{6,7},{8,9},{10,11},{12,13},{14,15},{16,17},{18,... | collective-permute-start | bytes 3464 | tf_op jit(solution)/shard_map/ppermute | solution.py:23
  194.9 33.8 %all-reduce.14 = (f32[]{:T(128)}, f32[]{:T(128)}) all-reduce(f32[]{:T(128)} %get-tuple-element.3, f32[]{:T(128)} %get-tuple-element.2), channel_id=1, replica_groups=mesh['member'=2,'lon'=8,'lat'=2] {'lon','lat'}, use_global_device_ids=true, to_apply=%region_5.6 | all-reduce | flops 2 | bytes 16 | tf_op jit(solution)/shard_map/psum | solution.py:97
  234.3 30.1 %all-reduce.13 = (f32[]{:T(128)}, f32[]{:T(128)}) all-reduce(f32[]{:T(128)} %get-tuple-element.5, f32[]{:T(128)} %get-tuple-element.4), channel_id=1, replica_groups=mesh['member'=2,'lon'=8,'lat'=2] {'lon','lat'}, use_global_device_ids=true, to_apply=%region_9.10 | all-reduce | flops 2 | bytes 16 | tf_op jit(solution)/shard_map/psum | solution.py:97
  (135 shorter events, 52.9 us)
Async XLA Ops:
  2.4 10.9 %collective-permute-start = (f32[16,1,128]{2,1,0:T(1,128)S(1)}, f32[16,1,128]{2,1,0:T(1,128)S(1)}, u32[]{:S(2)}, u32[]{:S(2)}) collective-permute-start(f32[16,1,128]{2,1,0:T(1,128)S(1)} %get-tuple-element.81), channel_id=1, source_target_pairs={{2,0},{4,2},{6,4},{8,6},{10,8},{12,10},{14,12},{0,14},{3,1},{5,3},... | collective-permute-start | bytes 24584 | tf_op jit(solution)/shard_map/ppermute | solution.py:26
  8.4 6.3 %collective-permute-start.2 = (f32[16,1,128]{2,1,0:T(1,128)S(1)}, f32[16,1,128]{2,1,0:T(1,128)S(1)}, u32[]{:S(2)}, u32[]{:S(2)}) collective-permute-start(f32[16,1,128]{2,1,0:T(1,128)S(1)} %get-tuple-element.82), channel_id=1, source_target_pairs={{0,2},{2,4},{4,6},{6,8},{8,10},{10,12},{12,14},{14,0},{1,3},{3,5},... | collective-permute-start | bytes 24584 | tf_op jit(solution)/shard_map/ppermute | solution.py:23
  8.4 6.5 %collective-permute-start.3 = (f32[16,1,128]{2,1,0:T(1,128)S(1)}, f32[16,1,128]{2,1,0:T(1,128)S(1)}, u32[]{:S(2)}, u32[]{:S(2)}) collective-permute-start(f32[16,1,128]{2,1,0:T(1,128)S(1)} %get-tuple-element.83), channel_id=1, source_target_pairs={{0,2},{2,4},{4,6},{6,8},{8,10},{10,12},{12,14},{14,0},{1,3},{3,5},... | collective-permute-start | bytes 24584 | tf_op jit(solution)/shard_map/ppermute | solution.py:23
  8.5 6.4 %collective-permute-start.1 = (f32[16,1,128]{2,1,0:T(1,128)S(1)}, f32[16,1,128]{2,1,0:T(1,128)S(1)}, u32[]{:S(2)}, u32[]{:S(2)}) collective-permute-start(f32[16,1,128]{2,1,0:T(1,128)S(1)} %get-tuple-element.84), channel_id=1, source_target_pairs={{2,0},{4,2},{6,4},{8,6},{10,8},{12,10},{14,12},{0,14},{3,1},{5,3},... | collective-permute-start | bytes 24584 | tf_op jit(solution)/shard_map/ppermute | solution.py:26
  15.1 7.0 %collective-permute-start.5 = (f32[16,18,1]{2,1,0:T(8,128)S(1)}, f32[16,18,1]{2,1,0:T(8,128)S(1)}, u32[]{:S(2)}, u32[]{:S(2)}) collective-permute-start(f32[16,18,1]{2,1,0:T(8,128)S(1)} %get-tuple-element.57), channel_id=1, source_target_pairs={{1,0},{3,2},{5,4},{7,6},{9,8},{11,10},{13,12},{15,14},{17,16},{19,... | collective-permute-start | bytes 3464 | tf_op jit(solution)/shard_map/ppermute | solution.py:26
  16.4 5.7 %collective-permute-start.7 = (f32[16,18,1]{2,1,0:T(8,128)S(1)}, f32[16,18,1]{2,1,0:T(8,128)S(1)}, u32[]{:S(2)}, u32[]{:S(2)}) collective-permute-start(f32[16,18,1]{2,1,0:T(8,128)S(1)} %get-tuple-element.58), channel_id=1, source_target_pairs={{0,1},{2,3},{4,5},{6,7},{8,9},{10,11},{12,13},{14,15},{16,17},{18,... | collective-permute-start | bytes 3464 | tf_op jit(solution)/shard_map/ppermute | solution.py:23
  24.6 6.4 %collective-permute-start.9 = (f32[16,1,128]{2,1,0:T(1,128)S(1)}, f32[16,1,128]{2,1,0:T(1,128)S(1)}, u32[]{:S(2)}, u32[]{:S(2)}) collective-permute-start(f32[16,1,128]{2,1,0:T(1,128)S(1)} %get-tuple-element.79), channel_id=1, source_target_pairs={{0,2},{2,4},{4,6},{6,8},{8,10},{10,12},{12,14},{14,0},{1,3},{3,5},... | collective-permute-start | bytes 24584 | tf_op jit(solution)/shard_map/ppermute | solution.py:23
  24.7 6.3 %collective-permute-start.8 = (f32[16,1,128]{2,1,0:T(1,128)S(1)}, f32[16,1,128]{2,1,0:T(1,128)S(1)}, u32[]{:S(2)}, u32[]{:S(2)}) collective-permute-start(f32[16,1,128]{2,1,0:T(1,128)S(1)} %get-tuple-element.80), channel_id=1, source_target_pairs={{2,0},{4,2},{6,4},{8,6},{10,8},{12,10},{14,12},{0,14},{3,1},{5,3},... | collective-permute-start | bytes 24584 | tf_op jit(solution)/shard_map/ppermute | solution.py:26
  37.0 6.4 %collective-permute-start.13 = (f32[16,1,128]{2,1,0:T(1,128)S(1)}, f32[16,1,128]{2,1,0:T(1,128)S(1)}, u32[]{:S(2)}, u32[]{:S(2)}) collective-permute-start(f32[16,1,128]{2,1,0:T(1,128)S(1)} %get-tuple-element.77), channel_id=1, source_target_pairs={{0,2},{2,4},{4,6},{6,8},{8,10},{10,12},{12,14},{14,0},{1,3},{3,5},... | collective-permute-start | bytes 24584 | tf_op jit(solution)/shard_map/ppermute | solution.py:23
  37.0 6.4 %collective-permute-start.12 = (f32[16,1,128]{2,1,0:T(1,128)S(1)}, f32[16,1,128]{2,1,0:T(1,128)S(1)}, u32[]{:S(2)}, u32[]{:S(2)}) collective-permute-start(f32[16,1,128]{2,1,0:T(1,128)S(1)} %get-tuple-element.78), channel_id=1, source_target_pairs={{2,0},{4,2},{6,4},{8,6},{10,8},{12,10},{14,12},{0,14},{3,1},{5,3},... | collective-permute-start | bytes 24584 | tf_op jit(solution)/shard_map/ppermute | solution.py:26
  49.3 6.5 %collective-permute-start.17 = (f32[16,1,128]{2,1,0:T(1,128)S(1)}, f32[16,1,128]{2,1,0:T(1,128)S(1)}, u32[]{:S(2)}, u32[]{:S(2)}) collective-permute-start(f32[16,1,128]{2,1,0:T(1,128)S(1)} %get-tuple-element.75), channel_id=1, source_target_pairs={{0,2},{2,4},{4,6},{6,8},{8,10},{10,12},{12,14},{14,0},{1,3},{3,5},... | collective-permute-start | bytes 24584 | tf_op jit(solution)/shard_map/ppermute | solution.py:23
  49.4 6.4 %collective-permute-start.16 = (f32[16,1,128]{2,1,0:T(1,128)S(1)}, f32[16,1,128]{2,1,0:T(1,128)S(1)}, u32[]{:S(2)}, u32[]{:S(2)}) collective-permute-start(f32[16,1,128]{2,1,0:T(1,128)S(1)} %get-tuple-element.76), channel_id=1, source_target_pairs={{2,0},{4,2},{6,4},{8,6},{10,8},{12,10},{14,12},{0,14},{3,1},{5,3},... | collective-permute-start | bytes 24584 | tf_op jit(solution)/shard_map/ppermute | solution.py:26
  62.3 6.5 %collective-permute-start.21 = (f32[16,1,128]{2,1,0:T(1,128)S(1)}, f32[16,1,128]{2,1,0:T(1,128)S(1)}, u32[]{:S(2)}, u32[]{:S(2)}) collective-permute-start(f32[16,1,128]{2,1,0:T(1,128)S(1)} %get-tuple-element.73), channel_id=1, source_target_pairs={{0,2},{2,4},{4,6},{6,8},{8,10},{10,12},{12,14},{14,0},{1,3},{3,5},... | collective-permute-start | bytes 24584 | tf_op jit(solution)/shard_map/ppermute | solution.py:23
  62.4 6.4 %collective-permute-start.20 = (f32[16,1,128]{2,1,0:T(1,128)S(1)}, f32[16,1,128]{2,1,0:T(1,128)S(1)}, u32[]{:S(2)}, u32[]{:S(2)}) collective-permute-start(f32[16,1,128]{2,1,0:T(1,128)S(1)} %get-tuple-element.74), channel_id=1, source_target_pairs={{2,0},{4,2},{6,4},{8,6},{10,8},{12,10},{14,12},{0,14},{3,1},{5,3},... | collective-permute-start | bytes 24584 | tf_op jit(solution)/shard_map/ppermute | solution.py:26
  74.7 6.5 %collective-permute-start.25 = (f32[16,1,128]{2,1,0:T(1,128)S(1)}, f32[16,1,128]{2,1,0:T(1,128)S(1)}, u32[]{:S(2)}, u32[]{:S(2)}) collective-permute-start(f32[16,1,128]{2,1,0:T(1,128)S(1)} %get-tuple-element.71), channel_id=1, source_target_pairs={{0,2},{2,4},{4,6},{6,8},{8,10},{10,12},{12,14},{14,0},{1,3},{3,5},... | collective-permute-start | bytes 24584 | tf_op jit(solution)/shard_map/ppermute | solution.py:23
  74.8 6.4 %collective-permute-start.24 = (f32[16,1,128]{2,1,0:T(1,128)S(1)}, f32[16,1,128]{2,1,0:T(1,128)S(1)}, u32[]{:S(2)}, u32[]{:S(2)}) collective-permute-start(f32[16,1,128]{2,1,0:T(1,128)S(1)} %get-tuple-element.72), channel_id=1, source_target_pairs={{2,0},{4,2},{6,4},{8,6},{10,8},{12,10},{14,12},{0,14},{3,1},{5,3},... | collective-permute-start | bytes 24584 | tf_op jit(solution)/shard_map/ppermute | solution.py:26
  87.1 6.5 %collective-permute-start.29 = (f32[16,1,128]{2,1,0:T(1,128)S(1)}, f32[16,1,128]{2,1,0:T(1,128)S(1)}, u32[]{:S(2)}, u32[]{:S(2)}) collective-permute-start(f32[16,1,128]{2,1,0:T(1,128)S(1)} %get-tuple-element.69), channel_id=1, source_target_pairs={{0,2},{2,4},{4,6},{6,8},{8,10},{10,12},{12,14},{14,0},{1,3},{3,5},... | collective-permute-start | bytes 24584 | tf_op jit(solution)/shard_map/ppermute | solution.py:23
  87.2 6.4 %collective-permute-start.28 = (f32[16,1,128]{2,1,0:T(1,128)S(1)}, f32[16,1,128]{2,1,0:T(1,128)S(1)}, u32[]{:S(2)}, u32[]{:S(2)}) collective-permute-start(f32[16,1,128]{2,1,0:T(1,128)S(1)} %get-tuple-element.70), channel_id=1, source_target_pairs={{2,0},{4,2},{6,4},{8,6},{10,8},{12,10},{14,12},{0,14},{3,1},{5,3},... | collective-permute-start | bytes 24584 | tf_op jit(solution)/shard_map/ppermute | solution.py:26
  99.5 6.5 %collective-permute-start.33 = (f32[16,1,128]{2,1,0:T(1,128)S(1)}, f32[16,1,128]{2,1,0:T(1,128)S(1)}, u32[]{:S(2)}, u32[]{:S(2)}) collective-permute-start(f32[16,1,128]{2,1,0:T(1,128)S(1)} %get-tuple-element.67), channel_id=1, source_target_pairs={{0,2},{2,4},{4,6},{6,8},{8,10},{10,12},{12,14},{14,0},{1,3},{3,5},... | collective-permute-start | bytes 24584 | tf_op jit(solution)/shard_map/ppermute | solution.py:23
  99.6 6.4 %collective-permute-start.32 = (f32[16,1,128]{2,1,0:T(1,128)S(1)}, f32[16,1,128]{2,1,0:T(1,128)S(1)}, u32[]{:S(2)}, u32[]{:S(2)}) collective-permute-start(f32[16,1,128]{2,1,0:T(1,128)S(1)} %get-tuple-element.68), channel_id=1, source_target_pairs={{2,0},{4,2},{6,4},{8,6},{10,8},{12,10},{14,12},{0,14},{3,1},{5,3},... | collective-permute-start | bytes 24584 | tf_op jit(solution)/shard_map/ppermute | solution.py:26
  106.2 39.6 %collective-permute-start.34 = (f32[16,18,1]{2,1,0:T(8,128)S(1)}, f32[16,18,1]{2,1,0:T(8,128)S(1)}, u32[]{:S(2)}, u32[]{:S(2)}) collective-permute-start(f32[16,18,1]{2,1,0:T(8,128)S(1)} %get-tuple-element.41), channel_id=1, source_target_pairs={{1,0},{3,2},{5,4},{7,6},{9,8},{11,10},{13,12},{15,14},{17,16},{19,... | collective-permute-start | bytes 3464 | tf_op jit(solution)/shard_map/ppermute | solution.py:26
  107.5 38.3 %collective-permute-start.35 = (f32[16,18,1]{2,1,0:T(8,128)S(1)}, f32[16,18,1]{2,1,0:T(8,128)S(1)}, u32[]{:S(2)}, u32[]{:S(2)}) collective-permute-start(f32[16,18,1]{2,1,0:T(8,128)S(1)} %get-tuple-element.42), channel_id=1, source_target_pairs={{0,1},{2,3},{4,5},{6,7},{8,9},{10,11},{12,13},{14,15},{16,17},{18,... | collective-permute-start | bytes 3464 | tf_op jit(solution)/shard_map/ppermute | solution.py:23
  146.9 6.4 %collective-permute-start.37 = (f32[16,1,128]{2,1,0:T(1,128)S(1)}, f32[16,1,128]{2,1,0:T(1,128)S(1)}, u32[]{:S(2)}, u32[]{:S(2)}) collective-permute-start(f32[16,1,128]{2,1,0:T(1,128)S(1)} %get-tuple-element.65), channel_id=1, source_target_pairs={{0,2},{2,4},{4,6},{6,8},{8,10},{10,12},{12,14},{14,0},{1,3},{3,5},... | collective-permute-start | bytes 24584 | tf_op jit(solution)/shard_map/ppermute | solution.py:23
  146.9 6.3 %collective-permute-start.36 = (f32[16,1,128]{2,1,0:T(1,128)S(1)}, f32[16,1,128]{2,1,0:T(1,128)S(1)}, u32[]{:S(2)}, u32[]{:S(2)}) collective-permute-start(f32[16,1,128]{2,1,0:T(1,128)S(1)} %get-tuple-element.66), channel_id=1, source_target_pairs={{2,0},{4,2},{6,4},{8,6},{10,8},{12,10},{14,12},{0,14},{3,1},{5,3},... | collective-permute-start | bytes 24584 | tf_op jit(solution)/shard_map/ppermute | solution.py:26
  159.2 6.4 %collective-permute-start.41 = (f32[16,1,128]{2,1,0:T(1,128)S(1)}, f32[16,1,128]{2,1,0:T(1,128)S(1)}, u32[]{:S(2)}, u32[]{:S(2)}) collective-permute-start(f32[16,1,128]{2,1,0:T(1,128)S(1)} %get-tuple-element.63), channel_id=1, source_target_pairs={{0,2},{2,4},{4,6},{6,8},{8,10},{10,12},{12,14},{14,0},{1,3},{3,5},... | collective-permute-start | bytes 24584 | tf_op jit(solution)/shard_map/ppermute | solution.py:23
  159.3 6.4 %collective-permute-start.40 = (f32[16,1,128]{2,1,0:T(1,128)S(1)}, f32[16,1,128]{2,1,0:T(1,128)S(1)}, u32[]{:S(2)}, u32[]{:S(2)}) collective-permute-start(f32[16,1,128]{2,1,0:T(1,128)S(1)} %get-tuple-element.64), channel_id=1, source_target_pairs={{2,0},{4,2},{6,4},{8,6},{10,8},{12,10},{14,12},{0,14},{3,1},{5,3},... | collective-permute-start | bytes 24584 | tf_op jit(solution)/shard_map/ppermute | solution.py:26
  171.5 6.5 %collective-permute-start.45 = (f32[16,1,128]{2,1,0:T(1,128)S(1)}, f32[16,1,128]{2,1,0:T(1,128)S(1)}, u32[]{:S(2)}, u32[]{:S(2)}) collective-permute-start(f32[16,1,128]{2,1,0:T(1,128)S(1)} %get-tuple-element.61), channel_id=1, source_target_pairs={{0,2},{2,4},{4,6},{6,8},{8,10},{10,12},{12,14},{14,0},{1,3},{3,5},... | collective-permute-start | bytes 24584 | tf_op jit(solution)/shard_map/ppermute | solution.py:23
  171.6 6.4 %collective-permute-start.44 = (f32[16,1,128]{2,1,0:T(1,128)S(1)}, f32[16,1,128]{2,1,0:T(1,128)S(1)}, u32[]{:S(2)}, u32[]{:S(2)}) collective-permute-start(f32[16,1,128]{2,1,0:T(1,128)S(1)} %get-tuple-element.62), channel_id=1, source_target_pairs={{2,0},{4,2},{6,4},{8,6},{10,8},{12,10},{14,12},{0,14},{3,1},{5,3},... | collective-permute-start | bytes 24584 | tf_op jit(solution)/shard_map/ppermute | solution.py:26
  183.9 6.5 %collective-permute-start.49 = (f32[16,1,128]{2,1,0:T(1,128)S(1)}, f32[16,1,128]{2,1,0:T(1,128)S(1)}, u32[]{:S(2)}, u32[]{:S(2)}) collective-permute-start(f32[16,1,128]{2,1,0:T(1,128)S(1)} %get-tuple-element.59), channel_id=1, source_target_pairs={{0,2},{2,4},{4,6},{6,8},{8,10},{10,12},{12,14},{14,0},{1,3},{3,5},... | collective-permute-start | bytes 24584 | tf_op jit(solution)/shard_map/ppermute | solution.py:23
  184.0 6.4 %collective-permute-start.48 = (f32[16,1,128]{2,1,0:T(1,128)S(1)}, f32[16,1,128]{2,1,0:T(1,128)S(1)}, u32[]{:S(2)}, u32[]{:S(2)}) collective-permute-start(f32[16,1,128]{2,1,0:T(1,128)S(1)} %get-tuple-element.60), channel_id=1, source_target_pairs={{2,0},{4,2},{6,4},{8,6},{10,8},{12,10},{14,12},{0,14},{3,1},{5,3},... | collective-permute-start | bytes 24584 | tf_op jit(solution)/shard_map/ppermute | solution.py:26
  190.5 42.7 %collective-permute-start.50 = (f32[16,18,1]{2,1,0:T(8,128)S(1)}, f32[16,18,1]{2,1,0:T(8,128)S(1)}, u32[]{:S(2)}, u32[]{:S(2)}) collective-permute-start(f32[16,18,1]{2,1,0:T(8,128)S(1)} %get-tuple-element.33), channel_id=1, source_target_pairs={{1,0},{3,2},{5,4},{7,6},{9,8},{11,10},{13,12},{15,14},{17,16},{19,... | collective-permute-start | bytes 3464 | tf_op jit(solution)/shard_map/ppermute | solution.py:26
  191.8 41.4 %collective-permute-start.51 = (f32[16,18,1]{2,1,0:T(8,128)S(1)}, f32[16,18,1]{2,1,0:T(8,128)S(1)}, u32[]{:S(2)}, u32[]{:S(2)}) collective-permute-start(f32[16,18,1]{2,1,0:T(8,128)S(1)} %get-tuple-element.34), channel_id=1, source_target_pairs={{0,1},{2,3},{4,5},{6,7},{8,9},{10,11},{12,13},{14,15},{16,17},{18,... | collective-permute-start | bytes 3464 | tf_op jit(solution)/shard_map/ppermute | solution.py:23
  (22 other events, 91.9 us)
where the time goes:
time: 270 us; the launch traced here: 269 us
  starting transfers between devices  119 us (44%)
  blocking collectives  97.8 us (36%)
  waiting for transfers between devices  30 us (11%)
  between operations  11.2 us (4%)
  other arithmetic  9.26 us (3%)
    psum x3, blocking collectives, local(): lax.psum((jnp.sum(residual * smoothed), jnp.sum(applied * smoothed)), ('l...  97.8 us
    ppermute x26, starting transfers between devices, with_halo(): lax.ppermute(lax.slice_in_dim(block, 0, width, axis=dim), axis, backward)  80.6 us
    ppermute x26, starting transfers between devices, with_halo(): lax.ppermute(lax.slice_in_dim(block, block.shape[dim] - width, None, axis...  38.6 us
    ppermute x26, waiting for transfers between devices, with_halo(): lax.ppermute(lax.slice_in_dim(block, block.shape[dim] - width, None, axis...  28 us
  transfers between devices with their start and end apart: 52, of which 22 were waited for; matrix products, arithmetic and copies ran while one was open for 0% of the time, Pallas kernels for 0%

commit v1 on v0

v1 whole, which is shorter than its diff:
```python
import functools

import jax
import jax.numpy as jnp
from jax import lax
from jax.experimental import pallas as pl
from jax.experimental.pallas import tpu as pltpu
from jax.sharding import PartitionSpec as P

ITERS = 3
CHEB = 3
DEPTH = ITERS * (CHEB + 1)
STRIP = 16
SEGS = 8
SUB = 8
LANES = 128

helm_shift = 0.05
vert_ratio = 4.0
cheb_low = 4.0
cheb_high = 150.0

CENTRE = 0.5 * (cheb_high + cheb_low)
HALF = 0.5 * (cheb_high - cheb_low)
MU = CENTRE / HALF
NU = MU * MU - 1.0
STEP = 5.0
VMEM_BYTES = 48 * 1024 * 1024


def prep_kernel(core_ref, right_ref, scale_ref, land_ref, bottom_ref, own_ref, fwd_ref, bwd_ref, strip_ref):
    rows = land_ref.shape[0]
    core = core_ref[0]
    sub = lax.broadcasted_iota(jnp.int32, (SUB, LANES), 0)
    lane = lax.broadcasted_iota(jnp.int32, (SUB, LANES), 1)
    for group in range(rows // SEGS):
        packed = {}
        for seg in range(SEGS):
            i = group * SEGS + seg
            sea = land_ref[i : i + 1, :] == 1
            deep = jnp.where(sea, bottom_ref[i : i + 1, :], 0)
            deep = jnp.broadcast_to(deep, (SUB, LANES))
            shift = lax.rem(STRIP * seg + STRIP * (1 - core), LANES)
            for par in range(2):
                wet = 2 * sub + par < deep
                at = pl.ds(par * rows + i, SUB, stride=2 * rows)
                for f, ref in enumerate((scale_ref, right_ref)):
                    x = jnp.where(wet, ref[at, :], 0.0)
                    own_ref[i, f, par] = x
                    if i >= rows - DEPTH:
                        fwd_ref[i - (rows - DEPTH), f, par] = x
                    if i < DEPTH:
                        bwd_ref[i, f, par] = x
                    y = pltpu.roll(x, shift, 1)
                    if seg == 0:
                        packed[f, par] = y
                    else:
                        packed[f, par] = jnp.where(lane >= STRIP * seg, y, packed[f, par])
        for (f, par), y in packed.items():
            strip_ref[group, f, par] = y


def prep(core, right, scale, land, bottom):
    rows = land.shape[0]
    out = lambda n: jax.ShapeDtypeStruct((n, 2, 2, SUB, LANES), jnp.float32)
    vmem = pl.BlockSpec(memory_space=pltpu.VMEM)
    return pl.pallas_call(
        prep_kernel,
        out_shape=(out(rows), out(DEPTH), out(DEPTH), out(rows // SEGS)),
        in_specs=[pl.BlockSpec(memory_space=pltpu.SMEM)] + [vmem] * 4,
        out_specs=(vmem,) * 4,
        compiler_params=pltpu.CompilerParams(vmem_limit_bytes=VMEM_BYTES),
        name="prep",
    )(core, right, scale, land, bottom)


def main_kernel(
    core_ref, own_ref, west_ref, east_ref, strip_ref, strip_w_ref, strip_e_ref,
    u_ref, r_ref, part_ref,
    w_ref, v_ref, p_ref, q_ref, ce_ref, cn_ref, ca_ref, cb_ref, d1_ref, d0_ref, hw_ref,
):
    rows = own_ref.shape[0]
    total = rows + 2 * DEPTH
    core = core_ref[0]
    sub = lax.broadcasted_iota(jnp.int32, (SUB, LANES), 0)
    lane = lax.broadcasted_iota(jnp.int32, (SUB, LANES), 1)
    base = core * (LANES - STRIP)
    in_strip = (lane >= base) & (lane < base + STRIP)
    first_lane = lane == 0
    last_lane = lane == LANES - 1

    def unpack(r, f, par):
        row = r - DEPTH
        if row < 0:
            ref, k, row = west_ref, r, row + rows
            strips = strip_w_ref
        elif row < rows:
            ref, k = own_ref, row
            strips = strip_ref
        else:
            ref, k, row = east_ref, row - rows, row - rows
            strips = strip_e_ref
        shift = lax.rem(base + (LANES - STRIP * (row % SEGS)), LANES)
        far = pltpu.roll(strips[row // SEGS, f, par], shift, 1)
        return ref[k, f, par], jnp.where(in_strip, far, 0.0)

    for r in range(total):
        for par in range(2):
            for f, ref in enumerate((w_ref, v_ref)):
                near, far = unpack(r, f, par)
                ref[r, par] = near
                ref[r, 2 + par] = far

    def north(x):
        a, b = (pltpu.roll(t, LANES - 1, 1) for t in x)
        return jnp.where(last_lane, b, a), jnp.where(last_lane, a, b)

    def south(x):
        a, b = (pltpu.roll(t, 1, 1) for t in x)
        return jnp.where(first_lane, b, a), jnp.where(first_lane, a, b)

    def up(x):
        return pltpu.roll(x, SUB - 1, 0)

    def down(x):
        return pltpu.roll(x, 1, 0)

    def conduct(x, y, factor):
        return jnp.where(jnp.minimum(x, y) > 0.0, (x + y) * (factor / HALF), 0.0)

    def coefs(r, _):
        w = [w_ref[r, t] for t in range(4)]
        ahead = jnp.minimum(r + 1, total - 1)
        for t in range(4):
            ce_ref[r, t] = conduct(w[t], w_ref[ahead, t], 0.5)
            hw = w[t] * (helm_shift / HALF)
            hw_ref[r, t] = hw
            d0_ref[r, t] = MU - hw
            d1_ref[r, t] = 2.0 * MU - hw
        for par in range(2):
            x = (w[par], w[2 + par])
            for side, y in enumerate(north(x)):
                cn_ref[r, 2 * side + par] = conduct(x[side], y, 0.5)
        for side in range(2):
            even, odd = w[2 * side], w[2 * side + 1]
            ca_ref[r, side] = conduct(even, odd, 0.5 * vert_ratio)
            above = jnp.where(sub == SUB - 1, 0.0, up(even))
            cb_ref[r, side] = conduct(odd, above, 0.5 * vert_ratio)
        return 0

    lax.fori_loop(0, total, coefs, 0)

    def apply(src, dst, level, finish):
        def row_step(r, now, flux_w):
            ahead = [src[r + 1, t] for t in range(4)]
            flux_e = [ce_ref[r, t] * (ahead[t] - now[t]) for t in range(4)]
            acc = [flux_e[t] - flux_w[t] for t in range(4)]
            for par in range(2):
                x = (now[par], now[2 + par])
                n = north(x)
                flux = [cn_ref[r, 2 * s + par] * (n[s] - x[s]) for s in range(2)]
                back = south(flux)
                for s in range(2):
                    acc[2 * s + par] = acc[2 * s + par] + (flux[s] - back[s])
            for s in range(2):
                even, odd = now[2 * s], now[2 * s + 1]
                fa = ca_ref[r, s] * (odd - even)
                fb = cb_ref[r, s] * (up(even) - odd)
                acc[2 * s] = acc[2 * s] + (fa - down(fb))
                acc[2 * s + 1] = acc[2 * s + 1] + (fb - fa)
            for t in range(4):
                dst[r, t] = finish(r, t, acc[t], now[t])
            return ahead, flux_e

        now = [src[level, t] for t in range(4)]
        flux_w = [ce_ref[level - 1, t] * (now[t] - src[level - 1, t]) for t in range(4)]

        def body(k, carry):
            now, flux_w = carry[:4], carry[4:]
            r = level + 2 * k
            now, flux_w = row_step(r, now, flux_w)
            now, flux_w = row_step(r + 1, now, flux_w)
            return tuple(now) + tuple(flux_w)

        lax.fori_loop(0, (total - 2 * level) // 2, body, tuple(now) + tuple(flux_w))

    def dots(k, left):
        acc = jnp.zeros((SUB, LANES), jnp.float32)
        for i in range(rows):
            for par in range(2):
                acc = acc + left(i, par) * u_ref[k, i, par]
        return jnp.sum(acc, axis=0, keepdims=True)

    parts = []
    for k in range(ITERS):
        level = k * (CHEB + 1)
        apply(v_ref, p_ref, level + 1, lambda r, t, g, x: g + d1_ref[r, t] * x)
        apply(p_ref, q_ref, level + 2, lambda r, t, g, x: g + d0_ref[r, t] * x + NU * v_ref[r, t])
        apply(q_ref, p_ref, level + 3, lambda r, t, g, x: g + d0_ref[r, t] * x + MU * NU * v_ref[r, t])
        for i in range(rows):
            for par in range(2):
                u_ref[k, i, par] = p_ref[i + DEPTH, par]
        parts.append(dots(k, lambda i, par: v_ref[i + DEPTH, par]))
        apply(p_ref, v_ref, level + 4, lambda r, t, g, x: v_ref[r, t] - STEP * (hw_ref[r, t] * x - g))
        for i in range(rows):
            for par in range(2):
                r_ref[k, i, par] = v_ref[i + DEPTH, par]
        parts.append(dots(k, lambda i, par: v_ref[i + DEPTH, par]))
    block = jnp.zeros((SUB, LANES), jnp.float32)
    for j, part in enumerate(parts):
        block = jnp.where(sub == j, part, block)
    for n in range(part_ref.shape[0]):
        part_ref[n] = block


def main(core, own, west, east, strip, strip_w, strip_e, peers):
    rows = own.shape[0]
    total = rows + 2 * DEPTH
    vmem = pl.BlockSpec(memory_space=pltpu.VMEM)
    field = jax.ShapeDtypeStruct((ITERS, rows, 2, SUB, LANES), jnp.float32)
    full = pltpu.VMEM((total, 4, SUB, LANES), jnp.float32)
    half = pltpu.VMEM((total, 2, SUB, LANES), jnp.float32)
    return pl.pallas_call(
        main_kernel,
        out_shape=(field, field, jax.ShapeDtypeStruct((peers, SUB, LANES), jnp.float32)),
        in_specs=[pl.BlockSpec(memory_space=pltpu.SMEM)] + [vmem] * 6,
        out_specs=(vmem,) * 3,
        scratch_shapes=[full] * 6 + [half] * 2 + [full] * 3,
        compiler_params=pltpu.CompilerParams(vmem_limit_bytes=VMEM_BYTES),
        name="krylov",
    )(core, own, west, east, strip, strip_w, strip_e)


def times_t(poly):
    out = [poly[0]]
    for i in range(1, len(poly)):
        out.append(poly[i] - poly[i - 1])
    out.append(-poly[-1])
    return out


def add_scaled(left, factor, right):
    out = []
    for i in range(max(len(left), len(right))):
        if i >= len(right):
            out.append(left[i])
        elif i >= len(left):
            out.append(factor * right[i])
        else:
            out.append(left[i] + factor * right[i])
    return out


def inner(left, right, moments):
    total = None
    for i, x in enumerate(left):
        for j, y in enumerate(right):
            term = x * y * moments[i + j]
            total = term if total is None else total + term
    return total


def last_kernel(sums_ref, own_ref, u_ref, r_ref, sol_ref, res_ref):
    rows = own_ref.shape[0]
    peers = sums_ref.shape[0]
    acc = sums_ref[0]
    for n in range(1, peers):
        acc = acc + sums_ref[n]
    sums = jnp.broadcast_to(jnp.sum(acc, axis=1, keepdims=True), (SUB, LANES))
    moments = [jnp.broadcast_to(sums[j : j + 1, :], (SUB, LANES)) for j in range(2 * ITERS)]
    res = [jnp.ones((SUB, LANES), jnp.float32)]
    direction = res
    sol = None
    gamma = alpha = None
    for turn in range(ITERS):
        gamma_now = inner(res, res, moments)
        delta = inner(times_t(res), res, moments)
        if turn == 0:
            alpha = gamma_now / delta
            sol = [alpha]
        else:
            beta = gamma_now / gamma
            alpha = gamma_now / (delta - beta * gamma_now / alpha)
            direction = add_scaled(res, beta, direction)
            sol = add_scaled(sol, alpha, direction)
        res = add_scaled(res, -alpha, times_t(direction))
        gamma = gamma_now
    sol = [x * (STEP / HALF) for x in sol]
    for i in range(rows):
        for par in range(2):
            at = pl.ds(par * rows + i, SUB, stride=2 * rows)
            x = sol[0] * u_ref[0, i, par]
            y = res[0] * own_ref[i, 1, par]
            for k in range(ITERS):
                if k:
                    x = x + sol[k] * u_ref[k, i, par]
                y = y + res[k + 1] * r_ref[k, i, par]
            sol_ref[at, :] = x
            res_ref[at, :] = y


def last(sums, own, u, r):
    rows = own.shape[0]
    vmem = pl.BlockSpec(memory_space=pltpu.VMEM)
    out = jax.ShapeDtypeStruct((2 * SUB * rows, LANES), jnp.float32)
    return pl.pallas_call(
        last_kernel,
        out_shape=(out, out),
        in_specs=[vmem] * 4,
        out_specs=(vmem,) * 2,
        compiler_params=pltpu.CompilerParams(vmem_limit_bytes=VMEM_BYTES),
        name="combine",
    )(sums, own, u, r)


def local(right_side, scale, land_mask, bottom):
    levels, rows, lats = right_side.shape
    lon = lax.axis_size("lon")
    lat = lax.axis_size("lat")
    assert levels == 2 * SUB and lats == LANES and lat == 2
    assert rows % SEGS == 0 and rows >= DEPTH and STRIP >= DEPTH
    both = ("lon", "lat")
    place = lambda i, j: (i % lon) * lat + j
    east = [(place(i, j), place(i + 1, j)) for i in range(lon) for j in range(lat)]
    west = [(place(i, j), place(i - 1, j)) for i in range(lon) for j in range(lat)]
    east_x = [(place(i, j), place(i + 1, 1 - j)) for i in range(lon) for j in range(lat)]
    west_x = [(place(i, j), place(i - 1, 1 - j)) for i in range(lon) for j in range(lat)]
    beside = [(place(i, j), place(i, 1 - j)) for i in range(lon) for j in range(lat)]

    core = lax.axis_index("lat").astype(jnp.int32).reshape(1)
    own, fwd, bwd, strip = prep(
        core,
        right_side.reshape(levels * rows, lats),
        scale.reshape(levels * rows, lats),
        land_mask,
        bottom,
    )
    from_west = lax.ppermute(fwd, both, east)
    from_east = lax.ppermute(bwd, both, west)
    strip_w = lax.ppermute(strip, both, east_x)
    strip_e = lax.ppermute(strip, both, west_x)
    strip_o = lax.ppermute(strip, both, beside)
    u, r, parts = main(core, own, from_west, from_east, strip_o, strip_w, strip_e, lon * lat)
    sums = lax.all_to_all(parts, both, 0, 0)
    sol, res = last(sums, own, u, r)
    return sol.reshape(right_side.shape), res.reshape(right_side.shape)


def solution(mesh):
    field = P("member", "lon", "lat")
    mask = P(("member", "lon"), "lat")
    return jax.shard_map(
        local,
        mesh=mesh,
        in_specs=(field, field, mask, mask),
        out_specs=(field, field),
        check_vma=False,
    )
```

time: 270 us -> 59.9 us (0.22)
  starting transfers between devices: 119 us -> 8.17 us
  blocking collectives: 97.8 us -> 11.6 us
  Pallas kernels: 0 us -> 29.5 us
  waiting for transfers between devices: 30 us -> 6.44 us
  between operations: 11.2 us -> 0.66 us
  other arithmetic: 9.26 us -> 0 us
    ppermute x52 -> x5, starting transfers between devices: 119 us -> 8.17 us  [the longest x1 3.1 us: local(): from_east = lax.ppermute(bwd, both, west)]
    psum x3 -> x0, blocking collectives: 97.8 us -> none  [local(): lax.psum((jnp.sum(residual * smoothed), jnp.sum(applied * smoothed)), ('l...]
    pallas_call x0 -> x3, Pallas kernels: none -> 29.5 us  [the longest x1 28.2 us: main(): pl.pallas_call(main_kernel, out_shape=(field, field, jax.ShapeDtypeStruct...]
    ppermute x52 -> x5, waiting for transfers between devices: 30 us -> 6.44 us  [the longest x1 4.97 us: local(): strip_e = lax.ppermute(strip, both, west_x)]
    all_to_all x0 -> x1, blocking collectives: none -> 11.6 us  [local(): sums = lax.all_to_all(parts, both, 0, 0)]
    add x9 -> x0, other arithmetic: 3.25 us -> none  [smooth_apply(): iterate = iterate + update]
    unnamed x4 -> x8, local copies, waits for them, and re-layouts: 0.01 us -> 3.19 us
    reduce_sum x3 -> x0, other arithmetic: 3.02 us -> none  [local(): jnp.sum(applied * smoothed)]
  transfers between devices with their start and end apart: 52 -> 5, of which waited for: 22 -> 2; matrix products, arithmetic and copies ran while one was open for 0% -> 0% of each run, Pallas kernels for 0% -> 0%
where the time goes in v1:
time: 59.9 us; the launch traced here: 59.7 us
  Pallas kernels  29.5 us (49%)
  blocking collectives  11.6 us (19%)
  starting transfers between devices  8.17 us (14%)
  waiting for transfers between devices  6.44 us (11%)
  local copies, waits for them, and re-layouts  3.19 us (5%)
  between operations  0.66 us (1%)
    pallas_call x1, Pallas kernels, main(): pl.pallas_call(main_kernel, out_shape=(field, field, jax.ShapeDtypeStruct...  28.2 us
    all_to_all x1, blocking collectives, local(): sums = lax.all_to_all(parts, both, 0, 0)  11.6 us
    ppermute x1, waiting for transfers between devices, local(): strip_e = lax.ppermute(strip, both, west_x)  4.97 us
    unnamed x8, local copies, waits for them, and re-layouts  3.19 us
    ppermute x1, starting transfers between devices, local(): from_east = lax.ppermute(bwd, both, west)  3.1 us
    ppermute x1, starting transfers between devices, local(): from_west = lax.ppermute(fwd, both, east)  2.99 us
    ppermute x1, waiting for transfers between devices, local(): from_east = lax.ppermute(bwd, both, west)  1.46 us
  transfers between devices with their start and end apart: 5, of which 2 were waited for; matrix products, arithmetic and copies ran while one was open for 0% of the time, Pallas kernels for 0%

profile of v1, /device:TPU:0, one launch (start us, length us, event | category | flops | bytes accessed | tf_op | source)
XLA Modules:
  0.0 59.7 jit_solution(9639653853932425030)
XLA Ops:
  0.6 0.0 copy-start.2
  0.6 0.7 %copy-done.2 = s32[16,128]{1,0:T(8,128)S(1)} copy-done((s32[16,128]{1,0:T(8,128)S(1)}, s32[16,128]{1,0:T(8,128)}, u32[]{:S(2)}) %copy-start.2) | copy-done | bytes 8216
  1.3 0.0 copy-start
  1.3 0.9 %copy-done = f32[16,16,128]{2,1,0:T(8,128)S(1)} copy-done((f32[16,16,128]{2,1,0:T(8,128)S(1)}, f32[16,16,128]{2,1,0:T(8,128)}, u32[]{:S(2)}) %copy-start) | copy-done | bytes 131096
  2.2 0.0 copy-start.1
  2.2 0.9 %copy-done.1 = f32[16,16,128]{2,1,0:T(8,128)S(1)} copy-done((f32[16,16,128]{2,1,0:T(8,128)S(1)}, f32[16,16,128]{2,1,0:T(8,128)}, u32[]{:S(2)}) %copy-start.1) | copy-done | bytes 131096
  3.1 0.0 copy-start.3
  3.1 0.7 %copy-done.3 = s32[16,128]{1,0:T(8,128)S(1)} copy-done((s32[16,128]{1,0:T(8,128)S(1)}, s32[16,128]{1,0:T(8,128)}, u32[]{:S(2)}) %copy-start.3) | copy-done | bytes 8216
  3.8 0.2 prep.1
  4.1 3.0 %collective-permute-start = (f32[12,2,2,8,128]{4,3,2,1,0:T(8,128)S(1)}, f32[12,2,2,8,128]{4,3,2,1,0:T(8,128)S(1)}, u32[]{:S(2)}, u32[]{:S(2)}) collective-permute-start(f32[12,2,2,8,128]{4,3,2,1,0:T(8,128)S(1)} %get-tuple-element.12), channel_id=1, source_target_pairs={{0,2},{1,3},{2,4},{3,5},{4,6},{5,7},{6,8},{7,9},{8,10},{9,11},{10,... | collective-permute-start | bytes 589832 | tf_op jit(solution)/shard_map/ppermute | solution.py:338
  7.1 3.1 %collective-permute-start.1 = (f32[12,2,2,8,128]{4,3,2,1,0:T(8,128)S(1)}, f32[12,2,2,8,128]{4,3,2,1,0:T(8,128)S(1)}, u32[]{:S(2)}, u32[]{:S(2)}) collective-permute-start(f32[12,2,2,8,128]{4,3,2,1,0:T(8,128)S(1)} %get-tuple-element.13), channel_id=1, source_target_pairs={{0,14},{1,15},{2,0},{3,1},{4,2},{5,3},{6,4},{7,5},{8,6},{9,7},{10,... | collective-permute-start | bytes 589832 | tf_op jit(solution)/shard_map/ppermute | solution.py:339
  10.2 0.8 %collective-permute-start.4 = (f32[2,2,2,8,128]{4,3,2,1,0:T(8,128)S(1)}, f32[2,2,2,8,128]{4,3,2,1,0:T(8,128)S(1)}, u32[]{:S(2)}, u32[]{:S(2)}) collective-permute-start(f32[2,2,2,8,128]{4,3,2,1,0:T(8,128)S(1)} %get-tuple-element.14), channel_id=1, source_target_pairs={{0,15},{1,14},{2,1},{3,0},{4,3},{5,2},{6,5},{7,4},{8,7},{9,6},{10,... | collective-permute-start | bytes 98312 | tf_op jit(solution)/shard_map/ppermute | solution.py:341
  11.0 0.9 %collective-permute-start.3 = (f32[2,2,2,8,128]{4,3,2,1,0:T(8,128)S(1)}, f32[2,2,2,8,128]{4,3,2,1,0:T(8,128)S(1)}, u32[]{:S(2)}, u32[]{:S(2)}) collective-permute-start(f32[2,2,2,8,128]{4,3,2,1,0:T(8,128)S(1)} %get-tuple-element.14), channel_id=1, source_target_pairs={{0,3},{1,2},{2,5},{3,4},{4,7},{5,6},{6,9},{7,8},{8,11},{9,10},{10,... | collective-permute-start | bytes 98312 | tf_op jit(solution)/shard_map/ppermute | solution.py:340
  11.9 0.3 collective-permute-start.2
  12.3 5.0 %collective-permute-done.4.strip_e_ref = f32[2,2,2,8,128]{4,3,2,1,0:T(8,128)S(1)} collective-permute-done((f32[2,2,2,8,128]{4,3,2,1,0:T(8,128)S(1)}, f32[2,2,2,8,128]{4,3,2,1,0:T(8,128)S(1)}, u32[]{:S(2)}, u32[]{:S(2)}) %collective-permute-start.4) | collective-permute-done | bytes 32800 | tf_op jit(solution)/shard_map/ppermute | solution.py:341
  17.2 0.0 collective-permute-done.3.strip_w_ref
  17.2 0.0 collective-permute-done.2.strip_ref
  17.2 0.0 collective-permute-done.west_ref
  17.2 1.5 %collective-permute-done.1.east_ref = f32[12,2,2,8,128]{4,3,2,1,0:T(8,128)S(1)} collective-permute-done((f32[12,2,2,8,128]{4,3,2,1,0:T(8,128)S(1)}, f32[12,2,2,8,128]{4,3,2,1,0:T(8,128)S(1)}, u32[]{:S(2)}, u32[]{:S(2)}) %collective-permute-start.1) | collective-permute-done | bytes 196640 | tf_op jit(solution)/shard_map/ppermute | solution.py:339
  18.7 28.2 %krylov.1 = (f32[3,16,2,8,128]{4,3,2,1,0:T(8,128)S(1)}, f32[3,16,2,8,128]{4,3,2,1,0:T(8,128)S(1)}, f32[16,8,128]{2,1,0:T(8,128)S(1)}) custom-call(s32[1]{0:T(128)} %bitcast.core_ref, f32[16,2,2,8,128]{4,3,2,1,0:T(8,128)S(1)} %get-tuple-element.11.own_ref, f32[12,2,2,8,128]{4,3,2,1,0:T(8,128)S(1)} %collective-permute-done.west_ref, ...), custom_call_target="tpu_custom_call" | custom-call | tf_op jit(solution)/shard_map/krylov/pallas_call | solution.py:223
  46.9 11.6 %all_to_all.5.sums_ref = f32[16,8,128]{2,1,0:T(8,128)S(1)} all-to-all(f32[16,8,128]{2,1,0:T(8,128)S(1)} %get-tuple-element.15), channel_id=1, replica_groups=mesh['member'=2,'lon'=8,'lat'=2] {'lon','lat'}, dimensions={0} | all-to-all | bytes 131072 | tf_op jit(solution)/shard_map/all_to_all | solution.py:344
  58.6 1.1 %combine.1 = (f32[256,128]{1,0:T(8,128)}, f32[256,128]{1,0:T(8,128)}) custom-call(f32[16,8,128]{2,1,0:T(8,128)S(1)} %all_to_all.5.sums_ref, f32[16,2,2,8,128]{4,3,2,1,0:T(8,128)S(1)} %get-tuple-element.11.own_ref, f32[3,16,2,8,128]{4,3,2,1,0:T(8,128)S(1)} %get-tuple-element.16.u_ref, f32[3,16,2,8,128]{4,3,2,1,0:T(8,128)S(1)} %get-tuple-element.17.r_ref), custom_call_target="tpu_custom_call" | custom-call | tf_op jit(solution)/shard_map/combine/pallas_call | solution.py:306
Async XLA Ops:
  0.6 0.7 %copy-start.2 = (s32[16,128]{1,0:T(8,128)S(1)}, s32[16,128]{1,0:T(8,128)}, u32[]{:S(2)}) copy-start(s32[16,128]{1,0:T(8,128)} %land_ref.1) | copy-start | bytes 24580
  1.3 0.9 %copy-start = (f32[16,16,128]{2,1,0:T(8,128)S(1)}, f32[16,16,128]{2,1,0:T(8,128)}, u32[]{:S(2)}) copy-start(f32[16,16,128]{2,1,0:T(8,128)} %param.4) | copy-start | bytes 393220
  2.2 0.9 %copy-start.1 = (f32[16,16,128]{2,1,0:T(8,128)S(1)}, f32[16,16,128]{2,1,0:T(8,128)}, u32[]{:S(2)}) copy-start(f32[16,16,128]{2,1,0:T(8,128)} %param.5) | copy-start | bytes 393220
  3.1 0.7 %copy-start.3 = (s32[16,128]{1,0:T(8,128)S(1)}, s32[16,128]{1,0:T(8,128)}, u32[]{:S(2)}) copy-start(s32[16,128]{1,0:T(8,128)} %bottom_ref.1) | copy-start | bytes 24580
  4.1 13.2 %collective-permute-start = (f32[12,2,2,8,128]{4,3,2,1,0:T(8,128)S(1)}, f32[12,2,2,8,128]{4,3,2,1,0:T(8,128)S(1)}, u32[]{:S(2)}, u32[]{:S(2)}) collective-permute-start(f32[12,2,2,8,128]{4,3,2,1,0:T(8,128)S(1)} %get-tuple-element.12), channel_id=1, source_target_pairs={{0,2},{1,3},{2,4},{3,5},{4,6},{5,7},{6,8},{7,9},{8,10},{9,11},{10,... | collective-permute-start | bytes 589832 | tf_op jit(solution)/shard_map/ppermute | solution.py:338
  7.1 11.6 %collective-permute-start.1 = (f32[12,2,2,8,128]{4,3,2,1,0:T(8,128)S(1)}, f32[12,2,2,8,128]{4,3,2,1,0:T(8,128)S(1)}, u32[]{:S(2)}, u32[]{:S(2)}) collective-permute-start(f32[12,2,2,8,128]{4,3,2,1,0:T(8,128)S(1)} %get-tuple-element.13), channel_id=1, source_target_pairs={{0,14},{1,15},{2,0},{3,1},{4,2},{5,3},{6,4},{7,5},{8,6},{9,7},{10,... | collective-permute-start | bytes 589832 | tf_op jit(solution)/shard_map/ppermute | solution.py:339
  10.2 7.1 %collective-permute-start.4 = (f32[2,2,2,8,128]{4,3,2,1,0:T(8,128)S(1)}, f32[2,2,2,8,128]{4,3,2,1,0:T(8,128)S(1)}, u32[]{:S(2)}, u32[]{:S(2)}) collective-permute-start(f32[2,2,2,8,128]{4,3,2,1,0:T(8,128)S(1)} %get-tuple-element.14), channel_id=1, source_target_pairs={{0,15},{1,14},{2,1},{3,0},{4,3},{5,2},{6,5},{7,4},{8,7},{9,6},{10,... | collective-permute-start | bytes 98312 | tf_op jit(solution)/shard_map/ppermute | solution.py:341
  11.0 6.2 %collective-permute-start.3 = (f32[2,2,2,8,128]{4,3,2,1,0:T(8,128)S(1)}, f32[2,2,2,8,128]{4,3,2,1,0:T(8,128)S(1)}, u32[]{:S(2)}, u32[]{:S(2)}) collective-permute-start(f32[2,2,2,8,128]{4,3,2,1,0:T(8,128)S(1)} %get-tuple-element.14), channel_id=1, source_target_pairs={{0,3},{1,2},{2,5},{3,4},{4,7},{5,6},{6,9},{7,8},{8,11},{9,10},{10,... | collective-permute-start | bytes 98312 | tf_op jit(solution)/shard_map/ppermute | solution.py:340
  11.9 5.3 %collective-permute-start.2 = (f32[2,2,2,8,128]{4,3,2,1,0:T(8,128)S(1)}, f32[2,2,2,8,128]{4,3,2,1,0:T(8,128)S(1)}, u32[]{:S(2)}, u32[]{:S(2)}) collective-permute-start(f32[2,2,2,8,128]{4,3,2,1,0:T(8,128)S(1)} %get-tuple-element.14), channel_id=1, source_target_pairs={{0,1},{1,0},{2,3},{3,2},{4,5},{5,4},{6,7},{7,6},{8,9},{9,8},{10,11... | collective-permute-start | bytes 98312 | tf_op jit(solution)/shard_map/ppermute | solution.py:342

commit v2 on v1

--- a/solution.py
+++ b/solution.py
@@ -10,10 +10,11 @@
 ITERS = 3
 CHEB = 3
 DEPTH = ITERS * (CHEB + 1)
-STRIP = 16
-SEGS = 8
 SUB = 8
 LANES = 128
+WIDE = LANES // 2
+SEGS = 8
+EDGE = WIDE // SEGS
 
 helm_shift = 0.05
 vert_ratio = 4.0
@@ -28,11 +29,24 @@
 VMEM_BYTES = 48 * 1024 * 1024
 
 
-def prep_kernel(core_ref, right_ref, scale_ref, land_ref, bottom_ref, own_ref, fwd_ref, bwd_ref, strip_ref):
+def take_lanes(x, index):
+    return jnp.take_along_axis(x, index, axis=1, mode="promise_in_bounds")
+
+
+def prep_kernel(core_ref, *refs):
+    sources, (own_ref, fwd_ref, bwd_ref, strip_ref), held, sems = refs[:4], refs[4:8], refs[8:12], refs[12]
+    copies = [pltpu.make_async_copy(a, b, sems.at[k]) for k, (a, b) in enumerate(zip(sources, held))]
+    for copy in copies:
+        copy.start()
+    for copy in copies:
+        copy.wait()
+    right_ref, scale_ref, land_ref, bottom_ref = held
     rows = land_ref.shape[0]
     core = core_ref[0]
     sub = lax.broadcasted_iota(jnp.int32, (SUB, LANES), 0)
     lane = lax.broadcasted_iota(jnp.int32, (SUB, LANES), 1)
+    half_lane = lane % WIDE
+    apart = 2 * half_lane + lane // WIDE
     for group in range(rows // SEGS):
         packed = {}
         for seg in range(SEGS):
@@ -40,12 +54,12 @@
             sea = land_ref[i : i + 1, :] == 1
             deep = jnp.where(sea, bottom_ref[i : i + 1, :], 0)
             deep = jnp.broadcast_to(deep, (SUB, LANES))
-            shift = lax.rem(STRIP * seg + STRIP * (1 - core), LANES)
+            shift = lax.rem(EDGE * seg + (1 - core) * (WIDE + EDGE), LANES)
             for par in range(2):
                 wet = 2 * sub + par < deep
                 at = pl.ds(par * rows + i, SUB, stride=2 * rows)
                 for f, ref in enumerate((scale_ref, right_ref)):
-                    x = jnp.where(wet, ref[at, :], 0.0)
+                    x = take_lanes(jnp.where(wet, ref[at, :], 0.0), apart)
                     own_ref[i, f, par] = x
                     if i >= rows - DEPTH:
                         fwd_ref[i - (rows - DEPTH), f, par] = x
@@ -55,7 +69,7 @@
                     if seg == 0:
                         packed[f, par] = y
                     else:
-                        packed[f, par] = jnp.where(lane >= STRIP * seg, y, packed[f, par])
+                        packed[f, par] = jnp.where(half_lane >= EDGE * seg, y, packed[f, par])
         for (f, par), y in packed.items():
             strip_ref[group, f, par] = y
 
@@ -67,9 +81,11 @@
     return pl.pallas_call(
         prep_kernel,
         out_shape=(out(rows), out(DEPTH), out(DEPTH), out(rows // SEGS)),
-        in_specs=[pl.BlockSpec(memory_space=pltpu.SMEM)] + [vmem] * 4,
+        in_specs=[pl.BlockSpec(memory_space=pltpu.SMEM)] + [pl.BlockSpec(memory_space=pltpu.HBM)] * 4,
         out_specs=(vmem,) * 4,
-        compiler_params=pltpu.CompilerParams(vmem_limit_bytes=VMEM_BYTES),
+        scratch_shapes=[pltpu.VMEM(x.shape, x.dtype) for x in (right, scale, land, bottom)]
+        + [pltpu.SemaphoreType.DMA((4,))],
+        compiler_params=pltpu.CompilerParams(vmem_limit_bytes=63 * 1024 * 1024),
         name="prep",
     )(core, right, scale, land, bottom)
 
@@ -77,17 +93,17 @@
 def main_kernel(
     core_ref, own_ref, west_ref, east_ref, strip_ref, strip_w_ref, strip_e_ref,
     u_ref, r_ref, part_ref,
-    w_ref, v_ref, p_ref, q_ref, ce_ref, cn_ref, ca_ref, cb_ref, d1_ref, d0_ref, hw_ref,
+    w_ref, v_ref, p_ref, q_ref, ce_ref, cn_ref, cl_ref, ca_ref, cb_ref, d1_ref, d0_ref, hw_ref,
 ):
     rows = own_ref.shape[0]
     total = rows + 2 * DEPTH
     core = core_ref[0]
     sub = lax.broadcasted_iota(jnp.int32, (SUB, LANES), 0)
     lane = lax.broadcasted_iota(jnp.int32, (SUB, LANES), 1)
-    base = core * (LANES - STRIP)
-    in_strip = (lane >= base) & (lane < base + STRIP)
-    first_lane = lane == 0
-    last_lane = lane == LANES - 1
+    base = WIDE + core * (WIDE - EDGE)
+    left = lane < WIDE
+    in_even = (lane >= base) & (lane < base + EDGE)
+    in_odd = (lane >= base - WIDE) & (lane < base - WIDE + EDGE)
 
     def unpack(r, f, par):
         row = r - DEPTH
@@ -100,24 +116,25 @@
         else:
             ref, k, row = east_ref, row - rows, row - rows
             strips = strip_e_ref
-        shift = lax.rem(base + (LANES - STRIP * (row % SEGS)), LANES)
+        shift = lax.rem(base + (LANES - EDGE * (row % SEGS)), LANES)
         far = pltpu.roll(strips[row // SEGS, f, par], shift, 1)
-        return ref[k, f, par], jnp.where(in_strip, far, 0.0)
+        near = ref[k, f, par]
+        even = jnp.where(left, near, jnp.where(in_even, far, 0.0))
+        odd = jnp.where(left, jnp.where(in_odd, far, 0.0), near)
+        return even, pltpu.roll(odd, WIDE, 1)
 
     for r in range(total):
         for par in range(2):
             for f, ref in enumerate((w_ref, v_ref)):
-                near, far = unpack(r, f, par)
-                ref[r, par] = near
-                ref[r, 2 + par] = far
+                even, odd = unpack(r, f, par)
+                ref[r, par] = even
+                ref[r, 2 + par] = odd
 
     def north(x):
-        a, b = (pltpu.roll(t, LANES - 1, 1) for t in x)
-        return jnp.where(last_lane, b, a), jnp.where(last_lane, a, b)
+        return pltpu.roll(x, LANES - 1, 1)
 
     def south(x):
-        a, b = (pltpu.roll(t, 1, 1) for t in x)
-        return jnp.where(first_lane, b, a), jnp.where(first_lane, a, b)
+        return pltpu.roll(x, 1, 1)
 
     def up(x):
         return pltpu.roll(x, SUB - 1, 0)
@@ -128,68 +145,63 @@
     def conduct(x, y, factor):
         return jnp.where(jnp.minimum(x, y) > 0.0, (x + y) * (factor / HALF), 0.0)
 
-    def coefs(r, _):
+    def coefs(r):
         w = [w_ref[r, t] for t in range(4)]
-        ahead = jnp.minimum(r + 1, total - 1)
-        for t in range(4):
-            ce_ref[r, t] = conduct(w[t], w_ref[ahead, t], 0.5)
-            hw = w[t] * (helm_shift / HALF)
-            hw_ref[r, t] = hw
-            d0_ref[r, t] = MU - hw
-            d1_ref[r, t] = 2.0 * MU - hw
+        ahead = min(r + 1, total - 1)
+        lat = [None] * 4
         for par in range(2):
-            x = (w[par], w[2 + par])
-            for side, y in enumerate(north(x)):
-                cn_ref[r, 2 * side + par] = conduct(x[side], y, 0.5)
+            even, odd = w[par], w[2 + par]
+            cl_ref[r, par] = conduct(even, odd, 0.5)
+            lat[2 + par] = conduct(odd, north(even), 0.5)
+            lat[par] = south(lat[2 + par])
+            cn_ref[r, par] = lat[par]
+            cn_ref[r, 2 + par] = lat[2 + par]
         for side in range(2):
             even, odd = w[2 * side], w[2 * side + 1]
             ca_ref[r, side] = conduct(even, odd, 0.5 * vert_ratio)
             above = jnp.where(sub == SUB - 1, 0.0, up(even))
-            cb_ref[r, side] = conduct(odd, above, 0.5 * vert_ratio)
-        return 0
-
-    lax.fori_loop(0, total, coefs, 0)
+            cb = conduct(odd, above, 0.5 * vert_ratio)
+            cb_ref[r, 2 * side] = down(cb)
+            cb_ref[r, 2 * side + 1] = cb
+            lat[2 * side] = lat[2 * side] + down(cb)
+            lat[2 * side + 1] = lat[2 * side + 1] + cb
+        for t in range(4):
+            ce_ref[r, t] = conduct(w[t], w_ref[ahead, t], 0.5)
+            hw = w[t] * (helm_shift / HALF) + lat[t]
+            hw_ref[r, t] = hw
+            d0_ref[r, t] = MU - hw
+            d1_ref[r, t] = 2.0 * MU - hw
+
+    for r in range(total):
+        coefs(r)
 
     def apply(src, dst, level, finish):
-        def row_step(r, now, flux_w):
+        last_flux = [ce_ref[level - 1, t] * (src[level, t] - src[level - 1, t]) for t in range(4)]
+        now = [src[level, t] for t in range(4)]
+        for r in range(level, total - level):
             ahead = [src[r + 1, t] for t in range(4)]
-            flux_e = [ce_ref[r, t] * (ahead[t] - now[t]) for t in range(4)]
-            acc = [flux_e[t] - flux_w[t] for t in range(4)]
+            flux = [ce_ref[r, t] * (ahead[t] - now[t]) for t in range(4)]
+            acc = [flux[t] - last_flux[t] for t in range(4)]
             for par in range(2):
-                x = (now[par], now[2 + par])
-                n = north(x)
-                flux = [cn_ref[r, 2 * s + par] * (n[s] - x[s]) for s in range(2)]
-                back = south(flux)
-                for s in range(2):
-                    acc[2 * s + par] = acc[2 * s + par] + (flux[s] - back[s])
+                even, odd = now[par], now[2 + par]
+                fl = cl_ref[r, par] * (odd - even)
+                acc[par] = acc[par] + (cn_ref[r, par] * south(odd) + fl)
+                acc[2 + par] = acc[2 + par] + (cn_ref[r, 2 + par] * north(even) - fl)
             for s in range(2):
                 even, odd = now[2 * s], now[2 * s + 1]
                 fa = ca_ref[r, s] * (odd - even)
-                fb = cb_ref[r, s] * (up(even) - odd)
-                acc[2 * s] = acc[2 * s] + (fa - down(fb))
-                acc[2 * s + 1] = acc[2 * s + 1] + (fb - fa)
+                acc[2 * s] = acc[2 * s] + (cb_ref[r, 2 * s] * down(odd) + fa)
+                acc[2 * s + 1] = acc[2 * s + 1] + (cb_ref[r, 2 * s + 1] * up(even) - fa)
             for t in range(4):
                 dst[r, t] = finish(r, t, acc[t], now[t])
-            return ahead, flux_e
-
-        now = [src[level, t] for t in range(4)]
-        flux_w = [ce_ref[level - 1, t] * (now[t] - src[level - 1, t]) for t in range(4)]
-
-        def body(k, carry):
-            now, flux_w = carry[:4], carry[4:]
-            r = level + 2 * k
-            now, flux_w = row_step(r, now, flux_w)
-            now, flux_w = row_step(r + 1, now, flux_w)
-            return tuple(now) + tuple(flux_w)
-
-        lax.fori_loop(0, (total - 2 * level) // 2, body, tuple(now) + tuple(flux_w))
-
-    def dots(k, left):
+            now, last_flux = ahead, flux
+
+    def dots(k, other):
         acc = jnp.zeros((SUB, LANES), jnp.float32)
         for i in range(rows):
-            for par in range(2):
-                acc = acc + left(i, par) * u_ref[k, i, par]
-        return jnp.sum(acc, axis=0, keepdims=True)
+            for t in range(4):
+                acc = acc + other(i, t) * u_ref[k, i, t]
+        return jnp.sum(jnp.where(left, acc, 0.0), axis=0, keepdims=True)
 
     parts = []
     for k in range(ITERS):
@@ -198,14 +210,14 @@
         apply(p_ref, q_ref, level + 2, lambda r, t, g, x: g + d0_ref[r, t] * x + NU * v_ref[r, t])
         apply(q_ref, p_ref, level + 3, lambda r, t, g, x: g + d0_ref[r, t] * x + MU * NU * v_ref[r, t])
         for i in range(rows):
-            for par in range(2):
-                u_ref[k, i, par] = p_ref[i + DEPTH, par]
-        parts.append(dots(k, lambda i, par: v_ref[i + DEPTH, par]))
+            for t in range(4):
+                u_ref[k, i, t] = p_ref[i + DEPTH, t]
+        parts.append(dots(k, lambda i, t: v_ref[i + DEPTH, t]))
         apply(p_ref, v_ref, level + 4, lambda r, t, g, x: v_ref[r, t] - STEP * (hw_ref[r, t] * x - g))
         for i in range(rows):
-            for par in range(2):
-                r_ref[k, i, par] = v_ref[i + DEPTH, par]
-        parts.append(dots(k, lambda i, par: v_ref[i + DEPTH, par]))
+            for t in range(4):
+                r_ref[k, i, t] = v_ref[i + DEPTH, t]
+        parts.append(dots(k, lambda i, t: v_ref[i + DEPTH, t]))
     block = jnp.zeros((SUB, LANES), jnp.float32)
     for j, part in enumerate(parts):
         block = jnp.where(sub == j, part, block)
@@ -217,7 +229,7 @@
     rows = own.shape[0]
     total = rows + 2 * DEPTH
     vmem = pl.BlockSpec(memory_space=pltpu.VMEM)
-    field = jax.ShapeDtypeStruct((ITERS, rows, 2, SUB, LANES), jnp.float32)
+    field = jax.ShapeDtypeStruct((ITERS, rows, 4, SUB, LANES), jnp.float32)
     full = pltpu.VMEM((total, 4, SUB, LANES), jnp.float32)
     half = pltpu.VMEM((total, 2, SUB, LANES), jnp.float32)
     return pl.pallas_call(
@@ -225,7 +237,7 @@
         out_shape=(field, field, jax.ShapeDtypeStruct((peers, SUB, LANES), jnp.float32)),
         in_specs=[pl.BlockSpec(memory_space=pltpu.SMEM)] + [vmem] * 6,
         out_specs=(vmem,) * 3,
-        scratch_shapes=[full] * 6 + [half] * 2 + [full] * 3,
+        scratch_shapes=[full] * 6 + [half] * 2 + [full] * 4,
         compiler_params=pltpu.CompilerParams(vmem_limit_bytes=VMEM_BYTES),
         name="krylov",
     )(core, own, west, east, strip, strip_w, strip_e)
@@ -286,15 +298,23 @@
         res = add_scaled(res, -alpha, times_t(direction))
         gamma = gamma_now
     sol = [x * (STEP / HALF) for x in sol]
+    lane = lax.broadcasted_iota(jnp.int32, (SUB, LANES), 1)
+    left = lane < WIDE
+    mixed = WIDE * (lane % 2) + lane // 2
     for i in range(rows):
         for par in range(2):
             at = pl.ds(par * rows + i, SUB, stride=2 * rows)
-            x = sol[0] * u_ref[0, i, par]
-            y = res[0] * own_ref[i, 1, par]
-            for k in range(ITERS):
-                if k:
-                    x = x + sol[k] * u_ref[k, i, par]
-                y = y + res[k + 1] * r_ref[k, i, par]
+            pair = []
+            for t in (par, 2 + par):
+                x = sol[0] * u_ref[0, i, t]
+                y = res[1] * r_ref[0, i, t]
+                for k in range(1, ITERS):
+                    x = x + sol[k] * u_ref[k, i, t]
+                    y = y + res[k + 1] * r_ref[k, i, t]
+                pair.append((x, y))
+            x, y = (jnp.where(left, even, pltpu.roll(odd, WIDE, 1)) for even, odd in zip(*pair))
+            x = take_lanes(x, mixed)
+            y = take_lanes(y + res[0] * own_ref[i, 1, par], mixed)
             sol_ref[at, :] = x
             res_ref[at, :] = y
 
@@ -318,7 +338,7 @@
     lon = lax.axis_size("lon")
     lat = lax.axis_size("lat")
     assert levels == 2 * SUB and lats == LANES and lat == 2
-    assert rows % SEGS == 0 and rows >= DEPTH and STRIP >= DEPTH
+    assert rows % SEGS == 0 and rows >= DEPTH and 2 * EDGE >= DEPTH
     both = ("lon", "lat")
     place = lambda i, j: (i % lon) * lat + j
     east = [(place(i, j), place(i + 1, j)) for i in range(lon) for j in range(lat)]

time: 59.9 us -> 35.3 us (0.59)
  Pallas kernels: 29.5 us -> 7.01 us
  local copies, waits for them, and re-layouts: 3.19 us -> 0.95 us
    pallas_call x1, Pallas kernels: 28.2 us -> 3.74 us  [main(): pl.pallas_call(main_kernel, out_shape=(field, field, jax.ShapeDtypeStruct...]
    unnamed x8 -> x4, local copies, waits for them, and re-layouts: 3.19 us -> 0.95 us
    pallas_call x1, Pallas kernels: 0.25 us -> 2.11 us  [prep(): pl.pallas_call(prep_kernel, out_shape=(out(rows), out(DEPTH), out(DEPTH),...]
where the time goes in v2:
time: 35.3 us; the launch traced here: 35.1 us
  blocking collectives  11.6 us (33%)
  starting transfers between devices  8.17 us (23%)
  Pallas kernels  7.01 us (20%)
  waiting for transfers between devices  6.65 us (19%)
  local copies, waits for them, and re-layouts  0.95 us (3%)
  between operations  0.66 us (2%)
    all_to_all x1, blocking collectives, local(): sums = lax.all_to_all(parts, both, 0, 0)  11.6 us
    ppermute x1, waiting for transfers between devices, local(): strip_e = lax.ppermute(strip, both, west_x)  5.18 us
    pallas_call x1, Pallas kernels, main(): pl.pallas_call(main_kernel, out_shape=(field, field, jax.ShapeDtypeStruct...  3.74 us
    ppermute x1, starting transfers between devices, local(): from_east = lax.ppermute(bwd, both, west)  3.1 us
    ppermute x1, starting transfers between devices, local(): from_west = lax.ppermute(fwd, both, east)  2.99 us
    pallas_call x1, Pallas kernels, prep(): pl.pallas_call(prep_kernel, out_shape=(out(rows), out(DEPTH), out(DEPTH),...  2.11 us
    ppermute x1, waiting for transfers between devices, local(): from_east = lax.ppermute(bwd, both, west)  1.46 us
    pallas_call x1, Pallas kernels, last(): pl.pallas_call(last_kernel, out_shape=(out, out), in_specs=[vmem] * 4, ou...  1.15 us
  transfers between devices with their start and end apart: 5, of which 2 were waited for; matrix products, arithmetic and copies ran while one was open for 0% of the time, Pallas kernels for 0%

profile of v2, /device:TPU:0, one launch (start us, length us, event | category | flops | bytes accessed | tf_op | source)
XLA Modules:
  0.0 35.1 jit_solution(10611255631811931217)
XLA Ops:
  0.6 2.1 %prep.1 = (f32[16,2,2,8,128]{4,3,2,1,0:T(8,128)}, f32[12,2,2,8,128]{4,3,2,1,0:T(8,128)}, f32[12,2,2,8,128]{4,3,2,1,0:T(8,128)}, f32[2,2,2,8,128]{4,3,2,1,0:T(8,128)}) custom-call(s32[1]{0:T(128)} %bitcast.core_ref, f32[256,128]{1,0:T(8,128)} %bitcast.5, f32[256,128]{1,0:T(8,128)} %bitcast.6, s32[16,128]{1,0:T(8,128)} %refs_2_.1, s32[16,128]{1,0:T(8,128)} %refs_3_.1), custom_call_target="tpu_custom_call" | custom-call | tf_op jit(solution)/shard_map/prep/pallas_call | solution.py:81
  2.8 3.0 %collective-permute-start = (f32[12,2,2,8,128]{4,3,2,1,0:T(8,128)}, f32[12,2,2,8,128]{4,3,2,1,0:T(8,128)S(1)}, u32[]{:S(2)}, u32[]{:S(2)}) collective-permute-start(f32[12,2,2,8,128]{4,3,2,1,0:T(8,128)} %get-tuple-element.12), channel_id=1, source_target_pairs={{0,2},{1,3},{2,4},{3,5},{4,6},{5,7},{6,8},{7,9},{8,10},{9,11},{10,... | collective-permute-start | bytes 589832 | tf_op jit(solution)/shard_map/ppermute | solution.py:358
  5.7 3.1 %collective-permute-start.1 = (f32[12,2,2,8,128]{4,3,2,1,0:T(8,128)}, f32[12,2,2,8,128]{4,3,2,1,0:T(8,128)S(1)}, u32[]{:S(2)}, u32[]{:S(2)}) collective-permute-start(f32[12,2,2,8,128]{4,3,2,1,0:T(8,128)} %get-tuple-element.13), channel_id=1, source_target_pairs={{0,14},{1,15},{2,0},{3,1},{4,2},{5,3},{6,4},{7,5},{8,6},{9,7},{10,... | collective-permute-start | bytes 589832 | tf_op jit(solution)/shard_map/ppermute | solution.py:359
  8.8 0.8 %collective-permute-start.4 = (f32[2,2,2,8,128]{4,3,2,1,0:T(8,128)}, f32[2,2,2,8,128]{4,3,2,1,0:T(8,128)S(1)}, u32[]{:S(2)}, u32[]{:S(2)}) collective-permute-start(f32[2,2,2,8,128]{4,3,2,1,0:T(8,128)} %get-tuple-element.14), channel_id=1, source_target_pairs={{0,15},{1,14},{2,1},{3,0},{4,3},{5,2},{6,5},{7,4},{8,7},{9,6},{10,... | collective-permute-start | bytes 98312 | tf_op jit(solution)/shard_map/ppermute | solution.py:361
  9.7 0.9 %collective-permute-start.3 = (f32[2,2,2,8,128]{4,3,2,1,0:T(8,128)}, f32[2,2,2,8,128]{4,3,2,1,0:T(8,128)S(1)}, u32[]{:S(2)}, u32[]{:S(2)}) collective-permute-start(f32[2,2,2,8,128]{4,3,2,1,0:T(8,128)} %get-tuple-element.14), channel_id=1, source_target_pairs={{0,3},{1,2},{2,5},{3,4},{4,7},{5,6},{6,9},{7,8},{8,11},{9,10},{10,... | collective-permute-start | bytes 98312 | tf_op jit(solution)/shard_map/ppermute | solution.py:360
  10.6 0.3 collective-permute-start.2
  10.9 5.2 %collective-permute-done.4.strip_e_ref = f32[2,2,2,8,128]{4,3,2,1,0:T(8,128)S(1)} collective-permute-done((f32[2,2,2,8,128]{4,3,2,1,0:T(8,128)}, f32[2,2,2,8,128]{4,3,2,1,0:T(8,128)S(1)}, u32[]{:S(2)}, u32[]{:S(2)}) %collective-permute-start.4) | collective-permute-done | bytes 32800 | tf_op jit(solution)/shard_map/ppermute | solution.py:361
  16.1 0.0 collective-permute-done.3.strip_w_ref
  16.1 0.0 collective-permute-done.2.strip_ref
  16.1 0.0 collective-permute-done.west_ref
  16.1 1.5 %collective-permute-done.1.east_ref = f32[12,2,2,8,128]{4,3,2,1,0:T(8,128)S(1)} collective-permute-done((f32[12,2,2,8,128]{4,3,2,1,0:T(8,128)}, f32[12,2,2,8,128]{4,3,2,1,0:T(8,128)S(1)}, u32[]{:S(2)}, u32[]{:S(2)}) %collective-permute-start.1) | collective-permute-done | bytes 196640 | tf_op jit(solution)/shard_map/ppermute | solution.py:359
  17.6 0.0 copy-start
  17.6 0.9 %copy-done = f32[16,2,2,8,128]{4,3,2,1,0:T(8,128)S(1)} copy-done((f32[16,2,2,8,128]{4,3,2,1,0:T(8,128)S(1)}, f32[16,2,2,8,128]{4,3,2,1,0:T(8,128)}, u32[]{:S(2)}) %copy-start) | copy-done | bytes 262168
  18.5 0.0 copy-start.1
  18.5 3.7 %krylov.1 = (f32[3,16,4,8,128]{4,3,2,1,0:T(8,128)S(1)}, f32[3,16,4,8,128]{4,3,2,1,0:T(8,128)S(1)}, f32[16,8,128]{2,1,0:T(8,128)S(1)}) custom-call(s32[1]{0:T(128)} %bitcast.core_ref, f32[16,2,2,8,128]{4,3,2,1,0:T(8,128)S(1)} %copy-done, f32[12,2,2,8,128]{4,3,2,1,0:T(8,128)S(1)} %collective-permute-done.west_ref, ...), custom_call_target="tpu_custom_call" | custom-call | tf_op jit(solution)/shard_map/krylov/pallas_call | solution.py:235
  22.3 11.6 %all_to_all.5.sums_ref = f32[16,8,128]{2,1,0:T(8,128)S(1)} all-to-all(f32[16,8,128]{2,1,0:T(8,128)S(1)} %get-tuple-element.15), channel_id=1, replica_groups=mesh['member'=2,'lon'=8,'lat'=2] {'lon','lat'}, dimensions={0} | all-to-all | bytes 131072 | tf_op jit(solution)/shard_map/all_to_all | solution.py:364
  33.9 0.0 copy-done.1
  33.9 1.2 %combine.1 = (f32[256,128]{1,0:T(8,128)}, f32[256,128]{1,0:T(8,128)}) custom-call(f32[16,8,128]{2,1,0:T(8,128)S(1)} %all_to_all.5.sums_ref, f32[16,2,2,8,128]{4,3,2,1,0:T(8,128)S(1)} %copy-done.1, f32[3,16,4,8,128]{4,3,2,1,0:T(8,128)S(1)} %get-tuple-element.16.u_ref, f32[3,16,4,8,128]{4,3,2,1,0:T(8,128)S(1)} %get-tuple-element.17.r_ref), custom_call_target="tpu_custom_call" | custom-call | tf_op jit(solution)/shard_map/combine/pallas_call | solution.py:326
Async XLA Ops:
  2.8 13.4 %collective-permute-start = (f32[12,2,2,8,128]{4,3,2,1,0:T(8,128)}, f32[12,2,2,8,128]{4,3,2,1,0:T(8,128)S(1)}, u32[]{:S(2)}, u32[]{:S(2)}) collective-permute-start(f32[12,2,2,8,128]{4,3,2,1,0:T(8,128)} %get-tuple-element.12), channel_id=1, source_target_pairs={{0,2},{1,3},{2,4},{3,5},{4,6},{5,7},{6,8},{7,9},{8,10},{9,11},{10,... | collective-permute-start | bytes 589832 | tf_op jit(solution)/shard_map/ppermute | solution.py:358
  5.7 11.8 %collective-permute-start.1 = (f32[12,2,2,8,128]{4,3,2,1,0:T(8,128)}, f32[12,2,2,8,128]{4,3,2,1,0:T(8,128)S(1)}, u32[]{:S(2)}, u32[]{:S(2)}) collective-permute-start(f32[12,2,2,8,128]{4,3,2,1,0:T(8,128)} %get-tuple-element.13), channel_id=1, source_target_pairs={{0,14},{1,15},{2,0},{3,1},{4,2},{5,3},{6,4},{7,5},{8,6},{9,7},{10,... | collective-permute-start | bytes 589832 | tf_op jit(solution)/shard_map/ppermute | solution.py:359
  8.8 7.3 %collective-permute-start.4 = (f32[2,2,2,8,128]{4,3,2,1,0:T(8,128)}, f32[2,2,2,8,128]{4,3,2,1,0:T(8,128)S(1)}, u32[]{:S(2)}, u32[]{:S(2)}) collective-permute-start(f32[2,2,2,8,128]{4,3,2,1,0:T(8,128)} %get-tuple-element.14), channel_id=1, source_target_pairs={{0,15},{1,14},{2,1},{3,0},{4,3},{5,2},{6,5},{7,4},{8,7},{9,6},{10,... | collective-permute-start | bytes 98312 | tf_op jit(solution)/shard_map/ppermute | solution.py:361
  9.7 6.4 %collective-permute-start.3 = (f32[2,2,2,8,128]{4,3,2,1,0:T(8,128)}, f32[2,2,2,8,128]{4,3,2,1,0:T(8,128)S(1)}, u32[]{:S(2)}, u32[]{:S(2)}) collective-permute-start(f32[2,2,2,8,128]{4,3,2,1,0:T(8,128)} %get-tuple-element.14), channel_id=1, source_target_pairs={{0,3},{1,2},{2,5},{3,4},{4,7},{5,6},{6,9},{7,8},{8,11},{9,10},{10,... | collective-permute-start | bytes 98312 | tf_op jit(solution)/shard_map/ppermute | solution.py:360
  10.6 5.5 %collective-permute-start.2 = (f32[2,2,2,8,128]{4,3,2,1,0:T(8,128)}, f32[2,2,2,8,128]{4,3,2,1,0:T(8,128)S(1)}, u32[]{:S(2)}, u32[]{:S(2)}) collective-permute-start(f32[2,2,2,8,128]{4,3,2,1,0:T(8,128)} %get-tuple-element.14), channel_id=1, source_target_pairs={{0,1},{1,0},{2,3},{3,2},{4,5},{5,4},{6,7},{7,6},{8,9},{9,8},{10,11... | collective-permute-start | bytes 98312 | tf_op jit(solution)/shard_map/ppermute | solution.py:362
  17.6 1.0 %copy-start = (f32[16,2,2,8,128]{4,3,2,1,0:T(8,128)S(1)}, f32[16,2,2,8,128]{4,3,2,1,0:T(8,128)}, u32[]{:S(2)}) copy-start(f32[16,2,2,8,128]{4,3,2,1,0:T(8,128)} %get-tuple-element.11.own_ref) | copy-start | bytes 786436
  18.5 15.4 %copy-start.1 = (f32[16,2,2,8,128]{4,3,2,1,0:T(8,128)S(1)}, f32[16,2,2,8,128]{4,3,2,1,0:T(8,128)}, u32[]{:S(2)}) copy-start(f32[16,2,2,8,128]{4,3,2,1,0:T(8,128)} %get-tuple-element.11.own_ref) | copy-start | bytes 786436

commit v3 on v0

v3 whole, which is shorter than its diff:
```python
import functools

import jax
import jax.numpy as jnp
from jax import lax
from jax.experimental import pallas as pl
from jax.experimental.pallas import tpu as pltpu
from jax.sharding import PartitionSpec as P

ITERS = 3
CHEB = 3
DEPTH = ITERS * (CHEB + 1)
SUB = 8
LANES = 128
WIDE = LANES // 2
SEGS = 8
EDGE = WIDE // SEGS

helm_shift = 0.05
vert_ratio = 4.0
cheb_low = 4.0
cheb_high = 150.0

CENTRE = 0.5 * (cheb_high + cheb_low)
HALF = 0.5 * (cheb_high - cheb_low)
MU = CENTRE / HALF
NU = MU * MU - 1.0
STEP = 5.0
NAMES = ("ce", "cn", "cl", "ca", "cb", "d1", "d0", "hw")
TILES = dict(ce=4, cn=4, cl=2, ca=2, cb=4, d1=4, d0=4, hw=4)
EVERY = CHEB + 1
SPARE = 2
MIB = 1024 * 1024


def take_lanes(x, index):
    return jnp.take_along_axis(x, index, axis=1, mode="promise_in_bounds")


def spread(ref, index, tiles):
    for t, tile in enumerate(tiles):
        ref[index + (t,)] = tile


def iotas():
    sub = lax.broadcasted_iota(jnp.int32, (SUB, LANES), 0)
    lane = lax.broadcasted_iota(jnp.int32, (SUB, LANES), 1)
    return sub, lane


def column(rows, r, flip):
    return r + flip * (rows - 1 - 2 * r)


def spare_lanes(core):
    _, lane = iotas()
    back = lax.rem(EDGE - SPARE + core * (LANES - 2 * (EDGE - SPARE)), LANES)
    start = (1 - core) * (EDGE - SPARE)
    in_slot = lane % EDGE
    return (in_slot >= start) & (in_slot < start + SPARE), back


def prep_kernel(place_ref, right_ref, scale_ref, own_ref, strip_ref, near_ref, corner_ref):
    rows = own_ref.shape[0]
    core, flip = place_ref[0] % 2, place_ref[0] // 2
    _, lane = iotas()
    half_lane = lane % WIDE
    apart = 2 * half_lane + lane // WIDE
    packed = {}
    for r in range(rows):
        group, seg = divmod(r, SEGS)
        shift = lax.rem(EDGE * seg + (1 - core) * (WIDE + EDGE), LANES)
        for par in range(2):
            at = pl.ds(par * rows + column(rows, r, flip), SUB, stride=2 * rows)
            for f, ref in enumerate((scale_ref, right_ref)):
                x = take_lanes(ref[at, :], apart)
                own_ref[r, f, par] = x
                if r < DEPTH:
                    near_ref[r, f, par] = x
                y = pltpu.roll(x, shift, 1)
                if seg:
                    y = jnp.where(half_lane >= EDGE * seg, y, packed[group, f, par])
                packed[group, f, par] = y
    for (group, f, par), y in packed.items():
        strip_ref[group, f, par] = y
    spare, back = spare_lanes(1 - core)
    for f in range(2):
        for par in range(2):
            first, second = packed[0, f, par], packed[1, f, par]
            corner_ref[f, par] = jnp.where(spare, pltpu.roll(second, back, 1), first)


def prep(place, right, scale, rows):
    vmem = pl.BlockSpec(memory_space=pltpu.VMEM)
    return pl.pallas_call(
        prep_kernel,
        out_shape=(tiles_of(rows, 2, 2), tiles_of(rows // SEGS, 2, 2), tiles_of(DEPTH, 2, 2), tiles_of(2, 2)),
        in_specs=[pl.BlockSpec(memory_space=pltpu.SMEM)] + [vmem] * 2,
        out_specs=(vmem,) * 4,
        compiler_params=pltpu.CompilerParams(vmem_limit_bytes=8 * MIB),
        name="prep",
    )(place, right, scale)


def pack_kernel(place_ref, own_ref, strip_ref, near_corner_ref, far_corner_ref, far_ref):
    rows = own_ref.shape[0]
    spare, back = spare_lanes(place_ref[0] % 2)
    for f in range(2):
        for par in range(2):
            for dist in range(1, DEPTH + 1):
                far_ref[dist - 1, f, par] = own_ref[rows - dist, f, par]
            first, second = strip_ref[0, f, par], strip_ref[1, f, par]
            far_corner_ref[f, par] = jnp.where(spare, pltpu.roll(first, back, 1), second)


def pack(place, own, strip, corner):
    vmem = pl.BlockSpec(memory_space=pltpu.VMEM)
    return pl.pallas_call(
        pack_kernel,
        out_shape=(tiles_of(2, 2), tiles_of(DEPTH, 2, 2)),
        in_specs=[pl.BlockSpec(memory_space=pltpu.SMEM)] + [vmem] * 3,
        out_specs=(vmem,) * 2,
        compiler_params=pltpu.CompilerParams(vmem_limit_bytes=8 * MIB),
        cost_estimate=pl.CostEstimate(flops=20000000, bytes_accessed=16 * MIB, transcendentals=0),
        name="pack",
    )(place, own, strip, corner)


def tiles_of(*n):
    return jax.ShapeDtypeStruct(n + (SUB, LANES), jnp.float32)


def conduct(x, y, factor):
    return jnp.where(jnp.minimum(x, y) > 0.0, (x + y) * (factor / HALF), 0.0)


def north(x):
    return pltpu.roll(x, LANES - 1, 1)


def south(x):
    return pltpu.roll(x, 1, 1)


def up(x):
    return pltpu.roll(x, SUB - 1, 0)


def down(x):
    return pltpu.roll(x, 1, 0)


class Lanes:
    def __init__(self, core):
        sub, lane = iotas()
        self.core = core
        self.base = WIDE + core * (WIDE - EDGE)
        self.left = lane < WIDE
        self.in_even = (lane >= self.base) & (lane < self.base + EDGE)
        self.in_odd = (lane >= self.base - WIDE) & (lane < self.base - WIDE + EDGE)

    def split(self, near, far, slot, spare=False):
        if far is None:
            even, odd = jnp.where(self.left, near, 0.0), jnp.where(self.left, 0.0, near)
        else:
            shift = self.base + (LANES - EDGE * slot)
            if spare:
                shift = shift + (LANES - (EDGE - SPARE)) + 2 * self.core * (EDGE - SPARE)
            far = pltpu.roll(far, lax.rem(shift, LANES), 1)
            even = jnp.where(self.left, near, jnp.where(self.in_even, far, 0.0))
            odd = jnp.where(self.left, jnp.where(self.in_odd, far, 0.0), near)
        return even, pltpu.roll(odd, WIDE, 1)

    def tiles(self, ref, row, far_of, slot, spare, f):
        e0, o0 = self.split(ref[row, f, 0], far_of(f, 0), slot, spare)
        e1, o1 = self.split(ref[row, f, 1], far_of(f, 1), slot, spare)
        return [e0, e1, o0, o1]

    def own(self, ref, strip_ref, r, f):
        group, slot = divmod(r, SEGS)
        return self.tiles(ref, r, lambda f, par: strip_ref[group, f, par], slot, False, f)

    def beyond(self, ref, corner, dist, f, near):
        slot = (dist - 1) % SEGS
        if not near:
            slot = SEGS - 1 - slot
        far = corner if dist < DEPTH else (lambda f, par: None)
        return self.tiles(ref, dist - 1, far, slot, dist > SEGS, f)


def row_coefs(w):
    sub, _ = iotas()
    out = {name: [None] * n for name, n in TILES.items() if name != "ce"}
    lat = [None] * 4
    for par in range(2):
        even, odd = w[par], w[2 + par]
        out["cl"][par] = conduct(even, odd, 0.5)
        lat[2 + par] = conduct(odd, north(even), 0.5)
        lat[par] = south(lat[2 + par])
    out["cn"] = list(lat)
    for side in range(2):
        even, odd = w[2 * side], w[2 * side + 1]
        out["ca"][side] = conduct(even, odd, 0.5 * vert_ratio)
        above = jnp.where(sub == SUB - 1, 0.0, up(even))
        cb = conduct(odd, above, 0.5 * vert_ratio)
        out["cb"][2 * side : 2 * side + 2] = [down(cb), cb]
    for t in range(4):
        hw = w[t] * (helm_shift / HALF) + (lat[t] + out["cb"][t])
        out["hw"][t] = hw
        out["d0"][t] = MU - hw
        out["d1"][t] = 2.0 * MU - hw
    return out


def sweep(span, step, read, write, coef):
    turn, stage = divmod(step - 1, EVERY)
    first = span[0]
    before, now = read(step - 1, first - 1), read(step - 1, first)
    last_flux = [coef("ce", first - 1, t) * (now[t] - before[t]) for t in range(4)]
    for r in span:
        ahead = read(step - 1, r + 1)
        flux = [coef("ce", r, t) * (ahead[t] - now[t]) for t in range(4)]
        acc = [flux[t] - last_flux[t] for t in range(4)]
        for par in range(2):
            even, odd = now[par], now[2 + par]
            fl = coef("cl", r, par) * (odd - even)
            acc[par] = acc[par] + (coef("cn", r, par) * south(odd) + fl)
            acc[2 + par] = acc[2 + par] + (coef("cn", r, 2 + par) * north(even) - fl)
        for s in range(2):
            even, odd = now[2 * s], now[2 * s + 1]
            fa = coef("ca", r, s) * (odd - even)
            acc[2 * s] = acc[2 * s] + (coef("cb", r, 2 * s) * down(odd) + fa)
            acc[2 * s + 1] = acc[2 * s + 1] + (coef("cb", r, 2 * s + 1) * up(even) - fa)
        v = read(turn * EVERY, r) if stage else None
        out = []
        for t in range(4):
            if stage == 0:
                y = acc[t] + coef("d1", r, t) * now[t]
            elif stage < CHEB:
                y = acc[t] + coef("d0", r, t) * now[t] + (NU if stage == 1 else MU * NU) * v[t]
            else:
                y = v[t] - STEP * (coef("hw", r, t) * now[t] - acc[t])
            out.append(y)
        write(step, r, out)
        now, last_flux = ahead, flux


class Moments:
    def __init__(self):
        self.acc = [[None] * 4 for _ in range(2 * ITERS)]

    def add(self, j, x, y):
        for t in range(4):
            term = x[t] * y[t]
            self.acc[j][t] = term if self.acc[j][t] is None else self.acc[j][t] + term

    def step(self, step, r, tiles, read):
        turn, stage = divmod(step - 1, EVERY)
        if stage == CHEB - 1:
            self.add(2 * turn, tiles, read(turn * EVERY, r))
        elif stage == CHEB:
            self.add(2 * turn + 1, tiles, read(step - 1, r))

    def total(self, j):
        a, b, c, d = self.acc[j]
        return (a + b) + (c + d)


def first_u(rows, k):
    return rows - (k * EVERY + CHEB), rows - (k + 1) * EVERY


def near_kernel(place_ref, own_ref, near_ref, corner_ref, strip_ref, *refs):
    rows = own_ref.shape[0]
    edge_ref, kept_ref, u_ref, r_ref, part_ref = refs[:5]
    coef_refs = dict(zip(NAMES, refs[5:13]))
    w_ref, v_ref, p_ref, q_ref = refs[13:]
    lanes = Lanes(place_ref[0] % 2)
    bufs = (v_ref, p_ref, q_ref, p_ref)

    def read(step, r):
        return [bufs[step % EVERY][r + DEPTH, t] for t in range(4)]

    def coef(name, r, t):
        return coef_refs[name][r + DEPTH, t]

    sums = Moments()

    def write(step, r, tiles):
        spread(bufs[step % EVERY], (r + DEPTH,), tiles)

    def keep(step):
        turn, stage = divmod(step - 1, EVERY)
        first = max(rows - EVERY - step, -DEPTH + step)
        for r in range(first, rows - step):
            tiles = read(step, r)
            if r >= rows - 2 - step:
                spread(edge_ref, (step, r - (rows - 2 - step)), tiles)
            if step % EVERY == 0:
                spread(kept_ref, (step // EVERY, r - (rows - EVERY - step)), tiles)

    for f, ref in enumerate((w_ref, v_ref)):
        for r in range(-DEPTH, rows):
            if r < 0:
                tiles = lanes.beyond(near_ref, lambda f, par: corner_ref[f, par], -r, f, True)
            else:
                tiles = lanes.own(own_ref, strip_ref, r, f)
            spread(ref, (r + DEPTH,), tiles)
    fill_coefs(coef_refs, w_ref)
    keep(0)
    for step in range(1, DEPTH + 1):
        turn, stage = divmod(step - 1, EVERY)
        sweep(range(step - DEPTH, rows - step), step, read, write, coef)
        if step < DEPTH:
            keep(step)
        for r in range(rows - step):
            tiles = read(step, r)
            if stage == CHEB - 1:
                spread(u_ref, (turn, r), tiles)
            elif stage == CHEB:
                spread(r_ref, (turn, r), tiles)
            sums.step(step, r, tiles, read)
    for j in range(2 * ITERS):
        part_ref[j] = sums.total(j)


def fill_coefs(coef_refs, w_ref):
    total = w_ref.shape[0]
    for k in range(total):
        w = [w_ref[k, t] for t in range(4)]
        for name, tiles in row_coefs(w).items():
            spread(coef_refs[name], (k,), tiles)
        if k < total - 1:
            spread(coef_refs["ce"], (k,), [conduct(w[t], w_ref[k + 1, t], 0.5) for t in range(4)])


def coef_scratch(total):
    return [pltpu.VMEM((total, TILES[name], SUB, LANES), jnp.float32) for name in NAMES]


def near_side(place, own, near, corner, strip):
    rows = own.shape[0]
    vmem = pl.BlockSpec(memory_space=pltpu.VMEM)
    outs = [tiles_of(DEPTH, 2, 4), tiles_of(ITERS, EVERY, 4)]
    outs += [tiles_of(ITERS, rows, 4)] * 2 + [tiles_of(2 * ITERS)]
    full = [pltpu.VMEM((rows + DEPTH, 4, SUB, LANES), jnp.float32)] * 4
    return pl.pallas_call(
        near_kernel,
        out_shape=outs,
        in_specs=[pl.BlockSpec(memory_space=pltpu.SMEM)] + [vmem] * 4,
        out_specs=[vmem] * len(outs),
        scratch_shapes=coef_scratch(rows + DEPTH) + full,
        compiler_params=pltpu.CompilerParams(vmem_limit_bytes=16 * MIB),
        cost_estimate=pl.CostEstimate(flops=20000000, bytes_accessed=4 * MIB, transcendentals=0),
        name="near_side",
    )(place, own, near, corner, strip)


def far_kernel(place_ref, own_ref, far_ref, corner_ref, strip_ref, edge_ref, kept_ref, part_in_ref, *refs):
    u_ref, r_ref, part_ref = refs[:3]
    coef_refs = dict(zip(NAMES, refs[3:11]))
    w_ref, v_ref, p_ref, q_ref = refs[11:]
    rows = own_ref.shape[0]
    base = rows - DEPTH - 1
    lanes = Lanes(place_ref[0] % 2)
    sub, lane = iotas()
    bufs = (v_ref, p_ref, q_ref, p_ref)

    def read(step, r):
        if r >= rows - step:
            return [bufs[step % EVERY][r, t] for t in range(4)]
        if r >= rows - 2 - step:
            return [edge_ref[step, r - (rows - 2 - step), t] for t in range(4)]
        return [kept_ref[step // EVERY, r - (rows - EVERY - step), t] for t in range(4)]

    def coef(name, r, t):
        return coef_refs[name][r - base, t]

    sums = Moments()

    def write(step, r, tiles):
        spread(bufs[step % EVERY], (r,), tiles)

    for r in range(base, rows + DEPTH):
        if r < rows:
            w = lanes.own(own_ref, strip_ref, r, 0)
        else:
            w, v = (
                lanes.beyond(far_ref, lambda f, par: corner_ref[f, par], r - rows + 1, f, False) for f in range(2)
            )
            spread(v_ref, (r,), v)
        spread(w_ref, (r - base,), w)
    fill_coefs(coef_refs, w_ref)
    for step in range(1, DEPTH + 1):
        turn, stage = divmod(step - 1, EVERY)
        sweep(range(rows - step, rows + DEPTH - step), step, read, write, coef)
        for r in range(rows - step, rows):
            tiles = read(step, r)
            if stage == CHEB - 1:
                spread(u_ref, (turn, r), tiles)
            elif stage == CHEB:
                spread(r_ref, (turn, r), tiles)
            sums.step(step, r, tiles, read)
    block = jnp.zeros((SUB, LANES), jnp.float32)
    for j in range(2 * ITERS):
        part = jnp.where(lanes.left, sums.total(j) + part_in_ref[j], 0.0)
        block = jnp.where(sub == j, jnp.sum(part, axis=0, keepdims=True), block)
    block = jnp.broadcast_to(jnp.sum(block, axis=1, keepdims=True), (SUB, LANES))
    row = jnp.sum(jnp.where(sub == lane, block, 0.0), axis=0, keepdims=True)
    row = jnp.broadcast_to(row, (SUB, LANES))
    for n in range(0, part_ref.shape[0], SUB):
        part_ref[n : n + SUB, :] = row


def far_side(place, own, far, corner, strip, edge, kept, part, peers):
    rows = own.shape[0]
    vmem = pl.BlockSpec(memory_space=pltpu.VMEM)
    outs = [tiles_of(ITERS, rows, 4)] * 2 + [jax.ShapeDtypeStruct((peers, LANES), jnp.float32)]
    full = [pltpu.VMEM((2 * DEPTH + 1, 4, SUB, LANES), jnp.float32)]
    full += [pltpu.VMEM((rows + DEPTH, 4, SUB, LANES), jnp.float32)] * 3
    return pl.pallas_call(
        far_kernel,
        out_shape=outs,
        in_specs=[pl.BlockSpec(memory_space=pltpu.SMEM)] + [vmem] * 7,
        out_specs=[vmem] * 3,
        scratch_shapes=coef_scratch(2 * DEPTH + 1) + full,
        compiler_params=pltpu.CompilerParams(vmem_limit_bytes=16 * MIB),
        cost_estimate=pl.CostEstimate(flops=15000000, bytes_accessed=4 * MIB, transcendentals=0),
        name="far_side",
    )(place, own, far, corner, strip, edge, kept, part)


def times_t(poly):
    out = [poly[0]]
    for i in range(1, len(poly)):
        out.append(poly[i] - poly[i - 1])
    out.append(-poly[-1])
    return out


def add_scaled(left, factor, right):
    out = []
    for i in range(max(len(left), len(right))):
        if i >= len(right):
            out.append(left[i])
        elif i >= len(left):
            out.append(factor * right[i])
        else:
            out.append(left[i] + factor * right[i])
    return out


def inner(left, right, moments):
    total = None
    for i, x in enumerate(left):
        for j, y in enumerate(right):
            term = x * y * moments[i + j]
            total = term if total is None else total + term
    return total


def last_kernel(place_ref, sums_ref, own_ref, u_near_ref, r_near_ref, u_far_ref, r_far_ref, sol_ref, res_ref):
    rows = own_ref.shape[0]
    flip = place_ref[0] // 2
    acc = sums_ref[:SUB, :]
    for n in range(SUB, sums_ref.shape[0], SUB):
        acc = acc + sums_ref[n : n + SUB, :]
    acc = jnp.sum(acc, axis=0, keepdims=True)
    moments = [jnp.broadcast_to(acc[:, j : j + 1], (SUB, LANES)) for j in range(2 * ITERS)]
    res = [jnp.ones((SUB, LANES), jnp.float32)]
    direction = res
    sol = None
    gamma = alpha = None
    for turn in range(ITERS):
        gamma_now = inner(res, res, moments)
        delta = inner(times_t(res), res, moments)
        if turn == 0:
            alpha = gamma_now / delta
            sol = [alpha]
        else:
            beta = gamma_now / gamma
            alpha = gamma_now / (delta - beta * gamma_now / alpha)
            direction = add_scaled(res, beta, direction)
            sol = add_scaled(sol, alpha, direction)
        res = add_scaled(res, -alpha, times_t(direction))
        gamma = gamma_now
    sol = [x * (STEP / HALF) for x in sol]
    _, lane = iotas()
    left = lane < WIDE
    mixed = WIDE * (lane % 2) + lane // 2
    for i in range(rows):
        u_refs, r_refs = [], []
        for k in range(ITERS):
            n_u, n_r = first_u(rows, k)
            u_refs.append(u_near_ref if i < n_u else u_far_ref)
            r_refs.append(r_near_ref if i < n_r else r_far_ref)
        for par in range(2):
            at = pl.ds(par * rows + column(rows, i, flip), SUB, stride=2 * rows)
            pair = []
            for t in (par, 2 + par):
                x = sol[0] * u_refs[0][0, i, t]
                y = res[1] * r_refs[0][0, i, t]
                for k in range(1, ITERS):
                    x = x + sol[k] * u_refs[k][k, i, t]
                    y = y + res[k + 1] * r_refs[k][k, i, t]
                pair.append((x, y))
            x, y = (jnp.where(left, even, pltpu.roll(odd, WIDE, 1)) for even, odd in zip(*pair))
            x = take_lanes(x, mixed)
            y = take_lanes(y + res[0] * own_ref[i, 1, par], mixed)
            sol_ref[at, :] = x
            res_ref[at, :] = y


def last(place, sums, own, *vectors):
    rows = own.shape[0]
    vmem = pl.BlockSpec(memory_space=pltpu.VMEM)
    out = jax.ShapeDtypeStruct((2 * SUB * rows, LANES), jnp.float32)
    return pl.pallas_call(
        last_kernel,
        out_shape=(out, out),
        in_specs=[pl.BlockSpec(memory_space=pltpu.SMEM)] + [vmem] * (2 + len(vectors)),
        out_specs=(vmem,) * 2,
        compiler_params=pltpu.CompilerParams(vmem_limit_bytes=48 * MIB),
        name="combine",
    )(place, sums, own, *vectors)


def local(right_side, scale, land_mask, bottom):
    levels, rows, lats = right_side.shape
    lon = lax.axis_size("lon")
    lat = lax.axis_size("lat")
    peers = lon * lat
    assert levels == 2 * SUB and lats == LANES and lat == 2
    assert rows == 2 * SEGS and rows >= DEPTH and 2 * EDGE >= DEPTH
    assert lon % 2 == 0 and peers % SUB == 0
    both = ("lon", "lat")

    def links(to):
        return [(i * lat + j, to(i, j)[0] % lon * lat + to(i, j)[1]) for i in range(lon) for j in range(lat)]

    beyond = lambda i: i + 1 if i % 2 else i - 1
    place = lax.axis_index("lat") + 2 * (1 - lax.axis_index("lon") % 2)
    place = place.astype(jnp.int32).reshape(1)
    depth = lax.broadcasted_iota(jnp.int32, right_side.shape, 0)
    wet = depth < jnp.where(land_mask == 1, bottom, 0)[None]
    right, weight = (jnp.where(wet, x, 0.0).reshape(levels * rows, lats) for x in (right_side, scale))
    own, strip, near, corner = prep(place, right, weight, rows)
    corner = lax.ppermute(corner, both, links(lambda i, j: (i ^ 1, 1 - j)))
    near = lax.ppermute(near, both, links(lambda i, j: (i ^ 1, j)))
    strip = lax.ppermute(strip, both, links(lambda i, j: (i, 1 - j)))
    far_corner, far = pack(place, own, strip, corner)
    far = lax.ppermute(far, both, links(lambda i, j: (beyond(i), j)))
    far_corner = lax.ppermute(far_corner, both, links(lambda i, j: (beyond(i), j)))
    edge, kept, u_near, r_near, part = near_side(place, own, near, corner, strip)
    u_far, r_far, parts = far_side(place, own, far, far_corner, strip, edge, kept, part, peers)
    sums = lax.all_to_all(parts, both, 0, 0, tiled=True)
    sol, res = last(place, sums, own, u_near, r_near, u_far, r_far)
    return sol.reshape(right_side.shape), res.reshape(right_side.shape)


def solution(mesh):
    field = P("member", "lon", "lat")
    mask = P(("member", "lon"), "lat")
    return jax.shard_map(
        local,
        mesh=mesh,
        in_specs=(field, field, mask, mask),
        out_specs=(field, field),
        check_vma=False,
    )
```

time: 270 us -> 34 us (0.13)
  starting transfers between devices: 119 us -> 7.92 us
  blocking collectives: 97.8 us -> 12.1 us
  waiting for transfers between devices: 30 us -> 5.6 us
  between operations: 11.2 us -> 0.68 us
  other arithmetic: 9.26 us -> 0.99 us
  Pallas kernels: 0 us -> 5.67 us
    ppermute x52 -> x5, starting transfers between devices: 119 us -> 7.92 us  [the longest x1 4.72 us: local(): far = lax.ppermute(far, both, links(lambda i, j: (beyond(i), j)))]
    psum x3 -> x0, blocking collectives: 97.8 us -> none  [local(): lax.psum((jnp.sum(residual * smoothed), jnp.sum(applied * smoothed)), ('l...]
    ppermute x52 -> x5, waiting for transfers between devices: 30 us -> 5.6 us  [the longest x1 3.65 us: local(): lax.ppermute(far_corner, both, links(lambda i, j: (beyond(i), j)))]
    all_to_all x0 -> x1, blocking collectives: none -> 12.1 us  [local(): sums = lax.all_to_all(parts, both, 0, 0, tiled=True)]
    pallas_call x0 -> x5, Pallas kernels: none -> 5.67 us  [the longest x1 2.15 us: near_side(): pl.pallas_call(near_kernel, out_shape=outs, in_specs=[pl.BlockSpec(memory...]
    add x9 -> x0, other arithmetic: 3.25 us -> none  [smooth_apply(): iterate = iterate + update]
    reduce_sum x3 -> x0, other arithmetic: 3.02 us -> none  [local(): jnp.sum(applied * smoothed)]
  transfers between devices with their start and end apart: 52 -> 5, of which waited for: 22 -> 3; matrix products, arithmetic and copies ran while one was open for 0% -> 0% of each run, Pallas kernels for 0% -> 7%
where the time goes in v3:
time: 34 us; the launch traced here: 33.7 us
  blocking collectives  12.1 us (36%)
  starting transfers between devices  7.92 us (23%)
  Pallas kernels  5.67 us (17%)
  waiting for transfers between devices  5.6 us (16%)
  other arithmetic  0.99 us (3%)
  local copies, waits for them, and re-layouts  0.69 us (2%)
  between operations  0.68 us (2%)
    all_to_all x1, blocking collectives, local(): sums = lax.all_to_all(parts, both, 0, 0, tiled=True)  12.1 us
    ppermute x1, starting transfers between devices, local(): far = lax.ppermute(far, both, links(lambda i, j: (beyond(i), j)))  4.72 us
    ppermute x1, waiting for transfers between devices, local(): lax.ppermute(far_corner, both, links(lambda i, j: (beyond(i), j)))  3.65 us
    ppermute x1, starting transfers between devices, local(): corner = lax.ppermute(corner, both, links(lambda i, j: (i ^ 1, 1 - j)))  2.61 us
    pallas_call x1, Pallas kernels, near_side(): pl.pallas_call(near_kernel, out_shape=outs, in_specs=[pl.BlockSpec(memory...  2.15 us
    pallas_call x1, Pallas kernels, far_side(): pl.pallas_call(far_kernel, out_shape=outs, in_specs=[pl.BlockSpec(memory_...  1.87 us
    ppermute x1, waiting for transfers between devices, local(): corner = lax.ppermute(corner, both, links(lambda i, j: (i ^ 1, 1 - j)))  1.4 us
    pallas_call x1, Pallas kernels, last(): pl.pallas_call(last_kernel, out_shape=(out, out), in_specs=[pl.BlockSpec(...  1.13 us
  transfers between devices with their start and end apart: 5, of which 3 were waited for; matrix products, arithmetic and copies ran while one was open for 0% of the time, Pallas kernels for 7%

profile of v3, /device:TPU:0, one launch (start us, length us, event | category | flops | bytes accessed | tf_op | source)
XLA Modules:
  0.0 33.7 jit_solution(9093042913700434877)
XLA Ops:
  0.6 0.0 copy-start.1
  0.6 0.0 copy-start
  0.7 0.7 %copy-done.1 = s32[16,128]{1,0:T(8,128)S(1)} copy-done((s32[16,128]{1,0:T(8,128)S(1)}, s32[16,128]{1,0:T(8,128)}, u32[]{:S(2)}) %copy-start.1) | copy-done | bytes 8216
  1.3 0.0 copy-done
  1.4 1.0 %fusion = (f32[16,16,128]{2,1,0:T(8,128)S(1)}, f32[16,16,128]{2,1,0:T(8,128)S(1)}) fusion(f32[16,16,128]{2,1,0:T(8,128)} %param.5, s32[16,128]{1,0:T(8,128)S(1)} %compare_select_fusion, f32[16,16,128]{2,1,0:T(8,128)} %param.4), kind=kLoop, calls=%fused_computation.1 | loop fusion | flops 98304 | bytes 532480 | tf_op jit(solution)/shard_map/jit(_where)/select_n | solution.py:546
  2.3 0.4 %prep.1 = (f32[16,2,2,8,128]{4,3,2,1,0:T(8,128)S(1)}, f32[2,2,2,8,128]{4,3,2,1,0:T(8,128)S(1)}, f32[12,2,2,8,128]{4,3,2,1,0:T(8,128)S(1)}, f32[2,2,8,128]{3,2,1,0:T(8,128)S(1)}) custom-call(s32[1]{0:T(128)} %bitcast.place_ref, f32[256,128]{1,0:T(8,128)S(1)} %bitcast.10, f32[256,128]{1,0:T(8,128)S(1)} %bitcast.9), custom_call_target="tpu_custom_call" | custom-call | tf_op jit(solution)/shard_map/prep/pallas_call | solution.py:95
  2.8 0.5 %collective-permute-start = (f32[2,2,2,8,128]{4,3,2,1,0:T(8,128)S(1)}, f32[2,2,2,8,128]{4,3,2,1,0:T(8,128)S(1)}, u32[]{:S(2)}, u32[]{:S(2)}) collective-permute-start(f32[2,2,2,8,128]{4,3,2,1,0:T(8,128)S(1)} %get-tuple-element.19), channel_id=1, source_target_pairs={{0,1},{1,0},{2,3},{3,2},{4,5},{5,4},{6,7},{7,6},{8,9},{9,8},{10,11... | collective-permute-start | bytes 98312 | tf_op jit(solution)/shard_map/ppermute | solution.py:550
  3.2 2.6 %collective-permute-start.1 = (f32[2,2,8,128]{3,2,1,0:T(8,128)S(1)}, f32[2,2,8,128]{3,2,1,0:T(8,128)S(1)}, u32[]{:S(2)}, u32[]{:S(2)}) collective-permute-start(f32[2,2,8,128]{3,2,1,0:T(8,128)S(1)} %get-tuple-element.20), channel_id=1, source_target_pairs={{0,3},{1,2},{2,1},{3,0},{4,7},{5,6},{6,5},{7,4},{8,11},{9,10},{10,... | collective-permute-start | bytes 49160 | tf_op jit(solution)/shard_map/ppermute | solution.py:548
  5.9 0.0 collective-permute-start.4
  5.9 1.4 %collective-permute-done.1.near_corner_ref.corner_ref = f32[2,2,8,128]{3,2,1,0:T(8,128)S(1)} collective-permute-done((f32[2,2,8,128]{3,2,1,0:T(8,128)S(1)}, f32[2,2,8,128]{3,2,1,0:T(8,128)S(1)}, u32[]{:S(2)}, u32[]{:S(2)}) %collective-permute-start.1) | collective-permute-done | bytes 16416 | tf_op jit(solution)/shard_map/ppermute | solution.py:548
  7.3 0.0 collective-permute-done.strip_ref
  7.3 0.1 pack.1
  7.4 4.7 %collective-permute-start.2 = (f32[12,2,2,8,128]{4,3,2,1,0:T(8,128)S(1)}, f32[12,2,2,8,128]{4,3,2,1,0:T(8,128)S(1)}, u32[]{:S(2)}, u32[]{:S(2)}) collective-permute-start(f32[12,2,2,8,128]{4,3,2,1,0:T(8,128)S(1)} %get-tuple-element.21), channel_id=1, source_target_pairs={{0,14},{1,15},{2,4},{3,5},{4,2},{5,3},{6,8},{7,9},{8,6},{9,7},{10,... | collective-permute-start | bytes 589832 | tf_op jit(solution)/shard_map/ppermute | solution.py:552
  12.1 0.1 collective-permute-start.3
  12.2 0.5 %collective-permute-done.4.near_ref = f32[12,2,2,8,128]{4,3,2,1,0:T(8,128)S(1)} collective-permute-done((f32[12,2,2,8,128]{4,3,2,1,0:T(8,128)S(1)}, f32[12,2,2,8,128]{4,3,2,1,0:T(8,128)S(1)}, u32[]{:S(2)}, u32[]{:S(2)}) %collective-permute-start.4) | collective-permute-done | bytes 196640 | tf_op jit(solution)/shard_map/ppermute | solution.py:549
  12.7 2.2 %near_side.1 = (f32[12,2,4,8,128]{4,3,2,1,0:T(8,128)S(1)}, f32[3,4,4,8,128]{4,3,2,1,0:T(8,128)S(1)}, f32[3,16,4,8,128]{4,3,2,1,0:T(8,128)S(1)}, f32[3,16,4,8,128]{4,3,2,1,0:T(8,128)S(1)}, f32[6,8,128]{2,1,0:T(8,128)S(1)}) custom-call(s32[1]{0:T(128)} %bitcast.place_ref, f32[16,2,2,8,128]{4,3,2,1,0:T(8,128)S(1)} %get-tuple-element.18.own_ref, ...), custom_call_target="tpu_custom_call" | custom-call | flops 20000000 | bytes 4194304 | tf_op jit(solution)/shard_map/near_side/pallas_call | solution.py:347
  14.9 3.6 %collective-permute-done.3.corner_ref = f32[2,2,8,128]{3,2,1,0:T(8,128)S(1)} collective-permute-done((f32[2,2,8,128]{3,2,1,0:T(8,128)S(1)}, f32[2,2,8,128]{3,2,1,0:T(8,128)S(1)}, u32[]{:S(2)}, u32[]{:S(2)}) %collective-permute-start.3) | collective-permute-done | bytes 16416 | tf_op jit(solution)/shard_map/ppermute | solution.py:553
  18.5 0.0 collective-permute-done.2.far_ref
  18.5 1.9 %far_side.1 = (f32[3,16,4,8,128]{4,3,2,1,0:T(8,128)S(1)}, f32[3,16,4,8,128]{4,3,2,1,0:T(8,128)S(1)}, f32[16,128]{1,0:T(8,128)S(1)}) custom-call(s32[1]{0:T(128)} %bitcast.place_ref, f32[16,2,2,8,128]{4,3,2,1,0:T(8,128)S(1)} %get-tuple-element.18.own_ref, f32[12,2,2,8,128]{4,3,2,1,0:T(8,128)S(1)} %collective-permute-done.2.far_ref, ...), custom_call_target="tpu_custom_call" | custom-call | flops 15000000 | bytes 4194304 | tf_op jit(solution)/shard_map/far_side/pallas_call | solution.py:421
  20.4 12.1 %all_to_all.11 = f32[16,1,128]{2,1,0:T(1,128)S(1)} all-to-all(f32[16,1,128]{2,1,0:T(1,128)S(1)} %bitcast.12), channel_id=1, replica_groups=mesh['member'=2,'lon'=8,'lat'=2] {'lon','lat'}, dimensions={0} | all-to-all | bytes 16384 | tf_op jit(solution)/shard_map/all_to_all | solution.py:556
  32.5 1.1 %combine.1 = (f32[256,128]{1,0:T(8,128)}, f32[256,128]{1,0:T(8,128)}) custom-call(s32[1]{0:T(128)} %bitcast.place_ref, f32[16,128]{1,0:T(8,128)S(1)} %bitcast.11, f32[16,2,2,8,128]{4,3,2,1,0:T(8,128)S(1)} %get-tuple-element.18.own_ref, f32[3,16,4,8,128]{4,3,2,1,0:T(8,128)S(1)} %get-tuple-element.28.u_near_ref, ...), custom_call_target="tpu_custom_call" | custom-call | tf_op jit(solution)/shard_map/combine/pallas_call | solution.py:518
  (1 shorter events, 0.0 us)
Async XLA Ops:
  0.6 0.7 %copy-start.1 = (s32[16,128]{1,0:T(8,128)S(1)}, s32[16,128]{1,0:T(8,128)}, u32[]{:S(2)}) copy-start(s32[16,128]{1,0:T(8,128)} %param.6) | copy-start | bytes 24580
  0.6 0.7 %copy-start = (s32[16,128]{1,0:T(8,128)S(1)}, s32[16,128]{1,0:T(8,128)}, u32[]{:S(2)}) copy-start(s32[16,128]{1,0:T(8,128)} %param.7) | copy-start | bytes 24580
  2.8 4.5 %collective-permute-start = (f32[2,2,2,8,128]{4,3,2,1,0:T(8,128)S(1)}, f32[2,2,2,8,128]{4,3,2,1,0:T(8,128)S(1)}, u32[]{:S(2)}, u32[]{:S(2)}) collective-permute-start(f32[2,2,2,8,128]{4,3,2,1,0:T(8,128)S(1)} %get-tuple-element.19), channel_id=1, source_target_pairs={{0,1},{1,0},{2,3},{3,2},{4,5},{5,4},{6,7},{7,6},{8,9},{9,8},{10,11... | collective-permute-start | bytes 98312 | tf_op jit(solution)/shard_map/ppermute | solution.py:550
  3.2 4.1 %collective-permute-start.1 = (f32[2,2,8,128]{3,2,1,0:T(8,128)S(1)}, f32[2,2,8,128]{3,2,1,0:T(8,128)S(1)}, u32[]{:S(2)}, u32[]{:S(2)}) collective-permute-start(f32[2,2,8,128]{3,2,1,0:T(8,128)S(1)} %get-tuple-element.20), channel_id=1, source_target_pairs={{0,3},{1,2},{2,1},{3,0},{4,7},{5,6},{6,5},{7,4},{8,11},{9,10},{10,... | collective-permute-start | bytes 49160 | tf_op jit(solution)/shard_map/ppermute | solution.py:548
  5.9 6.9 %collective-permute-start.4 = (f32[12,2,2,8,128]{4,3,2,1,0:T(8,128)S(1)}, f32[12,2,2,8,128]{4,3,2,1,0:T(8,128)S(1)}, u32[]{:S(2)}, u32[]{:S(2)}) collective-permute-start(f32[12,2,2,8,128]{4,3,2,1,0:T(8,128)S(1)} %get-tuple-element.23), channel_id=1, source_target_pairs={{0,2},{1,3},{2,0},{3,1},{4,6},{5,7},{6,4},{7,5},{8,10},{9,11},{10,... | collective-permute-start | bytes 589832 | tf_op jit(solution)/shard_map/ppermute | solution.py:549
  7.4 11.2 %collective-permute-start.2 = (f32[12,2,2,8,128]{4,3,2,1,0:T(8,128)S(1)}, f32[12,2,2,8,128]{4,3,2,1,0:T(8,128)S(1)}, u32[]{:S(2)}, u32[]{:S(2)}) collective-permute-start(f32[12,2,2,8,128]{4,3,2,1,0:T(8,128)S(1)} %get-tuple-element.21), channel_id=1, source_target_pairs={{0,14},{1,15},{2,4},{3,5},{4,2},{5,3},{6,8},{7,9},{8,6},{9,7},{10,... | collective-permute-start | bytes 589832 | tf_op jit(solution)/shard_map/ppermute | solution.py:552
  12.1 6.4 %collective-permute-start.3 = (f32[2,2,8,128]{3,2,1,0:T(8,128)S(1)}, f32[2,2,8,128]{3,2,1,0:T(8,128)S(1)}, u32[]{:S(2)}, u32[]{:S(2)}) collective-permute-start(f32[2,2,8,128]{3,2,1,0:T(8,128)S(1)} %get-tuple-element.22), channel_id=1, source_target_pairs={{0,14},{1,15},{2,4},{3,5},{4,2},{5,3},{6,8},{7,9},{8,6},{9,7},{10,... | collective-permute-start | bytes 49160 | tf_op jit(solution)/shard_map/ppermute | solution.py:553

commit v4 on v3

--- a/solution.py
+++ b/solution.py
@@ -60,20 +60,24 @@
     return (in_slot >= start) & (in_slot < start + SPARE), back
 
 
-def prep_kernel(place_ref, right_ref, scale_ref, own_ref, strip_ref, near_ref, corner_ref):
+def prep_kernel(place_ref, both_ref, land_ref, bottom_ref, own_ref, strip_ref, near_ref, corner_ref):
     rows = own_ref.shape[0]
     core, flip = place_ref[0] % 2, place_ref[0] // 2
-    _, lane = iotas()
+    sub, lane = iotas()
     half_lane = lane % WIDE
     apart = 2 * half_lane + lane // WIDE
     packed = {}
     for r in range(rows):
         group, seg = divmod(r, SEGS)
         shift = lax.rem(EDGE * seg + (1 - core) * (WIDE + EDGE), LANES)
+        i = column(rows, r, flip)
+        deep = jnp.where(land_ref[pl.ds(i, 1), :] == 1, bottom_ref[pl.ds(i, 1), :], 0)
+        deep = jnp.broadcast_to(deep, (SUB, LANES))
         for par in range(2):
-            at = pl.ds(par * rows + column(rows, r, flip), SUB, stride=2 * rows)
-            for f, ref in enumerate((scale_ref, right_ref)):
-                x = take_lanes(ref[at, :], apart)
+            wet = 2 * sub + par < deep
+            for f in range(2):
+                at = pl.ds((2 * SUB * f + par) * rows + i, SUB, stride=2 * rows)
+                x = take_lanes(jnp.where(wet, both_ref[at, :], 0.0), apart)
                 own_ref[r, f, par] = x
                 if r < DEPTH:
                     near_ref[r, f, par] = x
@@ -90,16 +94,17 @@
             corner_ref[f, par] = jnp.where(spare, pltpu.roll(second, back, 1), first)
 
 
-def prep(place, right, scale, rows):
+def prep(place, fields, land, bottom):
+    rows = land.shape[0]
     vmem = pl.BlockSpec(memory_space=pltpu.VMEM)
     return pl.pallas_call(
         prep_kernel,
         out_shape=(tiles_of(rows, 2, 2), tiles_of(rows // SEGS, 2, 2), tiles_of(DEPTH, 2, 2), tiles_of(2, 2)),
-        in_specs=[pl.BlockSpec(memory_space=pltpu.SMEM)] + [vmem] * 2,
+        in_specs=[pl.BlockSpec(memory_space=pltpu.SMEM)] + [vmem] * 3,
         out_specs=(vmem,) * 4,
         compiler_params=pltpu.CompilerParams(vmem_limit_bytes=8 * MIB),
         name="prep",
-    )(place, right, scale)
+    )(place, fields, land, bottom)
 
 
 def pack_kernel(place_ref, own_ref, strip_ref, near_corner_ref, far_corner_ref, far_ref):
@@ -541,10 +546,8 @@
     beyond = lambda i: i + 1 if i % 2 else i - 1
     place = lax.axis_index("lat") + 2 * (1 - lax.axis_index("lon") % 2)
     place = place.astype(jnp.int32).reshape(1)
-    depth = lax.broadcasted_iota(jnp.int32, right_side.shape, 0)
-    wet = depth < jnp.where(land_mask == 1, bottom, 0)[None]
-    right, weight = (jnp.where(wet, x, 0.0).reshape(levels * rows, lats) for x in (right_side, scale))
-    own, strip, near, corner = prep(place, right, weight, rows)
+    fields = jnp.stack([scale, right_side]).reshape(2 * levels * rows, lats)
+    own, strip, near, corner = prep(place, fields, land_mask, bottom)
     corner = lax.ppermute(corner, both, links(lambda i, j: (i ^ 1, 1 - j)))
     near = lax.ppermute(near, both, links(lambda i, j: (i ^ 1, j)))
     strip = lax.ppermute(strip, both, links(lambda i, j: (i, 1 - j)))

time: 34 us -> 33.2 us (0.976)
  local copies, waits for them, and re-layouts: 0.69 us -> 0.01 us
    another operation x0 -> x1, other arithmetic: none -> 1 us  [local(): fields = jnp.stack([scale, right_side]).reshape(2 * levels * rows, lats)]
    select_n x2 -> x0, other arithmetic: 0.99 us -> none  [the longest x1 0.99 us: local(): jnp.where(wet, x, 0.0).reshape(levels * rows, lats)]
    unnamed x4, local copies, waits for them, and re-layouts: 0.69 us -> 0.01 us
where the time goes in v4:
time: 33.2 us; the launch traced here: 33 us
  blocking collectives  12.1 us (36%)
  starting transfers between devices  7.92 us (24%)
  Pallas kernels  5.68 us (17%)
  waiting for transfers between devices  5.6 us (17%)
  other arithmetic  1 us (3%)
  between operations  0.69 us (2%)
    all_to_all x1, blocking collectives, local(): sums = lax.all_to_all(parts, both, 0, 0, tiled=True)  12.1 us
    ppermute x1, starting transfers between devices, local(): far = lax.ppermute(far, both, links(lambda i, j: (beyond(i), j)))  4.72 us
    ppermute x1, waiting for transfers between devices, local(): lax.ppermute(far_corner, both, links(lambda i, j: (beyond(i), j)))  3.65 us
    ppermute x1, starting transfers between devices, local(): corner = lax.ppermute(corner, both, links(lambda i, j: (i ^ 1, 1 - j)))  2.62 us
    pallas_call x1, Pallas kernels, near_side(): pl.pallas_call(near_kernel, out_shape=outs, in_specs=[pl.BlockSpec(memory...  2.15 us
    pallas_call x1, Pallas kernels, far_side(): pl.pallas_call(far_kernel, out_shape=outs, in_specs=[pl.BlockSpec(memory_...  1.87 us
    ppermute x1, waiting for transfers between devices, local(): corner = lax.ppermute(corner, both, links(lambda i, j: (i ^ 1, 1 - j)))  1.4 us
    pallas_call x1, Pallas kernels, last(): pl.pallas_call(last_kernel, out_shape=(out, out), in_specs=[pl.BlockSpec(...  1.13 us
  transfers between devices with their start and end apart: 5, of which 3 were waited for; matrix products, arithmetic and copies ran while one was open for 0% of the time, Pallas kernels for 7%

profile of v4, /device:TPU:0, one launch (start us, length us, event | category | flops | bytes accessed | tf_op | source)
XLA Modules:
  0.0 33.0 jit_solution(9682554137058736144)
XLA Ops:
  0.6 0.0 copy-start
  0.7 0.0 copy-start.1
  0.7 1.0 %pad_maximum_fusion = f32[2,16,16,128]{3,2,1,0:T(8,128)S(1)} fusion(f32[1,16,16,128]{3,2,1,0:T(8,128)} %bitcast.13, f32[1,16,16,128]{3,2,1,0:T(8,128)} %bitcast.14), kind=kLoop, calls=%fused_computation | loop fusion | flops 65536 | bytes 524288 | tf_op jit(solution)/shard_map/stack | solution.py:549
  1.7 0.0 copy-done
  1.7 0.0 copy-done.1
  1.7 0.5 %prep.1 = (f32[16,2,2,8,128]{4,3,2,1,0:T(8,128)S(1)}, f32[2,2,2,8,128]{4,3,2,1,0:T(8,128)S(1)}, f32[12,2,2,8,128]{4,3,2,1,0:T(8,128)S(1)}, f32[2,2,8,128]{3,2,1,0:T(8,128)S(1)}) custom-call(s32[1]{0:T(128)} %bitcast.place_ref, f32[512,128]{1,0:T(8,128)S(1)} %bitcast.10, s32[16,128]{1,0:T(8,128)S(1)} %copy-done, s32[16,128]{1,0:T(8,128)S(1)} %copy-done.1), custom_call_target="tpu_custom_call" | custom-call | tf_op jit(solution)/shard_map/prep/pallas_call | solution.py:100
  2.1 0.5 %collective-permute-start = (f32[2,2,2,8,128]{4,3,2,1,0:T(8,128)S(1)}, f32[2,2,2,8,128]{4,3,2,1,0:T(8,128)S(1)}, u32[]{:S(2)}, u32[]{:S(2)}) collective-permute-start(f32[2,2,2,8,128]{4,3,2,1,0:T(8,128)S(1)} %get-tuple-element.19), channel_id=1, source_target_pairs={{0,1},{1,0},{2,3},{3,2},{4,5},{5,4},{6,7},{7,6},{8,9},{9,8},{10,11... | collective-permute-start | bytes 98312 | tf_op jit(solution)/shard_map/ppermute | solution.py:553
  2.6 2.6 %collective-permute-start.1 = (f32[2,2,8,128]{3,2,1,0:T(8,128)S(1)}, f32[2,2,8,128]{3,2,1,0:T(8,128)S(1)}, u32[]{:S(2)}, u32[]{:S(2)}) collective-permute-start(f32[2,2,8,128]{3,2,1,0:T(8,128)S(1)} %get-tuple-element.20), channel_id=1, source_target_pairs={{0,3},{1,2},{2,1},{3,0},{4,7},{5,6},{6,5},{7,4},{8,11},{9,10},{10,... | collective-permute-start | bytes 49160 | tf_op jit(solution)/shard_map/ppermute | solution.py:551
  5.2 0.0 collective-permute-start.4
  5.3 1.4 %collective-permute-done.1.near_corner_ref.corner_ref = f32[2,2,8,128]{3,2,1,0:T(8,128)S(1)} collective-permute-done((f32[2,2,8,128]{3,2,1,0:T(8,128)S(1)}, f32[2,2,8,128]{3,2,1,0:T(8,128)S(1)}, u32[]{:S(2)}, u32[]{:S(2)}) %collective-permute-start.1) | collective-permute-done | bytes 16416 | tf_op jit(solution)/shard_map/ppermute | solution.py:551
  6.7 0.0 collective-permute-done.strip_ref
  6.7 0.1 pack.1
  6.7 4.7 %collective-permute-start.2 = (f32[12,2,2,8,128]{4,3,2,1,0:T(8,128)S(1)}, f32[12,2,2,8,128]{4,3,2,1,0:T(8,128)S(1)}, u32[]{:S(2)}, u32[]{:S(2)}) collective-permute-start(f32[12,2,2,8,128]{4,3,2,1,0:T(8,128)S(1)} %get-tuple-element.21), channel_id=1, source_target_pairs={{0,14},{1,15},{2,4},{3,5},{4,2},{5,3},{6,8},{7,9},{8,6},{9,7},{10,... | collective-permute-start | bytes 589832 | tf_op jit(solution)/shard_map/ppermute | solution.py:555
  11.5 0.1 collective-permute-start.3
  11.5 0.5 %collective-permute-done.4.near_ref = f32[12,2,2,8,128]{4,3,2,1,0:T(8,128)S(1)} collective-permute-done((f32[12,2,2,8,128]{4,3,2,1,0:T(8,128)S(1)}, f32[12,2,2,8,128]{4,3,2,1,0:T(8,128)S(1)}, u32[]{:S(2)}, u32[]{:S(2)}) %collective-permute-start.4) | collective-permute-done | bytes 196640 | tf_op jit(solution)/shard_map/ppermute | solution.py:552
  12.1 2.2 %near_side.1 = (f32[12,2,4,8,128]{4,3,2,1,0:T(8,128)S(1)}, f32[3,4,4,8,128]{4,3,2,1,0:T(8,128)S(1)}, f32[3,16,4,8,128]{4,3,2,1,0:T(8,128)S(1)}, f32[3,16,4,8,128]{4,3,2,1,0:T(8,128)S(1)}, f32[6,8,128]{2,1,0:T(8,128)S(1)}) custom-call(s32[1]{0:T(128)} %bitcast.place_ref, f32[16,2,2,8,128]{4,3,2,1,0:T(8,128)S(1)} %get-tuple-element.18.own_ref, ...), custom_call_target="tpu_custom_call" | custom-call | flops 20000000 | bytes 4194304 | tf_op jit(solution)/shard_map/near_side/pallas_call | solution.py:352
  14.3 3.6 %collective-permute-done.3.corner_ref = f32[2,2,8,128]{3,2,1,0:T(8,128)S(1)} collective-permute-done((f32[2,2,8,128]{3,2,1,0:T(8,128)S(1)}, f32[2,2,8,128]{3,2,1,0:T(8,128)S(1)}, u32[]{:S(2)}, u32[]{:S(2)}) %collective-permute-start.3) | collective-permute-done | bytes 16416 | tf_op jit(solution)/shard_map/ppermute | solution.py:556
  17.9 0.0 collective-permute-done.2.far_ref
  17.9 1.9 %far_side.1 = (f32[3,16,4,8,128]{4,3,2,1,0:T(8,128)S(1)}, f32[3,16,4,8,128]{4,3,2,1,0:T(8,128)S(1)}, f32[16,128]{1,0:T(8,128)S(1)}) custom-call(s32[1]{0:T(128)} %bitcast.place_ref, f32[16,2,2,8,128]{4,3,2,1,0:T(8,128)S(1)} %get-tuple-element.18.own_ref, f32[12,2,2,8,128]{4,3,2,1,0:T(8,128)S(1)} %collective-permute-done.2.far_ref, ...), custom_call_target="tpu_custom_call" | custom-call | flops 15000000 | bytes 4194304 | tf_op jit(solution)/shard_map/far_side/pallas_call | solution.py:426
  19.8 12.1 %all_to_all.11 = f32[16,1,128]{2,1,0:T(1,128)S(1)} all-to-all(f32[16,1,128]{2,1,0:T(1,128)S(1)} %bitcast.12), channel_id=1, replica_groups=mesh['member'=2,'lon'=8,'lat'=2] {'lon','lat'}, dimensions={0} | all-to-all | bytes 16384 | tf_op jit(solution)/shard_map/all_to_all | solution.py:559
  31.9 1.1 %combine.1 = (f32[256,128]{1,0:T(8,128)}, f32[256,128]{1,0:T(8,128)}) custom-call(s32[1]{0:T(128)} %bitcast.place_ref, f32[16,128]{1,0:T(8,128)S(1)} %bitcast.11, f32[16,2,2,8,128]{4,3,2,1,0:T(8,128)S(1)} %get-tuple-element.18.own_ref, f32[3,16,4,8,128]{4,3,2,1,0:T(8,128)S(1)} %get-tuple-element.28.u_near_ref, ...), custom_call_target="tpu_custom_call" | custom-call | tf_op jit(solution)/shard_map/combine/pallas_call | solution.py:523
Async XLA Ops:
  0.6 1.0 %copy-start = (s32[16,128]{1,0:T(8,128)S(1)}, s32[16,128]{1,0:T(8,128)}, u32[]{:S(2)}) copy-start(s32[16,128]{1,0:T(8,128)} %land_ref.1) | copy-start | bytes 24580
  0.7 1.0 %copy-start.1 = (s32[16,128]{1,0:T(8,128)S(1)}, s32[16,128]{1,0:T(8,128)}, u32[]{:S(2)}) copy-start(s32[16,128]{1,0:T(8,128)} %bottom_ref.1) | copy-start | bytes 24580
  2.1 4.5 %collective-permute-start = (f32[2,2,2,8,128]{4,3,2,1,0:T(8,128)S(1)}, f32[2,2,2,8,128]{4,3,2,1,0:T(8,128)S(1)}, u32[]{:S(2)}, u32[]{:S(2)}) collective-permute-start(f32[2,2,2,8,128]{4,3,2,1,0:T(8,128)S(1)} %get-tuple-element.19), channel_id=1, source_target_pairs={{0,1},{1,0},{2,3},{3,2},{4,5},{5,4},{6,7},{7,6},{8,9},{9,8},{10,11... | collective-permute-start | bytes 98312 | tf_op jit(solution)/shard_map/ppermute | solution.py:553
  2.6 4.1 %collective-permute-start.1 = (f32[2,2,8,128]{3,2,1,0:T(8,128)S(1)}, f32[2,2,8,128]{3,2,1,0:T(8,128)S(1)}, u32[]{:S(2)}, u32[]{:S(2)}) collective-permute-start(f32[2,2,8,128]{3,2,1,0:T(8,128)S(1)} %get-tuple-element.20), channel_id=1, source_target_pairs={{0,3},{1,2},{2,1},{3,0},{4,7},{5,6},{6,5},{7,4},{8,11},{9,10},{10,... | collective-permute-start | bytes 49160 | tf_op jit(solution)/shard_map/ppermute | solution.py:551
  5.2 6.9 %collective-permute-start.4 = (f32[12,2,2,8,128]{4,3,2,1,0:T(8,128)S(1)}, f32[12,2,2,8,128]{4,3,2,1,0:T(8,128)S(1)}, u32[]{:S(2)}, u32[]{:S(2)}) collective-permute-start(f32[12,2,2,8,128]{4,3,2,1,0:T(8,128)S(1)} %get-tuple-element.23), channel_id=1, source_target_pairs={{0,2},{1,3},{2,0},{3,1},{4,6},{5,7},{6,4},{7,5},{8,10},{9,11},{10,... | collective-permute-start | bytes 589832 | tf_op jit(solution)/shard_map/ppermute | solution.py:552
  6.7 11.2 %collective-permute-start.2 = (f32[12,2,2,8,128]{4,3,2,1,0:T(8,128)S(1)}, f32[12,2,2,8,128]{4,3,2,1,0:T(8,128)S(1)}, u32[]{:S(2)}, u32[]{:S(2)}) collective-permute-start(f32[12,2,2,8,128]{4,3,2,1,0:T(8,128)S(1)} %get-tuple-element.21), channel_id=1, source_target_pairs={{0,14},{1,15},{2,4},{3,5},{4,2},{5,3},{6,8},{7,9},{8,6},{9,7},{10,... | collective-permute-start | bytes 589832 | tf_op jit(solution)/shard_map/ppermute | solution.py:555
  11.5 6.4 %collective-permute-start.3 = (f32[2,2,8,128]{3,2,1,0:T(8,128)S(1)}, f32[2,2,8,128]{3,2,1,0:T(8,128)S(1)}, u32[]{:S(2)}, u32[]{:S(2)}) collective-permute-start(f32[2,2,8,128]{3,2,1,0:T(8,128)S(1)} %get-tuple-element.22), channel_id=1, source_target_pairs={{0,14},{1,15},{2,4},{3,5},{4,2},{5,3},{6,8},{7,9},{8,6},{9,7},{10,... | collective-permute-start | bytes 49160 | tf_op jit(solution)/shard_map/ppermute | solution.py:556

commit v5 on v4

--- a/solution.py
+++ b/solution.py
@@ -107,7 +107,7 @@
     )(place, fields, land, bottom)
 
 
-def pack_kernel(place_ref, own_ref, strip_ref, near_corner_ref, far_corner_ref, far_ref):
+def pack_kernel(place_ref, own_ref, strip_ref, near_corner_ref, far_corner_ref, far_ref, tile_ref):
     rows = own_ref.shape[0]
     spare, back = spare_lanes(place_ref[0] % 2)
     for f in range(2):
@@ -116,15 +116,19 @@
                 far_ref[dist - 1, f, par] = own_ref[rows - dist, f, par]
             first, second = strip_ref[0, f, par], strip_ref[1, f, par]
             far_corner_ref[f, par] = jnp.where(spare, pltpu.roll(first, back, 1), second)
+    lanes = Lanes(place_ref[0] % 2)
+    for f in range(2):
+        for r in range(rows):
+            spread(tile_ref, (f, r), lanes.own(own_ref, strip_ref, r, f))
 
 
 def pack(place, own, strip, corner):
     vmem = pl.BlockSpec(memory_space=pltpu.VMEM)
     return pl.pallas_call(
         pack_kernel,
-        out_shape=(tiles_of(2, 2), tiles_of(DEPTH, 2, 2)),
+        out_shape=(tiles_of(2, 2), tiles_of(DEPTH, 2, 2), tiles_of(2, own.shape[0], 4)),
         in_specs=[pl.BlockSpec(memory_space=pltpu.SMEM)] + [vmem] * 3,
-        out_specs=(vmem,) * 2,
+        out_specs=(vmem,) * 3,
         compiler_params=pltpu.CompilerParams(vmem_limit_bytes=8 * MIB),
         cost_estimate=pl.CostEstimate(flops=20000000, bytes_accessed=16 * MIB, transcendentals=0),
         name="pack",
@@ -236,13 +240,15 @@
             fa = coef("ca", r, s) * (odd - even)
             acc[2 * s] = acc[2 * s] + (coef("cb", r, 2 * s) * down(odd) + fa)
             acc[2 * s + 1] = acc[2 * s + 1] + (coef("cb", r, 2 * s + 1) * up(even) - fa)
-        v = read(turn * EVERY, r) if stage else None
+        v = read(turn * EVERY + (stage < CHEB), r) if stage >= CHEB - 1 else None
         out = []
         for t in range(4):
             if stage == 0:
                 y = acc[t] + coef("d1", r, t) * now[t]
             elif stage < CHEB:
-                y = acc[t] + coef("d0", r, t) * now[t] + (NU if stage == 1 else MU * NU) * v[t]
+                y = acc[t] + coef("d0", r, t) * now[t]
+                if stage == CHEB - 1:
+                    y = y + NU * v[t]
             else:
                 y = v[t] - STEP * (coef("hw", r, t) * now[t] - acc[t])
             out.append(y)
@@ -275,8 +281,8 @@
     return rows - (k * EVERY + CHEB), rows - (k + 1) * EVERY
 
 
-def near_kernel(place_ref, own_ref, near_ref, corner_ref, strip_ref, *refs):
-    rows = own_ref.shape[0]
+def near_kernel(place_ref, tile_ref, near_ref, corner_ref, *refs):
+    rows = tile_ref.shape[1]
     edge_ref, kept_ref, u_ref, r_ref, part_ref = refs[:5]
     coef_refs = dict(zip(NAMES, refs[5:13]))
     w_ref, v_ref, p_ref, q_ref = refs[13:]
@@ -309,7 +315,7 @@
             if r < 0:
                 tiles = lanes.beyond(near_ref, lambda f, par: corner_ref[f, par], -r, f, True)
             else:
-                tiles = lanes.own(own_ref, strip_ref, r, f)
+                tiles = [tile_ref[f, r, t] for t in range(4)]
             spread(ref, (r + DEPTH,), tiles)
     fill_coefs(coef_refs, w_ref)
     keep(0)
@@ -343,8 +349,8 @@
     return [pltpu.VMEM((total, TILES[name], SUB, LANES), jnp.float32) for name in NAMES]
 
 
-def near_side(place, own, near, corner, strip):
-    rows = own.shape[0]
+def near_side(place, tiles, near, corner):
+    rows = tiles.shape[1]
     vmem = pl.BlockSpec(memory_space=pltpu.VMEM)
     outs = [tiles_of(DEPTH, 2, 4), tiles_of(ITERS, EVERY, 4)]
     outs += [tiles_of(ITERS, rows, 4)] * 2 + [tiles_of(2 * ITERS)]
@@ -352,20 +358,20 @@
     return pl.pallas_call(
         near_kernel,
         out_shape=outs,
-        in_specs=[pl.BlockSpec(memory_space=pltpu.SMEM)] + [vmem] * 4,
+        in_specs=[pl.BlockSpec(memory_space=pltpu.SMEM)] + [vmem] * 3,
         out_specs=[vmem] * len(outs),
         scratch_shapes=coef_scratch(rows + DEPTH) + full,
         compiler_params=pltpu.CompilerParams(vmem_limit_bytes=16 * MIB),
         cost_estimate=pl.CostEstimate(flops=20000000, bytes_accessed=4 * MIB, transcendentals=0),
         name="near_side",
-    )(place, own, near, corner, strip)
-
-
-def far_kernel(place_ref, own_ref, far_ref, corner_ref, strip_ref, edge_ref, kept_ref, part_in_ref, *refs):
+    )(place, tiles, near, corner)
+
+
+def far_kernel(place_ref, tile_ref, far_ref, corner_ref, edge_ref, kept_ref, part_in_ref, *refs):
     u_ref, r_ref, part_ref = refs[:3]
     coef_refs = dict(zip(NAMES, refs[3:11]))
     w_ref, v_ref, p_ref, q_ref = refs[11:]
-    rows = own_ref.shape[0]
+    rows = tile_ref.shape[1]
     base = rows - DEPTH - 1
     lanes = Lanes(place_ref[0] % 2)
     sub, lane = iotas()
@@ -388,7 +394,7 @@
 
     for r in range(base, rows + DEPTH):
         if r < rows:
-            w = lanes.own(own_ref, strip_ref, r, 0)
+            w = [tile_ref[0, r, t] for t in range(4)]
         else:
             w, v = (
                 lanes.beyond(far_ref, lambda f, par: corner_ref[f, par], r - rows + 1, f, False) for f in range(2)
@@ -417,8 +423,8 @@
         part_ref[n : n + SUB, :] = row
 
 
-def far_side(place, own, far, corner, strip, edge, kept, part, peers):
-    rows = own.shape[0]
+def far_side(place, tiles, far, corner, edge, kept, part, peers):
+    rows = tiles.shape[1]
     vmem = pl.BlockSpec(memory_space=pltpu.VMEM)
     outs = [tiles_of(ITERS, rows, 4)] * 2 + [jax.ShapeDtypeStruct((peers, LANES), jnp.float32)]
     full = [pltpu.VMEM((2 * DEPTH + 1, 4, SUB, LANES), jnp.float32)]
@@ -426,13 +432,13 @@
     return pl.pallas_call(
         far_kernel,
         out_shape=outs,
-        in_specs=[pl.BlockSpec(memory_space=pltpu.SMEM)] + [vmem] * 7,
+        in_specs=[pl.BlockSpec(memory_space=pltpu.SMEM)] + [vmem] * 6,
         out_specs=[vmem] * 3,
         scratch_shapes=coef_scratch(2 * DEPTH + 1) + full,
         compiler_params=pltpu.CompilerParams(vmem_limit_bytes=16 * MIB),
         cost_estimate=pl.CostEstimate(flops=15000000, bytes_accessed=4 * MIB, transcendentals=0),
         name="far_side",
-    )(place, own, far, corner, strip, edge, kept, part)
+    )(place, tiles, far, corner, edge, kept, part)
 
 
 def times_t(poly):
@@ -551,11 +557,11 @@
     corner = lax.ppermute(corner, both, links(lambda i, j: (i ^ 1, 1 - j)))
     near = lax.ppermute(near, both, links(lambda i, j: (i ^ 1, j)))
     strip = lax.ppermute(strip, both, links(lambda i, j: (i, 1 - j)))
-    far_corner, far = pack(place, own, strip, corner)
+    far_corner, far, tiles = pack(place, own, strip, corner)
     far = lax.ppermute(far, both, links(lambda i, j: (beyond(i), j)))
     far_corner = lax.ppermute(far_corner, both, links(lambda i, j: (beyond(i), j)))
-    edge, kept, u_near, r_near, part = near_side(place, own, near, corner, strip)
-    u_far, r_far, parts = far_side(place, own, far, far_corner, strip, edge, kept, part, peers)
+    edge, kept, u_near, r_near, part = near_side(place, tiles, near, corner)
+    u_far, r_far, parts = far_side(place, tiles, far, far_corner, edge, kept, part, peers)
     sums = lax.all_to_all(parts, both, 0, 0, tiled=True)
     sol, res = last(place, sums, own, u_near, r_near, u_far, r_far)
     return sol.reshape(right_side.shape), res.reshape(right_side.shape)

time: 33.2 us -> 33 us (level)
    all_to_all x1, blocking collectives: 12.1 us -> 11.8 us  [local(): sums = lax.all_to_all(parts, both, 0, 0, tiled=True)]
    ppermute x1, waiting for transfers between devices: 3.65 us -> 3.99 us  [local(): lax.ppermute(far_corner, both, links(lambda i, j: (beyond(i), j)))]
where the time goes in v5:
time: 33 us; the launch traced here: 32.9 us
  blocking collectives  11.8 us (36%)
  starting transfers between devices  7.97 us (24%)
  Pallas kernels  5.74 us (17%)
  waiting for transfers between devices  5.67 us (17%)
  other arithmetic  1 us (3%)
  between operations  0.69 us (2%)
    all_to_all x1, blocking collectives, local(): sums = lax.all_to_all(parts, both, 0, 0, tiled=True)  11.8 us
    ppermute x1, starting transfers between devices, local(): far = lax.ppermute(far, both, links(lambda i, j: (beyond(i), j)))  4.77 us
    ppermute x1, waiting for transfers between devices, local(): lax.ppermute(far_corner, both, links(lambda i, j: (beyond(i), j)))  3.99 us
    ppermute x1, starting transfers between devices, local(): corner = lax.ppermute(corner, both, links(lambda i, j: (i ^ 1, 1 - j)))  2.62 us
    pallas_call x1, Pallas kernels, near_side(): pl.pallas_call(near_kernel, out_shape=outs, in_specs=[pl.BlockSpec(memory...  2.08 us
    pallas_call x1, Pallas kernels, far_side(): pl.pallas_call(far_kernel, out_shape=outs, in_specs=[pl.BlockSpec(memory_...  1.77 us
    ppermute x1, waiting for transfers between devices, local(): corner = lax.ppermute(corner, both, links(lambda i, j: (i ^ 1, 1 - j)))  1.4 us
    pallas_call x1, Pallas kernels, last(): pl.pallas_call(last_kernel, out_shape=(out, out), in_specs=[pl.BlockSpec(...  1.13 us
  transfers between devices with their start and end apart: 5, of which 3 were waited for; matrix products, arithmetic and copies ran while one was open for 0% of the time, Pallas kernels for 7%

profile of v5, /device:TPU:0, one launch (start us, length us, event | category | flops | bytes accessed | tf_op | source)
XLA Modules:
  0.0 32.9 jit_solution(12522248953193050517)
XLA Ops:
  0.6 0.0 copy-start
  0.7 0.0 copy-start.1
  0.7 1.0 %pad_maximum_fusion = f32[2,16,16,128]{3,2,1,0:T(8,128)S(1)} fusion(f32[1,16,16,128]{3,2,1,0:T(8,128)} %bitcast.13, f32[1,16,16,128]{3,2,1,0:T(8,128)} %bitcast.14), kind=kLoop, calls=%fused_computation | loop fusion | flops 65536 | bytes 524288 | tf_op jit(solution)/shard_map/stack | solution.py:555
  1.7 0.0 copy-done
  1.7 0.0 copy-done.1
  1.7 0.5 %prep.1 = (f32[16,2,2,8,128]{4,3,2,1,0:T(8,128)S(1)}, f32[2,2,2,8,128]{4,3,2,1,0:T(8,128)S(1)}, f32[12,2,2,8,128]{4,3,2,1,0:T(8,128)S(1)}, f32[2,2,8,128]{3,2,1,0:T(8,128)S(1)}) custom-call(s32[1]{0:T(128)} %bitcast.place_ref, f32[512,128]{1,0:T(8,128)S(1)} %bitcast.10, s32[16,128]{1,0:T(8,128)S(1)} %copy-done, s32[16,128]{1,0:T(8,128)S(1)} %copy-done.1), custom_call_target="tpu_custom_call" | custom-call | tf_op jit(solution)/shard_map/prep/pallas_call | solution.py:100
  2.1 0.5 %collective-permute-start = (f32[2,2,2,8,128]{4,3,2,1,0:T(8,128)S(1)}, f32[2,2,2,8,128]{4,3,2,1,0:T(8,128)S(1)}, u32[]{:S(2)}, u32[]{:S(2)}) collective-permute-start(f32[2,2,2,8,128]{4,3,2,1,0:T(8,128)S(1)} %get-tuple-element.20), channel_id=1, source_target_pairs={{0,1},{1,0},{2,3},{3,2},{4,5},{5,4},{6,7},{7,6},{8,9},{9,8},{10,11... | collective-permute-start | bytes 98312 | tf_op jit(solution)/shard_map/ppermute | solution.py:559
  2.6 2.6 %collective-permute-start.1 = (f32[2,2,8,128]{3,2,1,0:T(8,128)S(1)}, f32[2,2,8,128]{3,2,1,0:T(8,128)S(1)}, u32[]{:S(2)}, u32[]{:S(2)}) collective-permute-start(f32[2,2,8,128]{3,2,1,0:T(8,128)S(1)} %get-tuple-element.21), channel_id=1, source_target_pairs={{0,3},{1,2},{2,1},{3,0},{4,7},{5,6},{6,5},{7,4},{8,11},{9,10},{10,... | collective-permute-start | bytes 49160 | tf_op jit(solution)/shard_map/ppermute | solution.py:557
  5.2 0.0 collective-permute-start.4
  5.3 1.4 %collective-permute-done.1.near_corner_ref.corner_ref = f32[2,2,8,128]{3,2,1,0:T(8,128)S(1)} collective-permute-done((f32[2,2,8,128]{3,2,1,0:T(8,128)S(1)}, f32[2,2,8,128]{3,2,1,0:T(8,128)S(1)}, u32[]{:S(2)}, u32[]{:S(2)}) %collective-permute-start.1) | collective-permute-done | bytes 16416 | tf_op jit(solution)/shard_map/ppermute | solution.py:557
  6.7 0.0 collective-permute-done.strip_ref
  6.7 0.3 pack.1
  7.0 4.8 %collective-permute-start.2 = (f32[12,2,2,8,128]{4,3,2,1,0:T(8,128)S(1)}, f32[12,2,2,8,128]{4,3,2,1,0:T(8,128)S(1)}, u32[]{:S(2)}, u32[]{:S(2)}) collective-permute-start(f32[12,2,2,8,128]{4,3,2,1,0:T(8,128)S(1)} %get-tuple-element.23), channel_id=1, source_target_pairs={{0,14},{1,15},{2,4},{3,5},{4,2},{5,3},{6,8},{7,9},{8,6},{9,7},{10,... | collective-permute-start | bytes 589832 | tf_op jit(solution)/shard_map/ppermute | solution.py:561
  11.7 0.1 collective-permute-start.3
  11.8 0.3 collective-permute-done.4.near_ref
  12.1 2.1 %near_side.1 = (f32[12,2,4,8,128]{4,3,2,1,0:T(8,128)S(1)}, f32[3,4,4,8,128]{4,3,2,1,0:T(8,128)S(1)}, f32[3,16,4,8,128]{4,3,2,1,0:T(8,128)S(1)}, f32[3,16,4,8,128]{4,3,2,1,0:T(8,128)S(1)}, f32[6,8,128]{2,1,0:T(8,128)S(1)}) custom-call(s32[1]{0:T(128)} %bitcast.place_ref, f32[2,16,4,8,128]{4,3,2,1,0:T(8,128)S(1)} %get-tuple-element.22.tile_ref, ...), custom_call_target="tpu_custom_call" | custom-call | flops 20000000 | bytes 4194304 | tf_op jit(solution)/shard_map/near_side/pallas_call | solution.py:358
  14.2 4.0 %collective-permute-done.3.corner_ref = f32[2,2,8,128]{3,2,1,0:T(8,128)S(1)} collective-permute-done((f32[2,2,8,128]{3,2,1,0:T(8,128)S(1)}, f32[2,2,8,128]{3,2,1,0:T(8,128)S(1)}, u32[]{:S(2)}, u32[]{:S(2)}) %collective-permute-start.3) | collective-permute-done | bytes 16416 | tf_op jit(solution)/shard_map/ppermute | solution.py:562
  18.2 0.0 collective-permute-done.2.far_ref
  18.2 1.8 %far_side.1 = (f32[3,16,4,8,128]{4,3,2,1,0:T(8,128)S(1)}, f32[3,16,4,8,128]{4,3,2,1,0:T(8,128)S(1)}, f32[16,128]{1,0:T(8,128)S(1)}) custom-call(s32[1]{0:T(128)} %bitcast.place_ref, f32[2,16,4,8,128]{4,3,2,1,0:T(8,128)S(1)} %get-tuple-element.22.tile_ref, f32[12,2,2,8,128]{4,3,2,1,0:T(8,128)S(1)} %collective-permute-done.2.far_ref, ...), custom_call_target="tpu_custom_call" | custom-call | flops 15000000 | bytes 4194304 | tf_op jit(solution)/shard_map/far_side/pallas_call | solution.py:432
  19.9 11.8 %all_to_all.11 = f32[16,1,128]{2,1,0:T(1,128)S(1)} all-to-all(f32[16,1,128]{2,1,0:T(1,128)S(1)} %bitcast.12), channel_id=1, replica_groups=mesh['member'=2,'lon'=8,'lat'=2] {'lon','lat'}, dimensions={0} | all-to-all | bytes 16384 | tf_op jit(solution)/shard_map/all_to_all | solution.py:565
  31.7 1.1 %combine.1 = (f32[256,128]{1,0:T(8,128)}, f32[256,128]{1,0:T(8,128)}) custom-call(s32[1]{0:T(128)} %bitcast.place_ref, f32[16,128]{1,0:T(8,128)S(1)} %bitcast.11, f32[16,2,2,8,128]{4,3,2,1,0:T(8,128)S(1)} %get-tuple-element.19.own_ref, f32[3,16,4,8,128]{4,3,2,1,0:T(8,128)S(1)} %get-tuple-element.30.u_near_ref, ...), custom_call_target="tpu_custom_call" | custom-call | tf_op jit(solution)/shard_map/combine/pallas_call | solution.py:529
Async XLA Ops:
  0.6 1.0 %copy-start = (s32[16,128]{1,0:T(8,128)S(1)}, s32[16,128]{1,0:T(8,128)}, u32[]{:S(2)}) copy-start(s32[16,128]{1,0:T(8,128)} %land_ref.1) | copy-start | bytes 24580
  0.7 1.0 %copy-start.1 = (s32[16,128]{1,0:T(8,128)S(1)}, s32[16,128]{1,0:T(8,128)}, u32[]{:S(2)}) copy-start(s32[16,128]{1,0:T(8,128)} %bottom_ref.1) | copy-start | bytes 24580
  2.1 4.5 %collective-permute-start = (f32[2,2,2,8,128]{4,3,2,1,0:T(8,128)S(1)}, f32[2,2,2,8,128]{4,3,2,1,0:T(8,128)S(1)}, u32[]{:S(2)}, u32[]{:S(2)}) collective-permute-start(f32[2,2,2,8,128]{4,3,2,1,0:T(8,128)S(1)} %get-tuple-element.20), channel_id=1, source_target_pairs={{0,1},{1,0},{2,3},{3,2},{4,5},{5,4},{6,7},{7,6},{8,9},{9,8},{10,11... | collective-permute-start | bytes 98312 | tf_op jit(solution)/shard_map/ppermute | solution.py:559
  2.6 4.1 %collective-permute-start.1 = (f32[2,2,8,128]{3,2,1,0:T(8,128)S(1)}, f32[2,2,8,128]{3,2,1,0:T(8,128)S(1)}, u32[]{:S(2)}, u32[]{:S(2)}) collective-permute-start(f32[2,2,8,128]{3,2,1,0:T(8,128)S(1)} %get-tuple-element.21), channel_id=1, source_target_pairs={{0,3},{1,2},{2,1},{3,0},{4,7},{5,6},{6,5},{7,4},{8,11},{9,10},{10,... | collective-permute-start | bytes 49160 | tf_op jit(solution)/shard_map/ppermute | solution.py:557
  5.2 6.9 %collective-permute-start.4 = (f32[12,2,2,8,128]{4,3,2,1,0:T(8,128)S(1)}, f32[12,2,2,8,128]{4,3,2,1,0:T(8,128)S(1)}, u32[]{:S(2)}, u32[]{:S(2)}) collective-permute-start(f32[12,2,2,8,128]{4,3,2,1,0:T(8,128)S(1)} %get-tuple-element.25), channel_id=1, source_target_pairs={{0,2},{1,3},{2,0},{3,1},{4,6},{5,7},{6,4},{7,5},{8,10},{9,11},{10,... | collective-permute-start | bytes 589832 | tf_op jit(solution)/shard_map/ppermute | solution.py:558
  7.0 11.2 %collective-permute-start.2 = (f32[12,2,2,8,128]{4,3,2,1,0:T(8,128)S(1)}, f32[12,2,2,8,128]{4,3,2,1,0:T(8,128)S(1)}, u32[]{:S(2)}, u32[]{:S(2)}) collective-permute-start(f32[12,2,2,8,128]{4,3,2,1,0:T(8,128)S(1)} %get-tuple-element.23), channel_id=1, source_target_pairs={{0,14},{1,15},{2,4},{3,5},{4,2},{5,3},{6,8},{7,9},{8,6},{9,7},{10,... | collective-permute-start | bytes 589832 | tf_op jit(solution)/shard_map/ppermute | solution.py:561
  11.7 6.4 %collective-permute-start.3 = (f32[2,2,8,128]{3,2,1,0:T(8,128)S(1)}, f32[2,2,8,128]{3,2,1,0:T(8,128)S(1)}, u32[]{:S(2)}, u32[]{:S(2)}) collective-permute-start(f32[2,2,8,128]{3,2,1,0:T(8,128)S(1)} %get-tuple-element.24), channel_id=1, source_target_pairs={{0,14},{1,15},{2,4},{3,5},{4,2},{5,3},{6,8},{7,9},{8,6},{9,7},{10,... | collective-permute-start | bytes 49160 | tf_op jit(solution)/shard_map/ppermute | solution.py:562

commit v6 on v5

--- a/solution.py
+++ b/solution.py
@@ -48,8 +48,8 @@
     return sub, lane
 
 
-def column(rows, r, flip):
-    return r + flip * (rows - 1 - 2 * r)
+def either(flip, x, mirrored):
+    return jnp.where(jnp.broadcast_to(flip, x.shape) == 1, mirrored, x)
 
 
 def spare_lanes(core):
@@ -70,14 +70,15 @@
     for r in range(rows):
         group, seg = divmod(r, SEGS)
         shift = lax.rem(EDGE * seg + (1 - core) * (WIDE + EDGE), LANES)
-        i = column(rows, r, flip)
-        deep = jnp.where(land_ref[pl.ds(i, 1), :] == 1, bottom_ref[pl.ds(i, 1), :], 0)
+        pair = (r, rows - 1 - r)
+        deep = either(flip, *(jnp.where(land_ref[i : i + 1, :] == 1, bottom_ref[i : i + 1, :], 0) for i in pair))
         deep = jnp.broadcast_to(deep, (SUB, LANES))
         for par in range(2):
             wet = 2 * sub + par < deep
             for f in range(2):
-                at = pl.ds((2 * SUB * f + par) * rows + i, SUB, stride=2 * rows)
-                x = take_lanes(jnp.where(wet, both_ref[at, :], 0.0), apart)
+                start = (2 * SUB * f + par) * rows
+                x = either(flip, *(both_ref[pl.ds(start + i, SUB, stride=2 * rows), :] for i in pair))
+                x = take_lanes(jnp.where(wet, x, 0.0), apart)
                 own_ref[r, f, par] = x
                 if r < DEPTH:
                     near_ref[r, f, par] = x
@@ -499,14 +500,14 @@
     _, lane = iotas()
     left = lane < WIDE
     mixed = WIDE * (lane % 2) + lane // 2
-    for i in range(rows):
+    made = {}
+    for i in sorted(range(rows), key=lambda i: min(i, rows - 1 - i)):
         u_refs, r_refs = [], []
         for k in range(ITERS):
             n_u, n_r = first_u(rows, k)
             u_refs.append(u_near_ref if i < n_u else u_far_ref)
             r_refs.append(r_near_ref if i < n_r else r_far_ref)
         for par in range(2):
-            at = pl.ds(par * rows + column(rows, i, flip), SUB, stride=2 * rows)
             pair = []
             for t in (par, 2 + par):
                 x = sol[0] * u_refs[0][0, i, t]
@@ -518,8 +519,13 @@
             x, y = (jnp.where(left, even, pltpu.roll(odd, WIDE, 1)) for even, odd in zip(*pair))
             x = take_lanes(x, mixed)
             y = take_lanes(y + res[0] * own_ref[i, 1, par], mixed)
-            sol_ref[at, :] = x
-            res_ref[at, :] = y
+            made[i, par] = x, y
+            other = rows - 1 - i
+            if (other, par) in made:
+                for r, mirror in ((i, other), (other, i)):
+                    at = pl.ds(par * rows + r, SUB, stride=2 * rows)
+                    for ref, a, b in zip((sol_ref, res_ref), made[r, par], made[mirror, par]):
+                        ref[at, :] = either(flip, a, b)
 
 
 def last(place, sums, own, *vectors):

time: 33 us -> 33.1 us (level)
  no operation moved by 1% of the time
where the time goes in v6:
time: 33.1 us; the launch traced here: 32.9 us
  blocking collectives  11.8 us (36%)
  starting transfers between devices  7.98 us (24%)
  Pallas kernels  5.79 us (17%)
  waiting for transfers between devices  5.67 us (17%)
  other arithmetic  1 us (3%)
  between operations  0.69 us (2%)
    all_to_all x1, blocking collectives, local(): sums = lax.all_to_all(parts, both, 0, 0, tiled=True)  11.8 us
    ppermute x1, starting transfers between devices, local(): far = lax.ppermute(far, both, links(lambda i, j: (beyond(i), j)))  4.77 us
    ppermute x1, waiting for transfers between devices, local(): lax.ppermute(far_corner, both, links(lambda i, j: (beyond(i), j)))  3.99 us
    ppermute x1, starting transfers between devices, local(): corner = lax.ppermute(corner, both, links(lambda i, j: (i ^ 1, 1 - j)))  2.61 us
    pallas_call x1, Pallas kernels, near_side(): pl.pallas_call(near_kernel, out_shape=outs, in_specs=[pl.BlockSpec(memory...  2.08 us
    pallas_call x1, Pallas kernels, far_side(): pl.pallas_call(far_kernel, out_shape=outs, in_specs=[pl.BlockSpec(memory_...  1.77 us
    ppermute x1, waiting for transfers between devices, local(): corner = lax.ppermute(corner, both, links(lambda i, j: (i ^ 1, 1 - j)))  1.4 us
    pallas_call x1, Pallas kernels, last(): pl.pallas_call(last_kernel, out_shape=(out, out), in_specs=[pl.BlockSpec(...  1.14 us
  transfers between devices with their start and end apart: 5, of which 3 were waited for; matrix products, arithmetic and copies ran while one was open for 0% of the time, Pallas kernels for 7%

profile of v6, /device:TPU:0, one launch (start us, length us, event | category | flops | bytes accessed | tf_op | source)
XLA Modules:
  0.0 32.9 jit_solution(13695470569458303144)
XLA Ops:
  0.6 0.0 copy-start
  0.7 0.0 copy-start.1
  0.7 1.0 %pad_maximum_fusion = f32[2,16,16,128]{3,2,1,0:T(8,128)S(1)} fusion(f32[1,16,16,128]{3,2,1,0:T(8,128)} %bitcast.13, f32[1,16,16,128]{3,2,1,0:T(8,128)} %bitcast.14), kind=kLoop, calls=%fused_computation | loop fusion | flops 65536 | bytes 524288 | tf_op jit(solution)/shard_map/stack | solution.py:561
  1.7 0.0 copy-done
  1.7 0.0 copy-done.1
  1.7 0.5 %prep.1 = (f32[16,2,2,8,128]{4,3,2,1,0:T(8,128)S(1)}, f32[2,2,2,8,128]{4,3,2,1,0:T(8,128)S(1)}, f32[12,2,2,8,128]{4,3,2,1,0:T(8,128)S(1)}, f32[2,2,8,128]{3,2,1,0:T(8,128)S(1)}) custom-call(s32[1]{0:T(128)} %bitcast.place_ref, f32[512,128]{1,0:T(8,128)S(1)} %bitcast.10, s32[16,128]{1,0:T(8,128)S(1)} %copy-done, s32[16,128]{1,0:T(8,128)S(1)} %copy-done.1), custom_call_target="tpu_custom_call" | custom-call | tf_op jit(solution)/shard_map/prep/pallas_call | solution.py:101
  2.2 0.5 %collective-permute-start = (f32[2,2,2,8,128]{4,3,2,1,0:T(8,128)S(1)}, f32[2,2,2,8,128]{4,3,2,1,0:T(8,128)S(1)}, u32[]{:S(2)}, u32[]{:S(2)}) collective-permute-start(f32[2,2,2,8,128]{4,3,2,1,0:T(8,128)S(1)} %get-tuple-element.20), channel_id=1, source_target_pairs={{0,1},{1,0},{2,3},{3,2},{4,5},{5,4},{6,7},{7,6},{8,9},{9,8},{10,11... | collective-permute-start | bytes 98312 | tf_op jit(solution)/shard_map/ppermute | solution.py:565
  2.7 2.6 %collective-permute-start.1 = (f32[2,2,8,128]{3,2,1,0:T(8,128)S(1)}, f32[2,2,8,128]{3,2,1,0:T(8,128)S(1)}, u32[]{:S(2)}, u32[]{:S(2)}) collective-permute-start(f32[2,2,8,128]{3,2,1,0:T(8,128)S(1)} %get-tuple-element.21), channel_id=1, source_target_pairs={{0,3},{1,2},{2,1},{3,0},{4,7},{5,6},{6,5},{7,4},{8,11},{9,10},{10,... | collective-permute-start | bytes 49160 | tf_op jit(solution)/shard_map/ppermute | solution.py:563
  5.3 0.0 collective-permute-start.4
  5.3 1.4 %collective-permute-done.1.near_corner_ref.corner_ref = f32[2,2,8,128]{3,2,1,0:T(8,128)S(1)} collective-permute-done((f32[2,2,8,128]{3,2,1,0:T(8,128)S(1)}, f32[2,2,8,128]{3,2,1,0:T(8,128)S(1)}, u32[]{:S(2)}, u32[]{:S(2)}) %collective-permute-start.1) | collective-permute-done | bytes 16416 | tf_op jit(solution)/shard_map/ppermute | solution.py:563
  6.7 0.0 collective-permute-done.strip_ref
  6.7 0.3 pack.1
  7.0 4.8 %collective-permute-start.2 = (f32[12,2,2,8,128]{4,3,2,1,0:T(8,128)S(1)}, f32[12,2,2,8,128]{4,3,2,1,0:T(8,128)S(1)}, u32[]{:S(2)}, u32[]{:S(2)}) collective-permute-start(f32[12,2,2,8,128]{4,3,2,1,0:T(8,128)S(1)} %get-tuple-element.23), channel_id=1, source_target_pairs={{0,14},{1,15},{2,4},{3,5},{4,2},{5,3},{6,8},{7,9},{8,6},{9,7},{10,... | collective-permute-start | bytes 589832 | tf_op jit(solution)/shard_map/ppermute | solution.py:567
  11.8 0.1 collective-permute-start.3
  11.9 0.3 collective-permute-done.4.near_ref
  12.1 2.1 %near_side.1 = (f32[12,2,4,8,128]{4,3,2,1,0:T(8,128)S(1)}, f32[3,4,4,8,128]{4,3,2,1,0:T(8,128)S(1)}, f32[3,16,4,8,128]{4,3,2,1,0:T(8,128)S(1)}, f32[3,16,4,8,128]{4,3,2,1,0:T(8,128)S(1)}, f32[6,8,128]{2,1,0:T(8,128)S(1)}) custom-call(s32[1]{0:T(128)} %bitcast.place_ref, f32[2,16,4,8,128]{4,3,2,1,0:T(8,128)S(1)} %get-tuple-element.22.tile_ref, ...), custom_call_target="tpu_custom_call" | custom-call | flops 20000000 | bytes 4194304 | tf_op jit(solution)/shard_map/near_side/pallas_call | solution.py:359
  14.2 4.0 %collective-permute-done.3.corner_ref = f32[2,2,8,128]{3,2,1,0:T(8,128)S(1)} collective-permute-done((f32[2,2,8,128]{3,2,1,0:T(8,128)S(1)}, f32[2,2,8,128]{3,2,1,0:T(8,128)S(1)}, u32[]{:S(2)}, u32[]{:S(2)}) %collective-permute-start.3) | collective-permute-done | bytes 16416 | tf_op jit(solution)/shard_map/ppermute | solution.py:568
  18.2 0.0 collective-permute-done.2.far_ref
  18.2 1.8 %far_side.1 = (f32[3,16,4,8,128]{4,3,2,1,0:T(8,128)S(1)}, f32[3,16,4,8,128]{4,3,2,1,0:T(8,128)S(1)}, f32[16,128]{1,0:T(8,128)S(1)}) custom-call(s32[1]{0:T(128)} %bitcast.place_ref, f32[2,16,4,8,128]{4,3,2,1,0:T(8,128)S(1)} %get-tuple-element.22.tile_ref, f32[12,2,2,8,128]{4,3,2,1,0:T(8,128)S(1)} %collective-permute-done.2.far_ref, ...), custom_call_target="tpu_custom_call" | custom-call | flops 15000000 | bytes 4194304 | tf_op jit(solution)/shard_map/far_side/pallas_call | solution.py:433
  20.0 11.8 %all_to_all.11 = f32[16,1,128]{2,1,0:T(1,128)S(1)} all-to-all(f32[16,1,128]{2,1,0:T(1,128)S(1)} %bitcast.12), channel_id=1, replica_groups=mesh['member'=2,'lon'=8,'lat'=2] {'lon','lat'}, dimensions={0} | all-to-all | bytes 16384 | tf_op jit(solution)/shard_map/all_to_all | solution.py:571
  31.8 1.1 %combine.1 = (f32[256,128]{1,0:T(8,128)}, f32[256,128]{1,0:T(8,128)}) custom-call(s32[1]{0:T(128)} %bitcast.place_ref, f32[16,128]{1,0:T(8,128)S(1)} %bitcast.11, f32[16,2,2,8,128]{4,3,2,1,0:T(8,128)S(1)} %get-tuple-element.19.own_ref, f32[3,16,4,8,128]{4,3,2,1,0:T(8,128)S(1)} %get-tuple-element.30.u_near_ref, ...), custom_call_target="tpu_custom_call" | custom-call | tf_op jit(solution)/shard_map/combine/pallas_call | solution.py:535
Async XLA Ops:
  0.6 1.0 %copy-start = (s32[16,128]{1,0:T(8,128)S(1)}, s32[16,128]{1,0:T(8,128)}, u32[]{:S(2)}) copy-start(s32[16,128]{1,0:T(8,128)} %land_ref.1) | copy-start | bytes 24580
  0.7 1.0 %copy-start.1 = (s32[16,128]{1,0:T(8,128)S(1)}, s32[16,128]{1,0:T(8,128)}, u32[]{:S(2)}) copy-start(s32[16,128]{1,0:T(8,128)} %bottom_ref.1) | copy-start | bytes 24580
  2.2 4.5 %collective-permute-start = (f32[2,2,2,8,128]{4,3,2,1,0:T(8,128)S(1)}, f32[2,2,2,8,128]{4,3,2,1,0:T(8,128)S(1)}, u32[]{:S(2)}, u32[]{:S(2)}) collective-permute-start(f32[2,2,2,8,128]{4,3,2,1,0:T(8,128)S(1)} %get-tuple-element.20), channel_id=1, source_target_pairs={{0,1},{1,0},{2,3},{3,2},{4,5},{5,4},{6,7},{7,6},{8,9},{9,8},{10,11... | collective-permute-start | bytes 98312 | tf_op jit(solution)/shard_map/ppermute | solution.py:565
  2.7 4.1 %collective-permute-start.1 = (f32[2,2,8,128]{3,2,1,0:T(8,128)S(1)}, f32[2,2,8,128]{3,2,1,0:T(8,128)S(1)}, u32[]{:S(2)}, u32[]{:S(2)}) collective-permute-start(f32[2,2,8,128]{3,2,1,0:T(8,128)S(1)} %get-tuple-element.21), channel_id=1, source_target_pairs={{0,3},{1,2},{2,1},{3,0},{4,7},{5,6},{6,5},{7,4},{8,11},{9,10},{10,... | collective-permute-start | bytes 49160 | tf_op jit(solution)/shard_map/ppermute | solution.py:563
  5.3 6.9 %collective-permute-start.4 = (f32[12,2,2,8,128]{4,3,2,1,0:T(8,128)S(1)}, f32[12,2,2,8,128]{4,3,2,1,0:T(8,128)S(1)}, u32[]{:S(2)}, u32[]{:S(2)}) collective-permute-start(f32[12,2,2,8,128]{4,3,2,1,0:T(8,128)S(1)} %get-tuple-element.25), channel_id=1, source_target_pairs={{0,2},{1,3},{2,0},{3,1},{4,6},{5,7},{6,4},{7,5},{8,10},{9,11},{10,... | collective-permute-start | bytes 589832 | tf_op jit(solution)/shard_map/ppermute | solution.py:564
  7.0 11.2 %collective-permute-start.2 = (f32[12,2,2,8,128]{4,3,2,1,0:T(8,128)S(1)}, f32[12,2,2,8,128]{4,3,2,1,0:T(8,128)S(1)}, u32[]{:S(2)}, u32[]{:S(2)}) collective-permute-start(f32[12,2,2,8,128]{4,3,2,1,0:T(8,128)S(1)} %get-tuple-element.23), channel_id=1, source_target_pairs={{0,14},{1,15},{2,4},{3,5},{4,2},{5,3},{6,8},{7,9},{8,6},{9,7},{10,... | collective-permute-start | bytes 589832 | tf_op jit(solution)/shard_map/ppermute | solution.py:567
  11.8 6.4 %collective-permute-start.3 = (f32[2,2,8,128]{3,2,1,0:T(8,128)S(1)}, f32[2,2,8,128]{3,2,1,0:T(8,128)S(1)}, u32[]{:S(2)}, u32[]{:S(2)}) collective-permute-start(f32[2,2,8,128]{3,2,1,0:T(8,128)S(1)} %get-tuple-element.24), channel_id=1, source_target_pairs={{0,14},{1,15},{2,4},{3,5},{4,2},{5,3},{6,8},{7,9},{8,6},{9,7},{10,... | collective-permute-start | bytes 49160 | tf_op jit(solution)/shard_map/ppermute | solution.py:568

commit v7 on v6

--- a/solution.py
+++ b/solution.py
@@ -300,6 +300,9 @@
 
     def write(step, r, tiles):
         spread(bufs[step % EVERY], (r + DEPTH,), tiles)
+        turn, stage = divmod(step - 1, EVERY)
+        if 0 <= r < rows and stage >= CHEB - 1:
+            spread(u_ref if stage == CHEB - 1 else r_ref, (turn, r), tiles)
 
     def keep(step):
         turn, stage = divmod(step - 1, EVERY)
@@ -326,12 +329,7 @@
         if step < DEPTH:
             keep(step)
         for r in range(rows - step):
-            tiles = read(step, r)
-            if stage == CHEB - 1:
-                spread(u_ref, (turn, r), tiles)
-            elif stage == CHEB:
-                spread(r_ref, (turn, r), tiles)
-            sums.step(step, r, tiles, read)
+            sums.step(step, r, read(step, r), read)
     for j in range(2 * ITERS):
         part_ref[j] = sums.total(j)
 
@@ -392,6 +390,9 @@
 
     def write(step, r, tiles):
         spread(bufs[step % EVERY], (r,), tiles)
+        turn, stage = divmod(step - 1, EVERY)
+        if 0 <= r < rows and stage >= CHEB - 1:
+            spread(u_ref if stage == CHEB - 1 else r_ref, (turn, r), tiles)
 
     for r in range(base, rows + DEPTH):
         if r < rows:
@@ -407,12 +408,7 @@
         turn, stage = divmod(step - 1, EVERY)
         sweep(range(rows - step, rows + DEPTH - step), step, read, write, coef)
         for r in range(rows - step, rows):
-            tiles = read(step, r)
-            if stage == CHEB - 1:
-                spread(u_ref, (turn, r), tiles)
-            elif stage == CHEB:
-                spread(r_ref, (turn, r), tiles)
-            sums.step(step, r, tiles, read)
+            sums.step(step, r, read(step, r), read)
     block = jnp.zeros((SUB, LANES), jnp.float32)
     for j in range(2 * ITERS):
         part = jnp.where(lanes.left, sums.total(j) + part_in_ref[j], 0.0)

time: 33.1 us -> 33.1 us (level)
  no operation moved by 1% of the time
where the time goes in v7:
time: 33.1 us; the launch traced here: 32.9 us
  blocking collectives  11.8 us (36%)
  starting transfers between devices  7.98 us (24%)
  Pallas kernels  5.79 us (17%)
  waiting for transfers between devices  5.67 us (17%)
  other arithmetic  1 us (3%)
  between operations  0.69 us (2%)
    all_to_all x1, blocking collectives, local(): sums = lax.all_to_all(parts, both, 0, 0, tiled=True)  11.8 us
    ppermute x1, starting transfers between devices, local(): far = lax.ppermute(far, both, links(lambda i, j: (beyond(i), j)))  4.77 us
    ppermute x1, waiting for transfers between devices, local(): lax.ppermute(far_corner, both, links(lambda i, j: (beyond(i), j)))  3.99 us
    ppermute x1, starting transfers between devices, local(): corner = lax.ppermute(corner, both, links(lambda i, j: (i ^ 1, 1 - j)))  2.61 us
    pallas_call x1, Pallas kernels, near_side(): pl.pallas_call(near_kernel, out_shape=outs, in_specs=[pl.BlockSpec(memory...  2.08 us
    pallas_call x1, Pallas kernels, far_side(): pl.pallas_call(far_kernel, out_shape=outs, in_specs=[pl.BlockSpec(memory_...  1.77 us
    ppermute x1, waiting for transfers between devices, local(): corner = lax.ppermute(corner, both, links(lambda i, j: (i ^ 1, 1 - j)))  1.4 us
    pallas_call x1, Pallas kernels, last(): pl.pallas_call(last_kernel, out_shape=(out, out), in_specs=[pl.BlockSpec(...  1.14 us
  transfers between devices with their start and end apart: 5, of which 3 were waited for; matrix products, arithmetic and copies ran while one was open for 0% of the time, Pallas kernels for 7%

profile of v7, /device:TPU:0, one launch (start us, length us, event | category | flops | bytes accessed | tf_op | source)
XLA Modules:
  0.0 32.9 jit_solution(5341352704754304035)
XLA Ops:
  0.6 0.0 copy-start
  0.7 0.0 copy-start.1
  0.7 1.0 %pad_maximum_fusion = f32[2,16,16,128]{3,2,1,0:T(8,128)S(1)} fusion(f32[1,16,16,128]{3,2,1,0:T(8,128)} %bitcast.13, f32[1,16,16,128]{3,2,1,0:T(8,128)} %bitcast.14), kind=kLoop, calls=%fused_computation | loop fusion | flops 65536 | bytes 524288 | tf_op jit(solution)/shard_map/stack | solution.py:557
  1.7 0.0 copy-done
  1.7 0.0 copy-done.1
  1.7 0.5 %prep.1 = (f32[16,2,2,8,128]{4,3,2,1,0:T(8,128)S(1)}, f32[2,2,2,8,128]{4,3,2,1,0:T(8,128)S(1)}, f32[12,2,2,8,128]{4,3,2,1,0:T(8,128)S(1)}, f32[2,2,8,128]{3,2,1,0:T(8,128)S(1)}) custom-call(s32[1]{0:T(128)} %bitcast.place_ref, f32[512,128]{1,0:T(8,128)S(1)} %bitcast.10, s32[16,128]{1,0:T(8,128)S(1)} %copy-done, s32[16,128]{1,0:T(8,128)S(1)} %copy-done.1), custom_call_target="tpu_custom_call" | custom-call | tf_op jit(solution)/shard_map/prep/pallas_call | solution.py:101
  2.2 0.5 %collective-permute-start = (f32[2,2,2,8,128]{4,3,2,1,0:T(8,128)S(1)}, f32[2,2,2,8,128]{4,3,2,1,0:T(8,128)S(1)}, u32[]{:S(2)}, u32[]{:S(2)}) collective-permute-start(f32[2,2,2,8,128]{4,3,2,1,0:T(8,128)S(1)} %get-tuple-element.20), channel_id=1, source_target_pairs={{0,1},{1,0},{2,3},{3,2},{4,5},{5,4},{6,7},{7,6},{8,9},{9,8},{10,11... | collective-permute-start | bytes 98312 | tf_op jit(solution)/shard_map/ppermute | solution.py:561
  2.7 2.6 %collective-permute-start.1 = (f32[2,2,8,128]{3,2,1,0:T(8,128)S(1)}, f32[2,2,8,128]{3,2,1,0:T(8,128)S(1)}, u32[]{:S(2)}, u32[]{:S(2)}) collective-permute-start(f32[2,2,8,128]{3,2,1,0:T(8,128)S(1)} %get-tuple-element.21), channel_id=1, source_target_pairs={{0,3},{1,2},{2,1},{3,0},{4,7},{5,6},{6,5},{7,4},{8,11},{9,10},{10,... | collective-permute-start | bytes 49160 | tf_op jit(solution)/shard_map/ppermute | solution.py:559
  5.3 0.0 collective-permute-start.4
  5.3 1.4 %collective-permute-done.1.near_corner_ref.corner_ref = f32[2,2,8,128]{3,2,1,0:T(8,128)S(1)} collective-permute-done((f32[2,2,8,128]{3,2,1,0:T(8,128)S(1)}, f32[2,2,8,128]{3,2,1,0:T(8,128)S(1)}, u32[]{:S(2)}, u32[]{:S(2)}) %collective-permute-start.1) | collective-permute-done | bytes 16416 | tf_op jit(solution)/shard_map/ppermute | solution.py:559
  6.7 0.0 collective-permute-done.strip_ref
  6.7 0.3 pack.1
  7.0 4.8 %collective-permute-start.2 = (f32[12,2,2,8,128]{4,3,2,1,0:T(8,128)S(1)}, f32[12,2,2,8,128]{4,3,2,1,0:T(8,128)S(1)}, u32[]{:S(2)}, u32[]{:S(2)}) collective-permute-start(f32[12,2,2,8,128]{4,3,2,1,0:T(8,128)S(1)} %get-tuple-element.23), channel_id=1, source_target_pairs={{0,14},{1,15},{2,4},{3,5},{4,2},{5,3},{6,8},{7,9},{8,6},{9,7},{10,... | collective-permute-start | bytes 589832 | tf_op jit(solution)/shard_map/ppermute | solution.py:563
  11.8 0.1 collective-permute-start.3
  11.9 0.3 collective-permute-done.4.near_ref
  12.1 2.1 %near_side.1 = (f32[12,2,4,8,128]{4,3,2,1,0:T(8,128)S(1)}, f32[3,4,4,8,128]{4,3,2,1,0:T(8,128)S(1)}, f32[3,16,4,8,128]{4,3,2,1,0:T(8,128)S(1)}, f32[3,16,4,8,128]{4,3,2,1,0:T(8,128)S(1)}, f32[6,8,128]{2,1,0:T(8,128)S(1)}) custom-call(s32[1]{0:T(128)} %bitcast.place_ref, f32[2,16,4,8,128]{4,3,2,1,0:T(8,128)S(1)} %get-tuple-element.22.tile_ref, ...), custom_call_target="tpu_custom_call" | custom-call | flops 20000000 | bytes 4194304 | tf_op jit(solution)/shard_map/near_side/pallas_call | solution.py:357
  14.2 4.0 %collective-permute-done.3.corner_ref = f32[2,2,8,128]{3,2,1,0:T(8,128)S(1)} collective-permute-done((f32[2,2,8,128]{3,2,1,0:T(8,128)S(1)}, f32[2,2,8,128]{3,2,1,0:T(8,128)S(1)}, u32[]{:S(2)}, u32[]{:S(2)}) %collective-permute-start.3) | collective-permute-done | bytes 16416 | tf_op jit(solution)/shard_map/ppermute | solution.py:564
  18.2 0.0 collective-permute-done.2.far_ref
  18.2 1.8 %far_side.1 = (f32[3,16,4,8,128]{4,3,2,1,0:T(8,128)S(1)}, f32[3,16,4,8,128]{4,3,2,1,0:T(8,128)S(1)}, f32[16,128]{1,0:T(8,128)S(1)}) custom-call(s32[1]{0:T(128)} %bitcast.place_ref, f32[2,16,4,8,128]{4,3,2,1,0:T(8,128)S(1)} %get-tuple-element.22.tile_ref, f32[12,2,2,8,128]{4,3,2,1,0:T(8,128)S(1)} %collective-permute-done.2.far_ref, ...), custom_call_target="tpu_custom_call" | custom-call | flops 15000000 | bytes 4194304 | tf_op jit(solution)/shard_map/far_side/pallas_call | solution.py:429
  20.0 11.8 %all_to_all.11 = f32[16,1,128]{2,1,0:T(1,128)S(1)} all-to-all(f32[16,1,128]{2,1,0:T(1,128)S(1)} %bitcast.12), channel_id=1, replica_groups=mesh['member'=2,'lon'=8,'lat'=2] {'lon','lat'}, dimensions={0} | all-to-all | bytes 16384 | tf_op jit(solution)/shard_map/all_to_all | solution.py:567
  31.8 1.1 %combine.1 = (f32[256,128]{1,0:T(8,128)}, f32[256,128]{1,0:T(8,128)}) custom-call(s32[1]{0:T(128)} %bitcast.place_ref, f32[16,128]{1,0:T(8,128)S(1)} %bitcast.11, f32[16,2,2,8,128]{4,3,2,1,0:T(8,128)S(1)} %get-tuple-element.19.own_ref, f32[3,16,4,8,128]{4,3,2,1,0:T(8,128)S(1)} %get-tuple-element.30.u_near_ref, ...), custom_call_target="tpu_custom_call" | custom-call | tf_op jit(solution)/shard_map/combine/pallas_call | solution.py:531
Async XLA Ops:
  0.6 1.0 %copy-start = (s32[16,128]{1,0:T(8,128)S(1)}, s32[16,128]{1,0:T(8,128)}, u32[]{:S(2)}) copy-start(s32[16,128]{1,0:T(8,128)} %land_ref.1) | copy-start | bytes 24580
  0.7 1.0 %copy-start.1 = (s32[16,128]{1,0:T(8,128)S(1)}, s32[16,128]{1,0:T(8,128)}, u32[]{:S(2)}) copy-start(s32[16,128]{1,0:T(8,128)} %bottom_ref.1) | copy-start | bytes 24580
  2.2 4.5 %collective-permute-start = (f32[2,2,2,8,128]{4,3,2,1,0:T(8,128)S(1)}, f32[2,2,2,8,128]{4,3,2,1,0:T(8,128)S(1)}, u32[]{:S(2)}, u32[]{:S(2)}) collective-permute-start(f32[2,2,2,8,128]{4,3,2,1,0:T(8,128)S(1)} %get-tuple-element.20), channel_id=1, source_target_pairs={{0,1},{1,0},{2,3},{3,2},{4,5},{5,4},{6,7},{7,6},{8,9},{9,8},{10,11... | collective-permute-start | bytes 98312 | tf_op jit(solution)/shard_map/ppermute | solution.py:561
  2.7 4.1 %collective-permute-start.1 = (f32[2,2,8,128]{3,2,1,0:T(8,128)S(1)}, f32[2,2,8,128]{3,2,1,0:T(8,128)S(1)}, u32[]{:S(2)}, u32[]{:S(2)}) collective-permute-start(f32[2,2,8,128]{3,2,1,0:T(8,128)S(1)} %get-tuple-element.21), channel_id=1, source_target_pairs={{0,3},{1,2},{2,1},{3,0},{4,7},{5,6},{6,5},{7,4},{8,11},{9,10},{10,... | collective-permute-start | bytes 49160 | tf_op jit(solution)/shard_map/ppermute | solution.py:559
  5.3 6.9 %collective-permute-start.4 = (f32[12,2,2,8,128]{4,3,2,1,0:T(8,128)S(1)}, f32[12,2,2,8,128]{4,3,2,1,0:T(8,128)S(1)}, u32[]{:S(2)}, u32[]{:S(2)}) collective-permute-start(f32[12,2,2,8,128]{4,3,2,1,0:T(8,128)S(1)} %get-tuple-element.25), channel_id=1, source_target_pairs={{0,2},{1,3},{2,0},{3,1},{4,6},{5,7},{6,4},{7,5},{8,10},{9,11},{10,... | collective-permute-start | bytes 589832 | tf_op jit(solution)/shard_map/ppermute | solution.py:560
  7.0 11.2 %collective-permute-start.2 = (f32[12,2,2,8,128]{4,3,2,1,0:T(8,128)S(1)}, f32[12,2,2,8,128]{4,3,2,1,0:T(8,128)S(1)}, u32[]{:S(2)}, u32[]{:S(2)}) collective-permute-start(f32[12,2,2,8,128]{4,3,2,1,0:T(8,128)S(1)} %get-tuple-element.23), channel_id=1, source_target_pairs={{0,14},{1,15},{2,4},{3,5},{4,2},{5,3},{6,8},{7,9},{8,6},{9,7},{10,... | collective-permute-start | bytes 589832 | tf_op jit(solution)/shard_map/ppermute | solution.py:563
  11.8 6.4 %collective-permute-start.3 = (f32[2,2,8,128]{3,2,1,0:T(8,128)S(1)}, f32[2,2,8,128]{3,2,1,0:T(8,128)S(1)}, u32[]{:S(2)}, u32[]{:S(2)}) collective-permute-start(f32[2,2,8,128]{3,2,1,0:T(8,128)S(1)} %get-tuple-element.24), channel_id=1, source_target_pairs={{0,14},{1,15},{2,4},{3,5},{4,2},{5,3},{6,8},{7,9},{8,6},{9,7},{10,... | collective-permute-start | bytes 49160 | tf_op jit(solution)/shard_map/ppermute | solution.py:564
